TPU v7x, 256 devices: a whole 4x4x8 slice. The times are simulated.
256 devices in a mesh: blk: 16 (over x, y_hi, core), feat: 16 (over y_lo, z).
Axes of the slice: x: 4, y: 4 (y_hi: 2, y_lo: 2; y = y_hi * 2 + y_lo), z: 8, core: 2. Of those that a mesh axis runs over, the one named last changes fastest.
Arguments:
- noise_latents: bfloat16 [16384, 1024], P(('blk', 'feat')), may hold values from -30 to 30, as said below
- data_latents: bfloat16 [16384, 1024], P(('blk', 'feat')), may hold values from -30 to 30, as said below
Outputs:
- velocity: bfloat16 [16384, 1024], P(('blk', 'feat'))
Inputs may be any that keep to these rules, and one draw needn't show every extreme that they name: `noise_latents`: pooled latent features. `data_latents`: pooled latent features.
All inputs are finite; a program needn't handle non-finite values.
Results may differ from a plain program's by a relative error of at most 0.013.
Values may be sent and summed in bfloat16 or wider, within the bound.
No kernel may reach another device: no remote copies, remote signals or barrier semaphores. Data moves between devices by JAX's collectives and lax.ppermute only.
A program may use at most 64 MiB of HBM per device.

v0:
```python
import math

import jax
import jax.numpy as jnp
from jax import lax
from jax.sharding import PartitionSpec as P

WIDTH = 1024
ITERS = 3


eps_factor = 0.3


def merged(part, axis, combine):
    gathered = jax.tree.map(lambda a: lax.all_gather(a, axis), part)

    def take(source):
        return jax.tree.map(lambda a: lax.dynamic_index_in_dim(a, source, 0, False), gathered)

    return lax.fori_loop(
        1, lax.axis_size(axis), lambda source, state: combine(state, take(source)), take(0)
    )


def combine(former, latter):
    largest = jnp.maximum(former[0], latter[0])
    return (
        largest,
        former[1] * jnp.exp(former[0] - largest) + latter[1] * jnp.exp(latter[0] - largest),
    )


def row_stats(scores):
    local_max = jnp.max(scores, axis=1)
    local_sum = jnp.sum(jnp.exp(scores - local_max[:, None]), axis=1)
    return merged((local_max, local_sum), "feat", combine)


def column_stats(scores):
    local_max = jnp.max(scores, axis=0)
    local_sum = jnp.sum(jnp.exp(scores - local_max[None, :]), axis=0)
    return merged((local_max, local_sum), "blk", combine)


def per_device(noise_latents, data_latents):
    piece_rows = noise_latents.shape[0]
    groups = lax.axis_size("feat")
    row_count = piece_rows * groups
    epsilon = eps_factor * math.sqrt(WIDTH)
    log_mass = -math.log(row_count * lax.axis_size("blk"))
    noise_full = lax.all_gather(noise_latents, "feat", axis=0, tiled=True)
    noise_norms = jnp.sum(jnp.square(noise_full.astype(jnp.float32)), axis=1)
    columns = lax.all_gather(data_latents, "blk", axis=0, tiled=True)
    piece_norms = jnp.sum(jnp.square(columns.astype(jnp.float32)), axis=1)
    products = lax.dot_general(
        noise_full, columns, (((1,), (1,)), ((), ())), preferred_element_type=jnp.float32
    )
    cost_tile = noise_norms[:, None] + piece_norms[None, :] - 2.0 * products
    column_dual = jnp.zeros((cost_tile.shape[1],), jnp.float32)
    for iteration in range(ITERS):
        row_top, row_summed = row_stats((column_dual[None, :] - cost_tile) / epsilon)
        row_dual = epsilon * log_mass - epsilon * (row_top + jnp.log(row_summed))
        column_top, column_summed = column_stats((row_dual[:, None] - cost_tile) / epsilon)
        column_dual = epsilon * log_mass - epsilon * (column_top + jnp.log(column_summed))
    scores = (column_dual[None, :] - cost_tile) / epsilon
    row_top, row_summed = row_stats(scores)
    weights = jnp.exp(scores - row_top[:, None]).astype(jnp.bfloat16)
    summed_up = lax.psum_scatter(
        jnp.dot(weights, columns, preferred_element_type=jnp.float32).astype(jnp.bfloat16),
        "feat",
        scatter_dimension=0,
        tiled=True,
    ).astype(jnp.float32)
    own_totals = lax.dynamic_slice_in_dim(
        row_summed, lax.axis_index("feat") * piece_rows, piece_rows, 0
    )
    target = summed_up / own_totals[:, None]
    return (target - noise_latents.astype(jnp.float32)).astype(jnp.bfloat16)


def solution(mesh):
    return jax.shard_map(
        per_device,
        mesh=mesh,
        in_specs=(P(("blk", "feat"), None), P(("blk", "feat"), None)),
        out_specs=P(("blk", "feat"), None),
        check_vma=False,
    )
```

profile of v0, /device:TPU:2, one launch (start us, length us, event | category | flops | bytes accessed | tf_op | source)
XLA Modules:
  0.0 639.6 jit_solution(17641363396563680045)
XLA Ops:
  8.1 58.2 %all-gather.19.cloned.1.call-done = bf16[1024,1024]{1,0:T(8,128)(2,1)} async-done(((bf16[64,1024]{1,0:T(8,128)(2,1)}), bf16[1024,1024]{1,0:T(8,128)(2,1)}) %all-gather.19.cloned.1.call-update) | async-done | bytes 2097168 | tf_op jit(solution)/shard_map/all_gather | solution.py:54
  68.5 70.3 %all-gather.17.cloned.1.call-done = bf16[1024,1024]{1,0:T(8,128)(2,1)} async-done(((bf16[64,1024]{1,0:T(8,128)(2,1)}), bf16[1024,1024]{1,0:T(8,128)(2,1)}) %all-gather.17.cloned.1.call-update) | async-done | bytes 2097168 | tf_op jit(solution)/shard_map/all_gather | solution.py:52
  140.9 4.2 fusion
  147.9 32.4 %all-gather.1 = f32[16384]{0:T(1024)S(1)} all-gather(f32[1024]{0:T(1024)S(1)} %exponential_reduce_fusion.6), channel_id=3, replica_groups=mesh['blk'=16,'feat'=16] {'feat'}, dimensions={0}, use_global_device_ids=true | all-gather | bytes 69632 | tf_op jit(solution)/shard_map/all_gather | solution.py:16
  180.3 29.9 %all-gather = f32[16384]{0:T(1024)S(1)} all-gather(f32[1024]{0:T(1024)S(1)} %get-tuple-element.1048), channel_id=2, replica_groups=mesh['blk'=16,'feat'=16] {'feat'}, dimensions={0}, use_global_device_ids=true | all-gather | bytes 69632 | tf_op jit(solution)/shard_map/all_gather | solution.py:16
  211.1 2.8 fusion.1
  215.6 21.8 %all-gather.3 = f32[16384]{0:T(1024)S(1)} all-gather(f32[1024]{0:T(1024)S(1)} %exponential_reduce_fusion.5), channel_id=5, replica_groups=mesh['blk'=16,'feat'=16] {'blk'}, dimensions={0}, use_global_device_ids=true | all-gather | bytes 69632 | tf_op jit(solution)/shard_map/all_gather | solution.py:16
  237.4 19.4 %all-gather.2 = f32[16384]{0:T(1024)S(1)} all-gather(f32[1024]{0:T(1024)S(1)} %fusion.1), channel_id=4, replica_groups=mesh['blk'=16,'feat'=16] {'blk'}, dimensions={0}, use_global_device_ids=true | all-gather | bytes 69632 | tf_op jit(solution)/shard_map/all_gather | solution.py:16
  257.8 2.8 fusion.2
  262.2 31.9 %all-gather.5 = f32[16384]{0:T(1024)S(1)} all-gather(f32[1024]{0:T(1024)S(1)} %exponential_reduce_fusion.4), channel_id=7, replica_groups=mesh['blk'=16,'feat'=16] {'feat'}, dimensions={0}, use_global_device_ids=true | all-gather | bytes 69632 | tf_op jit(solution)/shard_map/all_gather | solution.py:16
  294.1 29.9 %all-gather.4 = f32[16384]{0:T(1024)S(1)} all-gather(f32[1024]{0:T(1024)S(1)} %fusion.2), channel_id=6, replica_groups=mesh['blk'=16,'feat'=16] {'feat'}, dimensions={0}, use_global_device_ids=true | all-gather | bytes 69632 | tf_op jit(solution)/shard_map/all_gather | solution.py:16
  324.9 2.8 fusion.3
  329.4 22.3 %all-gather.7 = f32[16384]{0:T(1024)S(1)} all-gather(f32[1024]{0:T(1024)S(1)} %exponential_reduce_fusion.3), channel_id=9, replica_groups=mesh['blk'=16,'feat'=16] {'blk'}, dimensions={0}, use_global_device_ids=true | all-gather | bytes 69632 | tf_op jit(solution)/shard_map/all_gather | solution.py:16
  351.7 19.4 %all-gather.6 = f32[16384]{0:T(1024)S(1)} all-gather(f32[1024]{0:T(1024)S(1)} %fusion.3), channel_id=8, replica_groups=mesh['blk'=16,'feat'=16] {'blk'}, dimensions={0}, use_global_device_ids=true | all-gather | bytes 69632 | tf_op jit(solution)/shard_map/all_gather | solution.py:16
  372.1 2.8 fusion.4
  376.4 31.9 %all-gather.9 = f32[16384]{0:T(1024)S(1)} all-gather(f32[1024]{0:T(1024)S(1)} %exponential_reduce_fusion.2), channel_id=11, replica_groups=mesh['blk'=16,'feat'=16] {'feat'}, dimensions={0}, use_global_device_ids=true | all-gather | bytes 69632 | tf_op jit(solution)/shard_map/all_gather | solution.py:16
  408.3 30.0 %all-gather.8 = f32[16384]{0:T(1024)S(1)} all-gather(f32[1024]{0:T(1024)S(1)} %fusion.4), channel_id=10, replica_groups=mesh['blk'=16,'feat'=16] {'feat'}, dimensions={0}, use_global_device_ids=true | all-gather | bytes 69632 | tf_op jit(solution)/shard_map/all_gather | solution.py:16
  439.3 2.8 fusion.5
  443.8 22.3 %all-gather.11 = f32[16384]{0:T(1024)S(1)} all-gather(f32[1024]{0:T(1024)S(1)} %exponential_reduce_fusion.1), channel_id=13, replica_groups=mesh['blk'=16,'feat'=16] {'blk'}, dimensions={0}, use_global_device_ids=true | all-gather | bytes 69632 | tf_op jit(solution)/shard_map/all_gather | solution.py:16
  466.1 19.4 %all-gather.10 = f32[16384]{0:T(1024)S(1)} all-gather(f32[1024]{0:T(1024)S(1)} %fusion.5), channel_id=12, replica_groups=mesh['blk'=16,'feat'=16] {'blk'}, dimensions={0}, use_global_device_ids=true | all-gather | bytes 69632 | tf_op jit(solution)/shard_map/all_gather | solution.py:16
  490.8 31.9 %all-gather.13 = f32[16384]{0:T(1024)S(1)} all-gather(f32[1024]{0:T(1024)S(1)} %exponential_reduce_fusion), channel_id=15, replica_groups=mesh['blk'=16,'feat'=16] {'feat'}, dimensions={0}, use_global_device_ids=true | all-gather | bytes 69632 | tf_op jit(solution)/shard_map/all_gather | solution.py:16
  522.7 29.9 %all-gather.12 = f32[16384]{0:T(1024)S(1)} all-gather(f32[1024]{0:T(1024)S(1)} %fusion.6), channel_id=14, replica_groups=mesh['blk'=16,'feat'=16] {'feat'}, dimensions={0}, use_global_device_ids=true | all-gather | bytes 69632 | tf_op jit(solution)/shard_map/all_gather | solution.py:16
  553.5 6.1 fusion.11
  559.7 71.7 %reduce-scatter.2.cloned.1.call-done = bf16[64,1024]{1,0:T(8,128)(2,1)} async-done(((bf16[1024,1024]{1,0:T(8,128)(2,1)}), bf16[64,1024]{1,0:T(8,128)(2,1)}) %reduce-scatter.2.cloned.1.call-update) | async-done | bytes 131088 | tf_op jit(solution)/shard_map/reduce_scatter | solution.py:69
  (287 shorter events, 31.9 us)
Async XLA Ops:
  6.5 59.7 %all-gather.19.cloned.1.call-start = ((), (), s32[]{:S(2)}) async-start(), calls=%async_computation.2 | async-start | bytes 2228224 | tf_op jit(solution)/shard_map/all_gather | solution.py:54
  7.3 131.5 %all-gather.17.cloned.1.call-start = ((), (), s32[]{:S(2)}) async-start(), calls=%async_computation.1 | async-start | bytes 2228224 | tf_op jit(solution)/shard_map/all_gather | solution.py:52
  8.0 623.4 %reduce-scatter.2.cloned.1.call-start = ((), (), s32[]{:S(2)}) async-start(), calls=%async_computation.3 | async-start | bytes 2228224 | tf_op jit(solution)/shard_map/reduce_scatter | solution.py:69
  66.3 74.6 %copy-start.7 = (bf16[1024,1024]{1,0:T(8,128)(2,1)S(1)}, bf16[1024,1024]{1,0:T(8,128)(2,1)}, u32[]{:S(2)}) copy-start(bf16[1024,1024]{1,0:T(8,128)(2,1)} %all-gather.19.cloned.1.call-done) | copy-start | bytes 6291460
  145.1 1.9 copy-start
  211.1 3.5 copy-start.1
  257.8 3.5 copy-start.2
  324.9 3.5 copy-start.3
  372.0 3.5 copy-start.4
  439.3 3.5 copy-start.5
  486.4 3.5 copy-start.6
  553.5 78.0 %copy-start.8 = (bf16[64,1024]{1,0:T(8,128)(2,1)S(1)}, bf16[64,1024]{1,0:T(8,128)(2,1)}, u32[]{:S(2)}) copy-start(bf16[64,1024]{1,0:T(8,128)(2,1)} %param.16) | copy-start | bytes 393220
Sparse Core Ops, SparseCore 0:
  10.0 56.1 all-gather.18
  68.1 70.6 all-gather.16
  559.8 71.6 reduce-scatter.1
where the time goes:
time: 640 us
  blocking collectives  372 us (58%)
  waiting for transfers between devices  202 us (32%)
  other arithmetic  30.8 us (5%)
  between operations  13.5 us (2%)
  matrix products  10.4 us (2%)
  local copies, waits for them, and re-layouts  7.46 us (1%)
    all_gather x14, blocking collectives, merged(): gathered = jax.tree.map(lambda a: lax.all_gather(a, axis), part)  372 us
    reduce_scatter x1, waiting for transfers between devices, per_device(): lax.psum_scatter(jnp.dot(weights, columns, preferred_element_type=jnp.flo...  71.7 us
    all_gather x1, waiting for transfers between devices, per_device(): noise_full = lax.all_gather(noise_latents, 'feat', axis=0, tiled=True)  70.3 us
    all_gather x1, waiting for transfers between devices, per_device(): columns = lax.all_gather(data_latents, 'blk', axis=0, tiled=True)  58.2 us
  transfers between devices with their start and end apart: 3, of which 3 were waited for; matrix products, arithmetic and copies ran while one was open for 0% of the time, Pallas kernels for 0%

commit v1 on v0

v1 whole, which is shorter than its diff:
```python
import math

import jax
import jax.numpy as jnp
from jax import lax
from jax.sharding import Mesh
from jax.sharding import PartitionSpec as P

WIDTH = 1024
eps_factor = 0.3

AXES = ("x", "yh", "core", "yl", "z")
SIZES = (4, 2, 2, 2, 8)
ROW_GROUP = ("core", "z")
COL_GROUP = ("x", "yh", "yl")


def device_pairs(move):
    pairs = []
    for x in range(4):
        for yh in range(2):
            for core in range(2):
                for yl in range(2):
                    for z in range(8):
                        place = (x, yh, core, yl, z)
                        pairs.append((number(place), number(move(*place))))
    return pairs


def number(place):
    index = 0
    for size, at in zip(SIZES, place):
        index = index * size + at % size
    return index


def shift_z(a, by):
    return lax.ppermute(a, AXES, device_pairs(lambda x, yh, c, yl, z: (x, yh, c, yl, z + by)))


def swap_core(a):
    return lax.ppermute(a, AXES, device_pairs(lambda x, yh, c, yl, z: (x, yh, 1 - c, yl, z)))


def spread(vector, group):
    wide = vector.reshape(1, 8, 128)
    copies = jnp.broadcast_to(wide, (16, 8, 128))
    return lax.all_to_all(copies, group, 0, 0).reshape(16, vector.shape[0])


def log_sum_exp(values, axis):
    top = jnp.max(values, axis=axis)
    total = jnp.sum(jnp.exp(values - jnp.expand_dims(top, axis)), axis=axis)
    return top + jnp.log(total)


def per_device(noise_latents, data_latents):
    piece = noise_latents.shape[0]
    batch = piece * 256
    epsilon = eps_factor * math.sqrt(WIDTH)
    log_mass = -math.log(batch)
    core = lax.axis_index("core")

    along_z = lax.all_gather(noise_latents, "z", axis=0, tiled=True)
    other = swap_core(along_z)
    first = jnp.where(core == 0, along_z, other)
    second = jnp.where(core == 0, other, along_z)
    noise_full = jnp.concatenate([first, second], axis=0)
    columns = lax.all_to_all(
        jnp.broadcast_to(data_latents[None], (16,) + data_latents.shape), COL_GROUP, 0, 0
    ).reshape(16 * piece, WIDTH)

    noise_norms = jnp.sum(jnp.square(noise_full.astype(jnp.float32)), axis=1)
    data_norms = jnp.sum(jnp.square(columns.astype(jnp.float32)), axis=1)
    products = lax.dot_general(
        noise_full, columns, (((1,), (1,)), ((), ())), preferred_element_type=jnp.float32
    )
    cost = noise_norms[:, None] + data_norms[None, :] - 2.0 * products

    row_lse = log_sum_exp(spread(log_sum_exp(-cost / epsilon, 1), ROW_GROUP), 0)
    row_dual = epsilon * log_mass - epsilon * row_lse
    col_lse = log_sum_exp(
        spread(log_sum_exp((row_dual[:, None] - cost) / epsilon, 0), COL_GROUP), 0
    )
    column_dual = epsilon * log_mass - epsilon * col_lse

    plan = jnp.exp((row_dual[:, None] + column_dual[None, :] - cost) / epsilon - log_mass)
    scale = None
    for iteration in range(2):
        scaled = plan if scale is None else plan * scale[None, :]
        row_sum = jnp.sum(spread(jnp.sum(scaled, axis=1), ROW_GROUP), axis=0)
        col_sum = jnp.sum(spread(jnp.sum(plan / row_sum[:, None], axis=0), COL_GROUP), axis=0)
        scale = 1.0 / col_sum
    scaled = plan * scale[None, :]
    totals = jnp.sum(scaled, axis=1)
    weights = scaled.astype(jnp.bfloat16)
    partial = jnp.dot(weights, columns, preferred_element_type=jnp.float32)

    high = totals.astype(jnp.bfloat16)
    low = (totals - high.astype(jnp.float32)).astype(jnp.bfloat16)
    tail = jnp.concatenate(
        [jnp.broadcast_to(high[:, None], (1024, 64)), jnp.broadcast_to(low[:, None], (1024, 64))], 1
    )
    halves = partial.astype(jnp.bfloat16).reshape(2, 8, piece, WIDTH)
    tails = tail.reshape(2, 8, piece, 128)

    def with_tail(a, b):
        return jnp.concatenate([a, b], axis=-1)

    def half(which):
        return with_tail(
            lax.dynamic_index_in_dim(halves, which, 0, False),
            lax.dynamic_index_in_dim(tails, which, 0, False),
        )

    def add(a, b):
        a32, b32 = a.astype(jnp.float32), b.astype(jnp.float32)
        body = a32[..., :WIDTH] + b32[..., :WIDTH]
        mass = a32[..., WIDTH : WIDTH + 64] + a32[..., WIDTH + 64 :]
        mass = mass + b32[..., WIDTH : WIDTH + 64] + b32[..., WIDTH + 64 :]
        return body, mass

    def packed(body, mass):
        upper = mass.astype(jnp.bfloat16)
        lower = (mass - upper.astype(jnp.float32)).astype(jnp.bfloat16)
        return jnp.concatenate([body.astype(jnp.bfloat16), upper, lower], axis=-1)

    own_half = packed(*add(half(core), swap_core(half(1 - core))))
    z = lax.axis_index("z")

    def own(offset):
        return lax.dynamic_index_in_dim(own_half, (z + offset) % 8, 0, False)

    right, left = own(4), own(5)
    right = shift_z(right, 1)
    for k in (3, 2, 1):
        right, left = (
            shift_z(packed(*add(right, own(k))), 1),
            shift_z(left if k == 3 else packed(*add(left, own(8 - k))), -1),
        )
    body, mass = add(right, left)
    body = body + own(0)[..., :WIDTH].astype(jnp.float32)
    mass = mass + own(0)[..., WIDTH : WIDTH + 64].astype(jnp.float32)
    mass = mass + own(0)[..., WIDTH + 64 :].astype(jnp.float32)
    target = body / mass[:, :1]
    return (target - noise_latents.astype(jnp.float32)).astype(jnp.bfloat16)


def solution(mesh):
    fine = Mesh(mesh.devices.reshape(SIZES), AXES)
    rows = P(AXES, None)
    return jax.shard_map(
        per_device, mesh=fine, in_specs=(rows, rows), out_specs=rows, check_vma=False
    )
```

time: 640 us -> 196 us (0.31)
  blocking collectives: 372 us -> 57.4 us
  waiting for transfers between devices: 202 us -> 60.9 us
  starting transfers between devices: 0.08 us -> 22.5 us
    all_gather x14 -> x0, blocking collectives: 372 us -> none  [merged(): gathered = jax.tree.map(lambda a: lax.all_gather(a, axis), part)]
    all_gather x2 -> x1, waiting for transfers between devices: 129 us -> 33.4 us  [per_device(): along_z = lax.all_gather(noise_latents, 'z', axis=0, tiled=True)]
    reduce_scatter x1 -> x0, waiting for transfers between devices: 71.7 us -> none  [per_device(): lax.psum_scatter(jnp.dot(weights, columns, preferred_element_type=jnp.flo...]
    all_to_all x0 -> x5, blocking collectives: none -> 57.4 us  [spread(): return lax.all_to_all(copies, group, 0, 0).reshape(16, vector.shape[0])]
    ppermute x0 -> x9, waiting for transfers between devices: none -> 20.4 us  [the longest x7 15.6 us: shift_z(): lax.ppermute(a, AXES, device_pairs(lambda x, yh, c, yl, z: (x, yh, c, yl,...]
    reduce_max x6 -> x3, other arithmetic: 16.9 us -> 2.85 us  [log_sum_exp(): top = jnp.max(values, axis=axis)]
    all_to_all x0 -> x2, starting transfers between devices: none -> 12.3 us  [the longest x1 7.48 us: per_device(): lax.all_to_all(jnp.broadcast_to(data_latents[None], (16,) + data_latents....]
    ppermute x0 -> x9, starting transfers between devices: none -> 10.2 us  [the longest x7 10.1 us: shift_z(): lax.ppermute(a, AXES, device_pairs(lambda x, yh, c, yl, z: (x, yh, c, yl,...]
  transfers between devices with their start and end apart: 3 -> 12, of which waited for: 3 -> 8; matrix products, arithmetic and copies ran while one was open for 0% -> 2% of each run, Pallas kernels for 0% -> 0%
where the time goes in v1:
time: 196 us
  waiting for transfers between devices  60.9 us (31%)
  blocking collectives  57.4 us (29%)
  other arithmetic  24.9 us (13%)
  starting transfers between devices  22.5 us (11%)
  between operations  13.9 us (7%)
  local copies, waits for them, and re-layouts  8.33 us (4%)
  matrix products  7.79 us (4%)
    all_to_all x5, blocking collectives, spread(): return lax.all_to_all(copies, group, 0, 0).reshape(16, vector.shape[0])  57.4 us
    all_gather x1, waiting for transfers between devices, per_device(): along_z = lax.all_gather(noise_latents, 'z', axis=0, tiled=True)  33.4 us
    ppermute x7, waiting for transfers between devices, shift_z(): lax.ppermute(a, AXES, device_pairs(lambda x, yh, c, yl, z: (x, yh, c, yl,...  15.6 us
    ppermute x7, starting transfers between devices, shift_z(): lax.ppermute(a, AXES, device_pairs(lambda x, yh, c, yl, z: (x, yh, c, yl,...  10.1 us
    all_to_all x1, starting transfers between devices, per_device(): lax.all_to_all(jnp.broadcast_to(data_latents[None], (16,) + data_latents....  7.48 us
    reduce_sum x2, other arithmetic, per_device(): jnp.sum(plan / row_sum[:, None], axis=0)  7.11 us
    all_to_all x1, waiting for transfers between devices, spread(): return lax.all_to_all(copies, group, 0, 0).reshape(16, vector.shape[0])  6.3 us
    reduce_sum x4, other arithmetic, per_device(): row_sum = jnp.sum(spread(jnp.sum(scaled, axis=1), ROW_GROUP), axis=0)  6.3 us
  transfers between devices with their start and end apart: 12, of which 8 were waited for; matrix products, arithmetic and copies ran while one was open for 2% of the time, Pallas kernels for 0%

profile of v1, /device:TPU:2, one launch (start us, length us, event | category | flops | bytes accessed | tf_op | source)
XLA Modules:
  0.0 195.7 jit_solution(1715887249097666777)
XLA Ops:
  7.3 2.5 %broadcast_in_dim.26 = bf16[16,64,1024]{2,1,0:T(8,128)(2,1)} broadcast(bf16[64,1024]{1,0:T(8,128)(2,1)} %param.3), dimensions={1,2} | broadcast | bytes 2228224 | tf_op jit(solution)/shard_map/broadcast_in_dim | solution.py:70
  9.8 7.5 %all-to-all-start = ((bf16[16,64,1024]{2,1,0:T(8,128)(2,1)}), bf16[16,64,1024]{2,1,0:T(8,128)(2,1)S(1)}, u32[]{:S(2)}, u32[]{:S(2)}) async-start(bf16[16,64,1024]{2,1,0:T(8,128)(2,1)} %broadcast_in_dim.26), calls=%async_computation | async-start | bytes 4194304 | tf_op jit(solution)/shard_map/all_to_all | solution.py:69
  17.3 33.4 %all-gather.2.cloned.1.call-done = bf16[512,1024]{1,0:T(8,128)(2,1)} async-done(((bf16[64,1024]{1,0:T(8,128)(2,1)}), bf16[512,1024]{1,0:T(8,128)(2,1)}) %all-gather.2.cloned.1.call-update) | async-done | bytes 1048592 | tf_op jit(solution)/shard_map/all_gather | solution.py:64
  55.4 2.5 %fusion = (f32[1024]{0:T(1024)S(1)}, f32[1024,1024]{0,1:T(8,128)S(1)}) fusion(bf16[1024,1024]{1,0:T(8,128)(2,1)S(1)} %bitcast.52, bf16[512,1024]{1,0:T(8,128)(2,1)S(1)} %get-tuple-element.22, bf16[512,1024]{1,0:T(8,128)(2,1)S(1)} %get-tuple-element.21, f32[1024]{0:T(1024)S(1)} %add.245, f32[1024]{0:T(1024)S(1)} %multiply_reduce_fusion.2), kind=kOutput, calls=%fused_computation.13 | convolution fusion | flops 2157968384 | bytes 8400896 | tf_op jit(solution)/shard_map/dot_general | solution.py:75
  60.6 12.4 %all_to_all.35 = f32[16,8,128]{2,1,0:T(8,128)S(1)} all-to-all(f32[16,8,128]{2,1,0:T(8,128)S(1)} %broadcast_in_dim.27), channel_id=1, replica_groups=mesh['x'=4,'yh'=2,'core'=2,'yl'=2,'z'=8] {'core','z'}, dimensions={0} | all-to-all | bytes 131072 | tf_op jit(solution)/shard_map/all_to_all | solution.py:48
  73.1 2.8 %fusion.1 = f32[1024]{0:T(1024)S(1)} fusion(f32[1024,1024]{0,1:T(8,128)} %copy-done, f32[1024]{0:T(1024)S(1)} %subtract_bitcast_fusion.1), kind=kLoop, calls=%fused_computation.14 | loop fusion | flops 3144704 | bytes 4202496 | tf_op jit(solution)/shard_map/reduce_max | solution.py:52
  77.6 13.1 %all_to_all.36 = f32[16,8,128]{2,1,0:T(8,128)S(1)} all-to-all(f32[16,8,128]{2,1,0:T(8,128)S(1)} %broadcast_in_dim.28), channel_id=1, replica_groups=mesh['x'=4,'yh'=2,'core'=2,'yl'=2,'z'=8] {'x','yh','yl'}, dimensions={0} | all-to-all | bytes 131072 | tf_op jit(solution)/shard_map/all_to_all | solution.py:48
  90.7 3.2 %fusion.19 = f32[1024]{0:T(1024)S(1)} fusion(f32[1024,1024]{0,1:T(8,128)} %copy-done, f32[1024]{0:T(1024)S(1)} %subtract_bitcast_fusion, f32[1024]{0:T(1024)S(1)} %subtract_bitcast_fusion.1), kind=kLoop, calls=%fused_computation.93 | loop fusion | flops 5241856 | bytes 4206592 | tf_op jit(solution)/shard_map/reduce_sum | solution.py:91
  93.9 10.5 %all_to_all.37 = f32[16,8,128]{2,1,0:T(8,128)S(1)} all-to-all(f32[16,8,128]{2,1,0:T(8,128)S(1)} %broadcast_in_dim.30), channel_id=1, replica_groups=mesh['x'=4,'yh'=2,'core'=2,'yl'=2,'z'=8] {'core','z'}, dimensions={0} | all-to-all | bytes 131072 | tf_op jit(solution)/shard_map/all_to_all | solution.py:48
  104.5 3.6 %divide_reduce_fusion.1 = f32[1024]{0:T(1024)S(1)} fusion(f32[1024]{0:T(1024)S(1)} %bitcast.57, f32[1024,1024]{0,1:T(8,128)} %copy-done, f32[1024]{0:T(1024)S(1)} %subtract_bitcast_fusion, f32[1024]{0:T(1024)S(1)} %subtract_bitcast_fusion.1), kind=kLoop, calls=%fused_computation.10 | loop fusion | flops 6290432 | bytes 4210688 | tf_op jit(solution)/shard_map/reduce_sum | solution.py:92
  108.0 10.9 %all_to_all.38 = f32[16,8,128]{2,1,0:T(8,128)S(1)} all-to-all(f32[16,8,128]{2,1,0:T(8,128)S(1)} %broadcast_in_dim.32), channel_id=1, replica_groups=mesh['x'=4,'yh'=2,'core'=2,'yl'=2,'z'=8] {'x','yh','yl'}, dimensions={0} | all-to-all | bytes 131072 | tf_op jit(solution)/shard_map/all_to_all | solution.py:48
  118.9 3.0 %multiply_reduce_fusion = f32[1024]{0:T(1024)S(1)} fusion(f32[1024]{0:T(1024)S(1)} %divide_bitcast_fusion.1, f32[1024,1024]{0,1:T(8,128)} %copy-done, f32[1024]{0:T(1024)S(1)} %subtract_bitcast_fusion, f32[1024]{0:T(1024)S(1)} %subtract_bitcast_fusion.1), kind=kLoop, calls=%fused_computation | loop fusion | flops 6290432 | bytes 4210688 | tf_op jit(solution)/shard_map/reduce_sum | solution.py:91
  122.0 10.5 %all_to_all.39 = f32[16,8,128]{2,1,0:T(8,128)S(1)} all-to-all(f32[16,8,128]{2,1,0:T(8,128)S(1)} %broadcast_in_dim.34), channel_id=1, replica_groups=mesh['x'=4,'yh'=2,'core'=2,'yl'=2,'z'=8] {'core','z'}, dimensions={0} | all-to-all | bytes 131072 | tf_op jit(solution)/shard_map/all_to_all | solution.py:48
  132.5 3.6 %divide_reduce_fusion = f32[1024]{0:T(1024)S(1)} fusion(f32[1024]{0:T(1024)S(1)} %bitcast.60, f32[1024,1024]{0,1:T(8,128)} %copy-done, f32[1024]{0:T(1024)S(1)} %subtract_bitcast_fusion, f32[1024]{0:T(1024)S(1)} %subtract_bitcast_fusion.1), kind=kLoop, calls=%fused_computation.9 | loop fusion | flops 6290432 | bytes 4210688 | tf_op jit(solution)/shard_map/reduce_sum | solution.py:92
  136.7 4.8 %all-to-all-start.6 = ((f32[16,8,128]{2,1,0:T(8,128)}), f32[16,8,128]{2,1,0:T(8,128)S(1)}, u32[]{:S(2)}, u32[]{:S(2)}) async-start(f32[16,8,128]{2,1,0:T(8,128)} %broadcast_in_dim.36), calls=%async_computation.6 | async-start | bytes 131072 | tf_op jit(solution)/shard_map/all_to_all | solution.py:48
  141.6 6.3 %all-to-all-done.6 = f32[16,8,128]{2,1,0:T(8,128)S(1)} async-done(((f32[16,8,128]{2,1,0:T(8,128)}), f32[16,8,128]{2,1,0:T(8,128)S(1)}, u32[]{:S(2)}, u32[]{:S(2)}) %all-to-all-start.6) | async-done | bytes 65568 | tf_op jit(solution)/shard_map/all_to_all | solution.py:48
  147.9 5.3 %fusion.5 = bf16[1024,1024]{1,0:T(8,128)(2,1)S(1)} fusion(bf16[1024,1024]{1,0:T(8,128)(2,1)S(1)} %bitcast.53, f32[1024]{0:T(1024)S(1)} %divide_bitcast_fusion, f32[1024,1024]{0,1:T(8,128)} %copy-done, f32[1024]{0:T(1024)S(1)} %subtract_bitcast_fusion, f32[1024]{0:T(1024)S(1)} %subtract_bitcast_fusion.1), kind=kOutput, calls=%fused_computation.20 | convolution fusion | flops 2154823680 | bytes 8400896 | tf_op jit(solution)/shard_map/dot_general | solution.py:97
  156.1 2.5 %collective-permute-done.1 = bf16[8,64,1152]{2,1,0:T(8,128)(2,1)S(1)} collective-permute-done((bf16[8,64,1152]{2,1,0:T(8,128)(2,1)S(1)}, bf16[8,64,1152]{2,1,0:T(8,128)(2,1)S(1)}, u32[]{:S(2)}, u32[]{:S(2)}) %collective-permute-start.1) | collective-permute-done | bytes 1179680 | tf_op jit(solution)/shard_map/ppermute | solution.py:42
  164.0 3.8 %collective-permute-done.2 = bf16[64,1152]{1,0:T(8,128)(2,1)S(1)} collective-permute-done((bf16[64,1152]{1,0:T(8,128)(2,1)S(1)}, bf16[64,1152]{1,0:T(8,128)(2,1)S(1)}, u32[]{:S(2)}, u32[]{:S(2)}) %collective-permute-start.2) | collective-permute-done | bytes 147488 | tf_op jit(solution)/shard_map/ppermute | solution.py:38
  168.5 3.3 %collective-permute-start.7 = (bf16[64,1152]{1,0:T(8,128)(2,1)S(1)}, bf16[64,1152]{1,0:T(8,128)(2,1)S(1)}, u32[]{:S(2)}, u32[]{:S(2)}) collective-permute-start(bf16[64,1152]{1,0:T(8,128)(2,1)S(1)} %concatenate.38), channel_id=1, source_target_pairs={{0,7},{1,0},{2,1},{3,2},{4,3},{5,4},{6,5},{7,6},{8,15},{9,8},{10,9... | collective-permute-start | bytes 442376 | tf_op jit(solution)/shard_map/ppermute | solution.py:38
  171.7 2.8 %collective-permute-done.3 = bf16[64,1152]{1,0:T(8,128)(2,1)S(1)} collective-permute-done((bf16[64,1152]{1,0:T(8,128)(2,1)S(1)}, bf16[64,1152]{1,0:T(8,128)(2,1)S(1)}, u32[]{:S(2)}, u32[]{:S(2)}) %collective-permute-start.3) | collective-permute-done | bytes 147488 | tf_op jit(solution)/shard_map/ppermute | solution.py:38
  175.1 3.3 %collective-permute-start.8 = (bf16[64,1152]{1,0:T(8,128)(2,1)S(1)}, bf16[64,1152]{1,0:T(8,128)(2,1)S(1)}, u32[]{:S(2)}, u32[]{:S(2)}) collective-permute-start(bf16[64,1152]{1,0:T(8,128)(2,1)S(1)} %concatenate.39), channel_id=1, source_target_pairs={{0,7},{1,0},{2,1},{3,2},{4,3},{5,4},{6,5},{7,6},{8,15},{9,8},{10,9... | collective-permute-start | bytes 442376 | tf_op jit(solution)/shard_map/ppermute | solution.py:38
  178.4 2.8 %collective-permute-done.4 = bf16[64,1152]{1,0:T(8,128)(2,1)S(1)} collective-permute-done((bf16[64,1152]{1,0:T(8,128)(2,1)S(1)}, bf16[64,1152]{1,0:T(8,128)(2,1)S(1)}, u32[]{:S(2)}, u32[]{:S(2)}) %collective-permute-start.4) | collective-permute-done | bytes 147488 | tf_op jit(solution)/shard_map/ppermute | solution.py:38
  181.7 6.2 %collective-permute-done.5 = bf16[64,1152]{1,0:T(8,128)(2,1)S(1)} collective-permute-done((bf16[64,1152]{1,0:T(8,128)(2,1)S(1)}, bf16[64,1152]{1,0:T(8,128)(2,1)S(1)}, u32[]{:S(2)}, u32[]{:S(2)}) %collective-permute-start.5) | collective-permute-done | bytes 147488 | tf_op jit(solution)/shard_map/ppermute | solution.py:38
  (89 shorter events, 21.2 us)
Async XLA Ops:
  6.5 44.1 %all-gather.2.cloned.1.call-start = ((), (), s32[]{:S(2)}) async-start(), calls=%async_computation.7 | async-start | bytes 1179648 | tf_op jit(solution)/shard_map/all_gather | solution.py:64
  9.8 40.9 %all-to-all-start = ((bf16[16,64,1024]{2,1,0:T(8,128)(2,1)}), bf16[16,64,1024]{2,1,0:T(8,128)(2,1)S(1)}, u32[]{:S(2)}, u32[]{:S(2)}) async-start(bf16[16,64,1024]{2,1,0:T(8,128)(2,1)} %broadcast_in_dim.26), calls=%async_computation | async-start | bytes 4194304 | tf_op jit(solution)/shard_map/all_to_all | solution.py:69
  50.7 2.9 %collective-permute-start = (bf16[512,1024]{1,0:T(8,128)(2,1)}, bf16[512,1024]{1,0:T(8,128)(2,1)S(1)}, u32[]{:S(2)}, u32[]{:S(2)}) collective-permute-start(bf16[512,1024]{1,0:T(8,128)(2,1)} %all-gather.2.cloned.1.call-done), channel_id=1, source_target_pairs={{0,16},{1,17},{2,18},{3,19},{4,20},{5,21},{6,22},{7,23},{8,24},{9,... | collective-permute-start | bytes 3145736 | tf_op jit(solution)/shard_map/ppermute | solution.py:42
  57.9 1.9 copy-start
  73.1 3.4 %copy-start.1 = (f32[1024,1024]{0,1:T(8,128)S(1)}, f32[1024,1024]{0,1:T(8,128)}, u32[]{:S(2)}) copy-start(f32[1024,1024]{0,1:T(8,128)} %copy-done) | copy-start | bytes 12582916
  136.7 11.1 %all-to-all-start.6 = ((f32[16,8,128]{2,1,0:T(8,128)}), f32[16,8,128]{2,1,0:T(8,128)S(1)}, u32[]{:S(2)}, u32[]{:S(2)}) async-start(f32[16,8,128]{2,1,0:T(8,128)} %broadcast_in_dim.36), calls=%async_computation.6 | async-start | bytes 131072 | tf_op jit(solution)/shard_map/all_to_all | solution.py:48
  147.9 5.3 %copy-start.2 = (f32[1024,1024]{0,1:T(8,128)S(1)}, f32[1024,1024]{0,1:T(8,128)}, u32[]{:S(2)}) copy-start(f32[1024,1024]{0,1:T(8,128)} %copy-done) | copy-start | bytes 12582916
  155.7 2.9 %collective-permute-start.1 = (bf16[8,64,1152]{2,1,0:T(8,128)(2,1)S(1)}, bf16[8,64,1152]{2,1,0:T(8,128)(2,1)S(1)}, u32[]{:S(2)}, u32[]{:S(2)}) collective-permute-start(bf16[8,64,1152]{2,1,0:T(8,128)(2,1)S(1)} %pad_maximum_fusion.2), channel_id=1, source_target_pairs={{0,16},{1,17},{2,18},{3,19},{4,20},{5,21},{6,22},{7,23},{8,24},{9,... | collective-permute-start | bytes 3538952 | tf_op jit(solution)/shard_map/ppermute | solution.py:42
  160.6 7.2 %collective-permute-start.2 = (bf16[64,1152]{1,0:T(8,128)(2,1)S(1)}, bf16[64,1152]{1,0:T(8,128)(2,1)S(1)}, u32[]{:S(2)}, u32[]{:S(2)}) collective-permute-start(bf16[64,1152]{1,0:T(8,128)(2,1)S(1)} %get-tuple-element.30), channel_id=1, source_target_pairs={{0,1},{1,2},{2,3},{3,4},{4,5},{5,6},{6,7},{7,0},{8,9},{9,10},{10,1... | collective-permute-start | bytes 442376 | tf_op jit(solution)/shard_map/ppermute | solution.py:38
  161.7 6.5 %collective-permute-start.6 = (bf16[64,1152]{1,0:T(8,128)(2,1)S(1)}, bf16[64,1152]{1,0:T(8,128)(2,1)S(1)}, u32[]{:S(2)}, u32[]{:S(2)}) collective-permute-start(bf16[64,1152]{1,0:T(8,128)(2,1)S(1)} %get-tuple-element.26), channel_id=1, source_target_pairs={{0,7},{1,0},{2,1},{3,2},{4,3},{5,4},{6,5},{7,6},{8,15},{9,8},{10,9... | collective-permute-start | bytes 442376 | tf_op jit(solution)/shard_map/ppermute | solution.py:38
  167.9 20.2 %copy-start.3 = (bf16[64,1024]{1,0:T(8,128)(2,1)S(1)}, bf16[64,1024]{1,0:T(8,128)(2,1)}, u32[]{:S(2)}) copy-start(bf16[64,1024]{1,0:T(8,128)(2,1)} %param.2) | copy-start | bytes 393220
  168.1 6.4 %collective-permute-start.3 = (bf16[64,1152]{1,0:T(8,128)(2,1)S(1)}, bf16[64,1152]{1,0:T(8,128)(2,1)S(1)}, u32[]{:S(2)}, u32[]{:S(2)}) collective-permute-start(bf16[64,1152]{1,0:T(8,128)(2,1)S(1)} %concatenate.35), channel_id=1, source_target_pairs={{0,1},{1,2},{2,3},{3,4},{4,5},{5,6},{6,7},{7,0},{8,9},{9,10},{10,1... | collective-permute-start | bytes 442376 | tf_op jit(solution)/shard_map/ppermute | solution.py:38
  168.5 6.4 %collective-permute-start.7 = (bf16[64,1152]{1,0:T(8,128)(2,1)S(1)}, bf16[64,1152]{1,0:T(8,128)(2,1)S(1)}, u32[]{:S(2)}, u32[]{:S(2)}) collective-permute-start(bf16[64,1152]{1,0:T(8,128)(2,1)S(1)} %concatenate.38), channel_id=1, source_target_pairs={{0,7},{1,0},{2,1},{3,2},{4,3},{5,4},{6,5},{7,6},{8,15},{9,8},{10,9... | collective-permute-start | bytes 442376 | tf_op jit(solution)/shard_map/ppermute | solution.py:38
  174.8 6.4 %collective-permute-start.4 = (bf16[64,1152]{1,0:T(8,128)(2,1)S(1)}, bf16[64,1152]{1,0:T(8,128)(2,1)S(1)}, u32[]{:S(2)}, u32[]{:S(2)}) collective-permute-start(bf16[64,1152]{1,0:T(8,128)(2,1)S(1)} %concatenate.36), channel_id=1, source_target_pairs={{0,1},{1,2},{2,3},{3,4},{4,5},{5,6},{6,7},{7,0},{8,9},{9,10},{10,1... | collective-permute-start | bytes 442376 | tf_op jit(solution)/shard_map/ppermute | solution.py:38
  175.1 6.4 %collective-permute-start.8 = (bf16[64,1152]{1,0:T(8,128)(2,1)S(1)}, bf16[64,1152]{1,0:T(8,128)(2,1)S(1)}, u32[]{:S(2)}, u32[]{:S(2)}) collective-permute-start(bf16[64,1152]{1,0:T(8,128)(2,1)S(1)} %concatenate.39), channel_id=1, source_target_pairs={{0,7},{1,0},{2,1},{3,2},{4,3},{5,4},{6,5},{7,6},{8,15},{9,8},{10,9... | collective-permute-start | bytes 442376 | tf_op jit(solution)/shard_map/ppermute | solution.py:38
  181.5 6.4 %collective-permute-start.5 = (bf16[64,1152]{1,0:T(8,128)(2,1)S(1)}, bf16[64,1152]{1,0:T(8,128)(2,1)S(1)}, u32[]{:S(2)}, u32[]{:S(2)}) collective-permute-start(bf16[64,1152]{1,0:T(8,128)(2,1)S(1)} %concatenate.37), channel_id=1, source_target_pairs={{0,1},{1,2},{2,3},{3,4},{4,5},{5,6},{6,7},{7,0},{8,9},{9,10},{10,1... | collective-permute-start | bytes 442376 | tf_op jit(solution)/shard_map/ppermute | solution.py:38
Sparse Core Ops, SparseCore 0:
  9.1 41.4 all-gather.1

commit v2 on v1

v2 whole, which is shorter than its diff:
```python
import math

import jax
import jax.numpy as jnp
from jax import lax
from jax.sharding import Mesh
from jax.sharding import PartitionSpec as P

WIDTH = 1024
eps_factor = 0.3

AXES = ("x", "yh", "core", "yl", "z")
SIZES = (4, 2, 2, 2, 8)
ROW_GROUP = ("core", "z")
COL_GROUP = ("x", "yh", "yl")


def device_pairs(move):
    pairs = []
    for x in range(4):
        for yh in range(2):
            for core in range(2):
                for yl in range(2):
                    for z in range(8):
                        place = (x, yh, core, yl, z)
                        pairs.append((number(place), number(move(*place))))
    return pairs


def number(place):
    index = 0
    for size, at in zip(SIZES, place):
        index = index * size + at % size
    return index


def shift_z(a, by):
    return lax.ppermute(a, AXES, device_pairs(lambda x, yh, c, yl, z: (x, yh, c, yl, z + by)))


def swap_core(a):
    return lax.ppermute(a, AXES, device_pairs(lambda x, yh, c, yl, z: (x, yh, 1 - c, yl, z)))


def spread(vector, group):
    wide = vector.reshape(1, 8, 128)
    copies = jnp.broadcast_to(wide, (16, 8, 128))
    return lax.all_to_all(copies, group, 0, 0).reshape(16, vector.shape[0])


def log_sum_exp(values, axis):
    top = jnp.max(values, axis=axis)
    total = jnp.sum(jnp.exp(values - jnp.expand_dims(top, axis)), axis=axis)
    return top + jnp.log(total)


def put(whole, part, at):
    return lax.dynamic_update_index_in_dim(whole, part, at, 0)


def pick(whole, at):
    return lax.dynamic_index_in_dim(whole, at, 0, False)


def added(a, b):
    return (a.astype(jnp.float32) + b.astype(jnp.float32)).astype(jnp.bfloat16)


def gather_z(part):
    z = lax.axis_index("z")
    whole = put(jnp.zeros((8,) + part.shape, part.dtype), part, z)
    right = left = part
    for k in (1, 2, 3, 4):
        right = shift_z(right, 1)
        whole = put(whole, right, jnp.bitwise_and(z - k, 7))
        if k < 4:
            left = shift_z(left, -1)
            whole = put(whole, left, jnp.bitwise_and(z + k, 7))
    return whole


def scatter_z(parts):
    z = lax.axis_index("z")

    def own(offset):
        return pick(parts, jnp.bitwise_and(z + offset, 7))

    right, left = shift_z(own(4), 1), shift_z(own(5), -1)
    for k in (3, 2, 1):
        right = shift_z(added(right, own(k)), 1)
        if k > 1:
            left = shift_z(added(left, own(9 - k)), -1)
    last = [a.astype(jnp.float32) for a in (right, left, own(0))]
    return last[0] + last[1] + last[2]


def per_device(noise_latents, data_latents):
    piece = noise_latents.shape[0]
    batch = piece * 256
    epsilon = eps_factor * math.sqrt(WIDTH)
    log_mass = -math.log(batch)
    core = lax.axis_index("core")

    columns = lax.all_to_all(
        jnp.broadcast_to(data_latents[None], (16,) + data_latents.shape), COL_GROUP, 0, 0
    ).reshape(16 * piece, WIDTH)
    along_z = gather_z(noise_latents)
    both = put(jnp.zeros((2,) + along_z.shape, along_z.dtype), along_z, core)
    noise_full = put(both, swap_core(along_z), 1 - core).reshape(16 * piece, WIDTH)

    noise_norms = jnp.sum(jnp.square(noise_full.astype(jnp.float32)), axis=1)
    data_norms = jnp.sum(jnp.square(columns.astype(jnp.float32)), axis=1)
    products = lax.dot_general(
        noise_full, columns, (((1,), (1,)), ((), ())), preferred_element_type=jnp.float32
    )
    cost = noise_norms[:, None] + data_norms[None, :] - 2.0 * products

    row_lse = log_sum_exp(spread(log_sum_exp(-cost / epsilon, 1), ROW_GROUP), 0)
    row_dual = epsilon * log_mass - epsilon * row_lse
    col_lse = log_sum_exp(
        spread(log_sum_exp((row_dual[:, None] - cost) / epsilon, 0), COL_GROUP), 0
    )
    column_dual = epsilon * log_mass - epsilon * col_lse

    plan = lax.optimization_barrier(
        jnp.exp((row_dual[:, None] + column_dual[None, :] - cost) / epsilon - log_mass)
    )
    row_sum = jnp.sum(spread(jnp.sum(plan, axis=1), ROW_GROUP), axis=0)
    col_sum = jnp.sum(spread(jnp.sum(plan * (1.0 / row_sum)[:, None], axis=0), COL_GROUP), axis=0)
    row_sum = jnp.sum(spread(jnp.sum(plan * (1.0 / col_sum)[None, :], axis=1), ROW_GROUP), axis=0)
    col_sum = jnp.sum(spread(jnp.sum(plan * (1.0 / row_sum)[:, None], axis=0), COL_GROUP), axis=0)

    scaled = plan * (1.0 / col_sum)[None, :]
    weights = scaled.astype(jnp.bfloat16)
    row_total = jnp.sum(spread(jnp.sum(scaled, axis=1), ROW_GROUP), axis=0)
    partial = jnp.dot(weights, columns, preferred_element_type=jnp.float32)
    halves = partial.astype(jnp.bfloat16).reshape(2, 8, piece, WIDTH)

    own_half = added(pick(halves, core), swap_core(pick(halves, 1 - core)))
    summed_up = scatter_z(own_half)
    z = lax.axis_index("z")
    own_total = lax.dynamic_slice_in_dim(row_total, (core * 8 + z) * piece, piece, 0)
    target = summed_up / own_total[:, None]
    return (target - noise_latents.astype(jnp.float32)).astype(jnp.bfloat16)


def solution(mesh):
    fine = Mesh(mesh.devices.reshape(SIZES), AXES)
    rows = P(AXES, None)
    return jax.shard_map(
        per_device, mesh=fine, in_specs=(rows, rows), out_specs=rows, check_vma=False
    )
```

time: 196 us -> 190 us (0.969); the launches traced: 196 us -> 188 us
  waiting for transfers between devices: 60.9 us -> 39.5 us
  between operations: 13.9 us -> 0.42 us
  blocking collectives: 57.4 us -> 68.8 us
  starting transfers between devices: 22.5 us -> 33.7 us
  local copies, waits for them, and re-layouts: 8.33 us -> 10.6 us
    all_gather x1 -> x0, waiting for transfers between devices: 33.4 us -> none  [per_device(): along_z = lax.all_gather(noise_latents, 'z', axis=0, tiled=True)]
    ppermute x7 -> x14, starting transfers between devices: 10.1 us -> 22.6 us  [shift_z(): lax.ppermute(a, AXES, device_pairs(lambda x, yh, c, yl, z: (x, yh, c, yl,...]
    all_to_all x5 -> x6, blocking collectives: 57.4 us -> 68.8 us  [spread(): return lax.all_to_all(copies, group, 0, 0).reshape(16, vector.shape[0])]
    ppermute x7 -> x14, waiting for transfers between devices: 15.6 us -> 24.5 us  [shift_z(): lax.ppermute(a, AXES, device_pairs(lambda x, yh, c, yl, z: (x, yh, c, yl,...]
    exp x0 -> x1, other arithmetic: none -> 5 us  [per_device(): jnp.exp((row_dual[:, None] + column_dual[None, :] - cost) / epsilon - log...]
    unnamed x8 -> x10, local copies, waits for them, and re-layouts: 2.51 us -> 5.16 us
    reduce_sum x9 -> x10, other arithmetic: 15 us -> 12.7 us  [the longest x2 5.07 us: per_device(): jnp.sum(plan * (1.0 / row_sum)[:, None], axis=0)]
    all_to_all x1, waiting for transfers between devices: 0.01 us -> 2.03 us  [per_device(): lax.all_to_all(jnp.broadcast_to(data_latents[None], (16,) + data_latents....]
  transfers between devices with their start and end apart: 12 -> 18, of which waited for: 8 -> 10; matrix products, arithmetic and copies ran while one was open for 2% -> 4% of each run, Pallas kernels for 0% -> 0%
where the time goes in v2:
time: 190 us; the launch traced here: 188 us
  blocking collectives  68.8 us (36%)
  waiting for transfers between devices  39.5 us (21%)
  starting transfers between devices  33.7 us (18%)
  other arithmetic  26 us (14%)
  local copies, waits for them, and re-layouts  10.6 us (6%)
  matrix products  8.71 us (5%)
    all_to_all x6, blocking collectives, spread(): return lax.all_to_all(copies, group, 0, 0).reshape(16, vector.shape[0])  68.8 us
    ppermute x14, waiting for transfers between devices, shift_z(): lax.ppermute(a, AXES, device_pairs(lambda x, yh, c, yl, z: (x, yh, c, yl,...  24.5 us
    ppermute x14, starting transfers between devices, shift_z(): lax.ppermute(a, AXES, device_pairs(lambda x, yh, c, yl, z: (x, yh, c, yl,...  22.6 us
    all_to_all x1, waiting for transfers between devices, spread(): return lax.all_to_all(copies, group, 0, 0).reshape(16, vector.shape[0])  7.86 us
    all_to_all x1, starting transfers between devices, per_device(): lax.all_to_all(jnp.broadcast_to(data_latents[None], (16,) + data_latents....  7.48 us
    unnamed x10, local copies, waits for them, and re-layouts  5.16 us
    reduce_sum x2, other arithmetic, per_device(): jnp.sum(plan * (1.0 / row_sum)[:, None], axis=0)  5.07 us
    ppermute x2, waiting for transfers between devices, swap_core(): lax.ppermute(a, AXES, device_pairs(lambda x, yh, c, yl, z: (x, yh, 1 - c,...  5.03 us
  transfers between devices with their start and end apart: 18, of which 10 were waited for; matrix products, arithmetic and copies ran while one was open for 4% of the time, Pallas kernels for 0%

profile of v2, /device:TPU:2, one launch (start us, length us, event | category | flops | bytes accessed | tf_op | source)
XLA Modules:
  0.0 187.7 jit_solution(8502651768925532379)
XLA Ops:
  1.9 4.0 %collective-permute-start.1 = (bf16[64,1024]{1,0:T(8,128)(2,1)}, bf16[64,1024]{1,0:T(8,128)(2,1)S(1)}, u32[]{:S(2)}, u32[]{:S(2)}) collective-permute-start(bf16[64,1024]{1,0:T(8,128)(2,1)} %param.2), channel_id=1, source_target_pairs={{0,7},{1,0},{2,1},{3,2},{4,3},{5,4},{6,5},{7,6},{8,15},{9,8},{10,9... | collective-permute-start | bytes 393224 | tf_op jit(solution)/shard_map/ppermute | solution.py:38
  8.5 7.5 %all-to-all-start = ((bf16[16,64,1024]{2,1,0:T(8,128)(2,1)}), bf16[16,64,1024]{2,1,0:T(8,128)(2,1)S(1)}, u32[]{:S(2)}, u32[]{:S(2)}) async-start(bf16[16,64,1024]{2,1,0:T(8,128)(2,1)} %broadcast_in_dim.115), calls=%async_computation | async-start | bytes 4194304 | tf_op jit(solution)/shard_map/all_to_all | solution.py:104
  16.2 3.2 %collective-permute-start.3 = (bf16[64,1024]{1,0:T(8,128)(2,1)S(1)}, bf16[64,1024]{1,0:T(8,128)(2,1)S(1)}, u32[]{:S(2)}, u32[]{:S(2)}) collective-permute-start(bf16[64,1024]{1,0:T(8,128)(2,1)S(1)} %collective-permute-done.1), channel_id=1, source_target_pairs={{0,7},{1,0},{2,1},{3,2},{4,3},{5,4},{6,5},{7,6},{8,15},{9,8},{10,9... | collective-permute-start | bytes 393224 | tf_op jit(solution)/shard_map/ppermute | solution.py:38
  19.5 2.9 %collective-permute-done.2 = bf16[64,1024]{1,0:T(8,128)(2,1)S(1)} collective-permute-done((bf16[64,1024]{1,0:T(8,128)(2,1)S(1)}, bf16[64,1024]{1,0:T(8,128)(2,1)S(1)}, u32[]{:S(2)}, u32[]{:S(2)}) %collective-permute-start.2) | collective-permute-done | bytes 131104 | tf_op jit(solution)/shard_map/ppermute | solution.py:38
  22.4 3.2 %collective-permute-start.5 = (bf16[64,1024]{1,0:T(8,128)(2,1)S(1)}, bf16[64,1024]{1,0:T(8,128)(2,1)S(1)}, u32[]{:S(2)}, u32[]{:S(2)}) collective-permute-start(bf16[64,1024]{1,0:T(8,128)(2,1)S(1)} %collective-permute-done.3), channel_id=1, source_target_pairs={{0,7},{1,0},{2,1},{3,2},{4,3},{5,4},{6,5},{7,6},{8,15},{9,8},{10,9... | collective-permute-start | bytes 393224 | tf_op jit(solution)/shard_map/ppermute | solution.py:38
  25.6 2.9 %collective-permute-done.4 = bf16[64,1024]{1,0:T(8,128)(2,1)S(1)} collective-permute-done((bf16[64,1024]{1,0:T(8,128)(2,1)S(1)}, bf16[64,1024]{1,0:T(8,128)(2,1)S(1)}, u32[]{:S(2)}, u32[]{:S(2)}) %collective-permute-start.4) | collective-permute-done | bytes 131104 | tf_op jit(solution)/shard_map/ppermute | solution.py:38
  28.6 6.1 %collective-permute-done.6 = bf16[64,1024]{1,0:T(8,128)(2,1)S(1)} collective-permute-done((bf16[64,1024]{1,0:T(8,128)(2,1)S(1)}, bf16[64,1024]{1,0:T(8,128)(2,1)S(1)}, u32[]{:S(2)}, u32[]{:S(2)}) %collective-permute-start.6) | collective-permute-done | bytes 131104 | tf_op jit(solution)/shard_map/ppermute | solution.py:38
  43.4 4.2 %fusion = (f32[1024]{0:T(1024)S(1)}, f32[1024,1024]{1,0:T(8,128)S(1)}) fusion(bf16[1024,1024]{1,0:T(8,128)(2,1)} %bitcast.77, bf16[1024,1024]{1,0:T(8,128)(2,1)S(1)} %bitcast.75, f32[1024]{0:T(1024)S(1)} %add.195, f32[1024]{0:T(1024)S(1)} %add.193), kind=kOutput, calls=%fused_computation.13 | convolution fusion | flops 2153774080 | bytes 8400896 | tf_op jit(solution)/shard_map/dot_general | solution.py:113
  50.5 13.4 %all_to_all.40 = f32[16,8,128]{2,1,0:T(8,128)S(1)} all-to-all(f32[16,8,128]{2,1,0:T(8,128)S(1)} %broadcast_in_dim.116), channel_id=1, replica_groups=mesh['x'=4,'yh'=2,'core'=2,'yl'=2,'z'=8] {'core','z'}, dimensions={0} | all-to-all | bytes 131072 | tf_op jit(solution)/shard_map/all_to_all | solution.py:48
  63.9 2.8 %fusion.1 = f32[1024]{0:T(1024)S(1)} fusion(f32[1024,1024]{1,0:T(8,128)} %copy-done, f32[1024]{0:T(1024)S(1)} %subtract_bitcast_fusion.1), kind=kLoop, calls=%fused_computation.14 | loop fusion | flops 3144704 | bytes 4202496 | tf_op jit(solution)/shard_map/reduce_max | solution.py:52
  68.2 12.7 %all_to_all.41 = f32[16,8,128]{2,1,0:T(8,128)S(1)} all-to-all(f32[16,8,128]{2,1,0:T(8,128)S(1)} %broadcast_in_dim.117), channel_id=1, replica_groups=mesh['x'=4,'yh'=2,'core'=2,'yl'=2,'z'=8] {'x','yh','yl'}, dimensions={0} | all-to-all | bytes 131072 | tf_op jit(solution)/shard_map/all_to_all | solution.py:48
  81.0 5.0 %add_exponential_fusion = f32[1024,1024]{1,0:T(8,128)} fusion(f32[1024,1024]{1,0:T(8,128)} %copy-done, f32[1024]{0:T(1024)S(1)} %subtract_bitcast_fusion, f32[1024]{0:T(1024)S(1)} %subtract_bitcast_fusion.1), kind=kLoop, calls=%fused_computation.3 | loop fusion | flops 4194304 | bytes 8396800 | tf_op jit(solution)/shard_map/exp | solution.py:126
  88.4 10.5 %all_to_all.42 = f32[16,8,128]{2,1,0:T(8,128)S(1)} all-to-all(f32[16,8,128]{2,1,0:T(8,128)S(1)} %broadcast_in_dim.119), channel_id=1, replica_groups=mesh['x'=4,'yh'=2,'core'=2,'yl'=2,'z'=8] {'core','z'}, dimensions={0} | all-to-all | bytes 131072 | tf_op jit(solution)/shard_map/all_to_all | solution.py:48
  101.5 10.9 %all_to_all.43 = f32[16,8,128]{2,1,0:T(8,128)S(1)} all-to-all(f32[16,8,128]{2,1,0:T(8,128)S(1)} %broadcast_in_dim.121), channel_id=1, replica_groups=mesh['x'=4,'yh'=2,'core'=2,'yl'=2,'z'=8] {'x','yh','yl'}, dimensions={0} | all-to-all | bytes 131072 | tf_op jit(solution)/shard_map/all_to_all | solution.py:48
  115.0 10.5 %all_to_all.44 = f32[16,8,128]{2,1,0:T(8,128)S(1)} all-to-all(f32[16,8,128]{2,1,0:T(8,128)S(1)} %broadcast_in_dim.123), channel_id=1, replica_groups=mesh['x'=4,'yh'=2,'core'=2,'yl'=2,'z'=8] {'core','z'}, dimensions={0} | all-to-all | bytes 131072 | tf_op jit(solution)/shard_map/all_to_all | solution.py:48
  128.1 10.9 %all_to_all.45 = f32[16,8,128]{2,1,0:T(8,128)S(1)} all-to-all(f32[16,8,128]{2,1,0:T(8,128)S(1)} %broadcast_in_dim.125), channel_id=1, replica_groups=mesh['x'=4,'yh'=2,'core'=2,'yl'=2,'z'=8] {'x','yh','yl'}, dimensions={0} | all-to-all | bytes 131072 | tf_op jit(solution)/shard_map/all_to_all | solution.py:48
  139.0 4.5 %fusion.5 = bf16[1024,1024]{1,0:T(8,128)(2,1)S(1)} fusion(bf16[1024,1024]{1,0:T(8,128)(2,1)S(1)} %bitcast.76, f32[1024,1024]{1,0:T(8,128)} %add_exponential_fusion, f32[1024]{0:T(1024)S(1)} %divide_bitcast_fusion), kind=kOutput, calls=%fused_computation.19 | convolution fusion | flops 2150629376 | bytes 8392704 | tf_op jit(solution)/shard_map/dot_general | solution.py:136
  152.7 3.5 %collective-permute-done.9 = bf16[64,1024]{1,0:T(8,128)(2,1)S(1)} collective-permute-done((bf16[64,1024]{1,0:T(8,128)(2,1)S(1)}, bf16[64,1024]{1,0:T(8,128)(2,1)S(1)}, u32[]{:S(2)}, u32[]{:S(2)}) %collective-permute-start.9) | collective-permute-done | bytes 131104 | tf_op jit(solution)/shard_map/ppermute | solution.py:38
  156.3 6.2 %collective-permute-done.10 = bf16[64,1024]{1,0:T(8,128)(2,1)S(1)} collective-permute-done((bf16[64,1024]{1,0:T(8,128)(2,1)S(1)}, bf16[64,1024]{1,0:T(8,128)(2,1)S(1)}, u32[]{:S(2)}, u32[]{:S(2)}) %collective-permute-start.10) | collective-permute-done | bytes 131104 | tf_op jit(solution)/shard_map/ppermute | solution.py:38
  162.7 3.2 %collective-permute-start.14 = (bf16[64,1024]{1,0:T(8,128)(2,1)S(1)}, bf16[64,1024]{1,0:T(8,128)(2,1)S(1)}, u32[]{:S(2)}, u32[]{:S(2)}) collective-permute-start(bf16[64,1024]{1,0:T(8,128)(2,1)S(1)} %get-tuple-element.8), channel_id=1, source_target_pairs={{0,7},{1,0},{2,1},{3,2},{4,3},{5,4},{6,5},{7,6},{8,15},{9,8},{10,9... | collective-permute-start | bytes 393224 | tf_op jit(solution)/shard_map/ppermute | solution.py:38
  165.9 2.9 %collective-permute-done.11 = bf16[64,1024]{1,0:T(8,128)(2,1)S(1)} collective-permute-done((bf16[64,1024]{1,0:T(8,128)(2,1)S(1)}, bf16[64,1024]{1,0:T(8,128)(2,1)S(1)}, u32[]{:S(2)}, u32[]{:S(2)}) %collective-permute-start.11) | collective-permute-done | bytes 131104 | tf_op jit(solution)/shard_map/ppermute | solution.py:38
  169.0 3.3 %collective-permute-start.15 = (bf16[64,1024]{1,0:T(8,128)(2,1)S(1)}, bf16[64,1024]{1,0:T(8,128)(2,1)S(1)}, u32[]{:S(2)}, u32[]{:S(2)}) collective-permute-start(bf16[64,1024]{1,0:T(8,128)(2,1)S(1)} %get-tuple-element.6), channel_id=1, source_target_pairs={{0,7},{1,0},{2,1},{3,2},{4,3},{5,4},{6,5},{7,6},{8,15},{9,8},{10,9... | collective-permute-start | bytes 393224 | tf_op jit(solution)/shard_map/ppermute | solution.py:38
  175.5 3.5 %all-to-all-start.7 = ((f32[16,8,128]{2,1,0:T(8,128)}), f32[16,8,128]{2,1,0:T(8,128)S(1)}, u32[]{:S(2)}, u32[]{:S(2)}) async-start(f32[16,8,128]{2,1,0:T(8,128)} %broadcast_in_dim.127), calls=%async_computation.7 | async-start | bytes 131072 | tf_op jit(solution)/shard_map/all_to_all | solution.py:48
  179.0 7.9 %all-to-all-done.7 = f32[16,8,128]{2,1,0:T(8,128)S(1)} async-done(((f32[16,8,128]{2,1,0:T(8,128)}), f32[16,8,128]{2,1,0:T(8,128)S(1)}, u32[]{:S(2)}, u32[]{:S(2)}) %all-to-all-start.7) | async-done | bytes 65568 | tf_op jit(solution)/shard_map/all_to_all | solution.py:48
  (88 shorter events, 41.6 us)
Async XLA Ops:
  0.0 16.1 %copy-start.4 = (bf16[64,1024]{1,0:T(8,128)(2,1)S(1)}, bf16[64,1024]{1,0:T(8,128)(2,1)}, u32[]{:S(2)}) copy-start(bf16[64,1024]{1,0:T(8,128)(2,1)} %param.2) | copy-start | bytes 393220
  0.0 16.1 %collective-permute-start = (bf16[64,1024]{1,0:T(8,128)(2,1)}, bf16[64,1024]{1,0:T(8,128)(2,1)S(1)}, u32[]{:S(2)}, u32[]{:S(2)}) collective-permute-start(bf16[64,1024]{1,0:T(8,128)(2,1)} %param.2), channel_id=1, source_target_pairs={{0,1},{1,2},{2,3},{3,4},{4,5},{5,6},{6,7},{7,0},{8,9},{9,10},{10,1... | collective-permute-start | bytes 393224 | tf_op jit(solution)/shard_map/ppermute | solution.py:38
  1.9 14.3 %collective-permute-start.1 = (bf16[64,1024]{1,0:T(8,128)(2,1)}, bf16[64,1024]{1,0:T(8,128)(2,1)S(1)}, u32[]{:S(2)}, u32[]{:S(2)}) collective-permute-start(bf16[64,1024]{1,0:T(8,128)(2,1)} %param.2), channel_id=1, source_target_pairs={{0,7},{1,0},{2,1},{3,2},{4,3},{5,4},{6,5},{7,6},{8,15},{9,8},{10,9... | collective-permute-start | bytes 393224 | tf_op jit(solution)/shard_map/ppermute | solution.py:38
  8.5 34.4 %all-to-all-start = ((bf16[16,64,1024]{2,1,0:T(8,128)(2,1)}), bf16[16,64,1024]{2,1,0:T(8,128)(2,1)S(1)}, u32[]{:S(2)}, u32[]{:S(2)}) async-start(bf16[16,64,1024]{2,1,0:T(8,128)(2,1)} %broadcast_in_dim.115), calls=%async_computation | async-start | bytes 4194304 | tf_op jit(solution)/shard_map/all_to_all | solution.py:104
  16.1 6.3 %collective-permute-start.2 = (bf16[64,1024]{1,0:T(8,128)(2,1)S(1)}, bf16[64,1024]{1,0:T(8,128)(2,1)S(1)}, u32[]{:S(2)}, u32[]{:S(2)}) collective-permute-start(bf16[64,1024]{1,0:T(8,128)(2,1)S(1)} %collective-permute-done), channel_id=1, source_target_pairs={{0,1},{1,2},{2,3},{3,4},{4,5},{5,6},{6,7},{7,0},{8,9},{9,10},{10,1... | collective-permute-start | bytes 393224 | tf_op jit(solution)/shard_map/ppermute | solution.py:38
  16.2 6.2 %collective-permute-start.3 = (bf16[64,1024]{1,0:T(8,128)(2,1)S(1)}, bf16[64,1024]{1,0:T(8,128)(2,1)S(1)}, u32[]{:S(2)}, u32[]{:S(2)}) collective-permute-start(bf16[64,1024]{1,0:T(8,128)(2,1)S(1)} %collective-permute-done.1), channel_id=1, source_target_pairs={{0,7},{1,0},{2,1},{3,2},{4,3},{5,4},{6,5},{7,6},{8,15},{9,8},{10,9... | collective-permute-start | bytes 393224 | tf_op jit(solution)/shard_map/ppermute | solution.py:38
  22.4 6.2 %collective-permute-start.4 = (bf16[64,1024]{1,0:T(8,128)(2,1)S(1)}, bf16[64,1024]{1,0:T(8,128)(2,1)S(1)}, u32[]{:S(2)}, u32[]{:S(2)}) collective-permute-start(bf16[64,1024]{1,0:T(8,128)(2,1)S(1)} %collective-permute-done.2), channel_id=1, source_target_pairs={{0,1},{1,2},{2,3},{3,4},{4,5},{5,6},{6,7},{7,0},{8,9},{9,10},{10,1... | collective-permute-start | bytes 393224 | tf_op jit(solution)/shard_map/ppermute | solution.py:38
  22.4 6.2 %collective-permute-start.5 = (bf16[64,1024]{1,0:T(8,128)(2,1)S(1)}, bf16[64,1024]{1,0:T(8,128)(2,1)S(1)}, u32[]{:S(2)}, u32[]{:S(2)}) collective-permute-start(bf16[64,1024]{1,0:T(8,128)(2,1)S(1)} %collective-permute-done.3), channel_id=1, source_target_pairs={{0,7},{1,0},{2,1},{3,2},{4,3},{5,4},{6,5},{7,6},{8,15},{9,8},{10,9... | collective-permute-start | bytes 393224 | tf_op jit(solution)/shard_map/ppermute | solution.py:38
  28.5 6.2 %collective-permute-start.6 = (bf16[64,1024]{1,0:T(8,128)(2,1)S(1)}, bf16[64,1024]{1,0:T(8,128)(2,1)S(1)}, u32[]{:S(2)}, u32[]{:S(2)}) collective-permute-start(bf16[64,1024]{1,0:T(8,128)(2,1)S(1)} %collective-permute-done.4), channel_id=1, source_target_pairs={{0,1},{1,2},{2,3},{3,4},{4,5},{5,6},{6,7},{7,0},{8,9},{9,10},{10,1... | collective-permute-start | bytes 393224 | tf_op jit(solution)/shard_map/ppermute | solution.py:38
  34.7 2.9 %collective-permute-start.7 = (bf16[8,64,1024]{2,1,0:T(8,128)(2,1)S(1)}, bf16[8,64,1024]{2,1,0:T(8,128)(2,1)}, u32[]{:S(2)}, u32[]{:S(2)}) collective-permute-start(bf16[8,64,1024]{2,1,0:T(8,128)(2,1)S(1)} %bitcast_dynamic-update-slice_fusion.2), channel_id=1, source_target_pairs={{0,16},{1,17},{2,18},{3,19},{4,20},{5,21},{6,22},{7,23},{8,24},{9,... | collective-permute-start | bytes 3145736 | tf_op jit(solution)/shard_map/ppermute | solution.py:42
  38.9 1.3 copy-start.2
  47.5 2.0 %copy-start = (f32[1024,1024]{1,0:T(8,128)}, f32[1024,1024]{1,0:T(8,128)S(1)}, u32[]{:S(2)}) copy-start(f32[1024,1024]{1,0:T(8,128)S(1)} %get-tuple-element.12) | copy-start | bytes 12582916
  63.9 3.4 %copy-start.1 = (f32[1024,1024]{1,0:T(8,128)S(1)}, f32[1024,1024]{1,0:T(8,128)}, u32[]{:S(2)}) copy-start(f32[1024,1024]{1,0:T(8,128)} %copy-done) | copy-start | bytes 12582916
  143.5 1.3 copy-start.3
  144.9 2.7 %collective-permute-start.8 = (bf16[8,64,1024]{2,1,0:T(8,128)(2,1)S(1)}, bf16[8,64,1024]{2,1,0:T(8,128)(2,1)S(1)}, u32[]{:S(2)}, u32[]{:S(2)}) collective-permute-start(bf16[8,64,1024]{2,1,0:T(8,128)(2,1)S(1)} %dynamic-slice_bitcast_fusion), channel_id=1, source_target_pairs={{0,16},{1,17},{2,18},{3,19},{4,20},{5,21},{6,22},{7,23},{8,24},{9,... | collective-permute-start | bytes 3145736 | tf_op jit(solution)/shard_map/ppermute | solution.py:42
  149.4 6.8 %collective-permute-start.9 = (bf16[64,1024]{1,0:T(8,128)(2,1)S(1)}, bf16[64,1024]{1,0:T(8,128)(2,1)S(1)}, u32[]{:S(2)}, u32[]{:S(2)}) collective-permute-start(bf16[64,1024]{1,0:T(8,128)(2,1)S(1)} %get-tuple-element.9), channel_id=1, source_target_pairs={{0,1},{1,2},{2,3},{3,4},{4,5},{5,6},{6,7},{7,0},{8,9},{9,10},{10,1... | collective-permute-start | bytes 393224 | tf_op jit(solution)/shard_map/ppermute | solution.py:38
  150.4 5.9 %collective-permute-start.13 = (bf16[64,1024]{1,0:T(8,128)(2,1)S(1)}, bf16[64,1024]{1,0:T(8,128)(2,1)S(1)}, u32[]{:S(2)}, u32[]{:S(2)}) collective-permute-start(bf16[64,1024]{1,0:T(8,128)(2,1)S(1)} %get-tuple-element.10), channel_id=1, source_target_pairs={{0,7},{1,0},{2,1},{3,2},{4,3},{5,4},{6,5},{7,6},{8,15},{9,8},{10,9... | collective-permute-start | bytes 393224 | tf_op jit(solution)/shard_map/ppermute | solution.py:38
  156.2 6.3 %collective-permute-start.10 = (bf16[64,1024]{1,0:T(8,128)(2,1)S(1)}, bf16[64,1024]{1,0:T(8,128)(2,1)S(1)}, u32[]{:S(2)}, u32[]{:S(2)}) collective-permute-start(bf16[64,1024]{1,0:T(8,128)(2,1)S(1)} %fusion.13), channel_id=1, source_target_pairs={{0,1},{1,2},{2,3},{3,4},{4,5},{5,6},{6,7},{7,0},{8,9},{9,10},{10,1... | collective-permute-start | bytes 393224 | tf_op jit(solution)/shard_map/ppermute | solution.py:38
  162.6 6.3 %collective-permute-start.11 = (bf16[64,1024]{1,0:T(8,128)(2,1)S(1)}, bf16[64,1024]{1,0:T(8,128)(2,1)S(1)}, u32[]{:S(2)}, u32[]{:S(2)}) collective-permute-start(bf16[64,1024]{1,0:T(8,128)(2,1)S(1)} %get-tuple-element.7), channel_id=1, source_target_pairs={{0,1},{1,2},{2,3},{3,4},{4,5},{5,6},{6,7},{7,0},{8,9},{9,10},{10,1... | collective-permute-start | bytes 393224 | tf_op jit(solution)/shard_map/ppermute | solution.py:38
  162.7 6.2 %collective-permute-start.14 = (bf16[64,1024]{1,0:T(8,128)(2,1)S(1)}, bf16[64,1024]{1,0:T(8,128)(2,1)S(1)}, u32[]{:S(2)}, u32[]{:S(2)}) collective-permute-start(bf16[64,1024]{1,0:T(8,128)(2,1)S(1)} %get-tuple-element.8), channel_id=1, source_target_pairs={{0,7},{1,0},{2,1},{3,2},{4,3},{5,4},{6,5},{7,6},{8,15},{9,8},{10,9... | collective-permute-start | bytes 393224 | tf_op jit(solution)/shard_map/ppermute | solution.py:38
  168.9 18.1 %collective-permute-start.12 = (bf16[64,1024]{1,0:T(8,128)(2,1)S(1)}, bf16[64,1024]{1,0:T(8,128)(2,1)S(1)}, u32[]{:S(2)}, u32[]{:S(2)}) collective-permute-start(bf16[64,1024]{1,0:T(8,128)(2,1)S(1)} %get-tuple-element.5), channel_id=1, source_target_pairs={{0,1},{1,2},{2,3},{3,4},{4,5},{5,6},{6,7},{7,0},{8,9},{9,10},{10,1... | collective-permute-start | bytes 393224 | tf_op jit(solution)/shard_map/ppermute | solution.py:38
  169.0 18.0 %collective-permute-start.15 = (bf16[64,1024]{1,0:T(8,128)(2,1)S(1)}, bf16[64,1024]{1,0:T(8,128)(2,1)S(1)}, u32[]{:S(2)}, u32[]{:S(2)}) collective-permute-start(bf16[64,1024]{1,0:T(8,128)(2,1)S(1)} %get-tuple-element.6), channel_id=1, source_target_pairs={{0,7},{1,0},{2,1},{3,2},{4,3},{5,4},{6,5},{7,6},{8,15},{9,8},{10,9... | collective-permute-start | bytes 393224 | tf_op jit(solution)/shard_map/ppermute | solution.py:38
  175.5 11.4 %all-to-all-start.7 = ((f32[16,8,128]{2,1,0:T(8,128)}), f32[16,8,128]{2,1,0:T(8,128)S(1)}, u32[]{:S(2)}, u32[]{:S(2)}) async-start(f32[16,8,128]{2,1,0:T(8,128)} %broadcast_in_dim.127), calls=%async_computation.7 | async-start | bytes 131072 | tf_op jit(solution)/shard_map/all_to_all | solution.py:48

commit v3 on v2

v3 whole, which is shorter than its diff:
```python
import functools
import math

import jax
import jax.numpy as jnp
from jax import lax
from jax.experimental import pallas as pl
from jax.experimental.pallas import tpu as pltpu
from jax.sharding import Mesh
from jax.sharding import PartitionSpec as P

WIDTH = 1024
ROWS = 1024
eps_factor = 0.3

AXES = ("x", "yh", "core", "yl", "z")
SIZES = (4, 2, 2, 2, 8)
ROW_GROUP = ("core", "z")
COL_GROUP = ("x", "yh", "yl")

EPSILON = eps_factor * math.sqrt(WIDTH)
LOG2E = math.log2(math.e)
LOG2_MASS = -math.log2(16384)


def device_pairs(move):
    pairs = []
    for x in range(4):
        for yh in range(2):
            for core in range(2):
                for yl in range(2):
                    for z in range(8):
                        place = (x, yh, core, yl, z)
                        pairs.append((number(place), number(move(*place))))
    return pairs


def number(place):
    index = 0
    for size, at in zip(SIZES, place):
        index = index * size + at % size
    return index


def shift_z(a, by):
    return lax.ppermute(a, AXES, device_pairs(lambda x, yh, c, yl, z: (x, yh, c, yl, z + by)))


def swap_core(a):
    return lax.ppermute(a, AXES, device_pairs(lambda x, yh, c, yl, z: (x, yh, 1 - c, yl, z)))


def spread(copies, group):
    return lax.all_to_all(copies, group, 0, 0)


def put(whole, part, at):
    return lax.dynamic_update_index_in_dim(whole, part, at, 0)


def pick(whole, at):
    return lax.dynamic_index_in_dim(whole, at, 0, False)


def added(a, b):
    return (a.astype(jnp.float32) + b.astype(jnp.float32)).astype(jnp.bfloat16)


def gather_z(part):
    z = lax.axis_index("z")
    whole = put(jnp.zeros((8,) + part.shape, part.dtype), part, z)
    right = left = part
    for k in (1, 2, 3, 4):
        right = shift_z(right, 1)
        whole = put(whole, right, jnp.bitwise_and(z - k, 7))
        if k < 4:
            left = shift_z(left, -1)
            whole = put(whole, left, jnp.bitwise_and(z + k, 7))
    return whole


def scatter_z(parts):
    z = lax.axis_index("z")

    def own(offset):
        return pick(parts, jnp.bitwise_and(z + offset, 7))

    right, left = shift_z(own(4), 1), shift_z(own(5), -1)
    for k in (3, 2, 1):
        right = shift_z(added(right, own(k)), 1)
        if k > 1:
            left = shift_z(added(left, own(9 - k)), -1)
    last = [a.astype(jnp.float32) for a in (right, left, own(0))]
    return last[0] + last[1] + last[2]


def to_lanes(square):
    return jnp.concatenate([square[k : k + 1, :] for k in range(8)], axis=1)


def to_square(lanes):
    return jnp.concatenate([lanes[:, 128 * k : 128 * k + 128] for k in range(8)], axis=0)


def own_first(square):
    swapped = jnp.concatenate([square[4:, :], square[:4, :]], axis=0)
    return jnp.where(lax.axis_index("core") == 0, square, swapped)


def lse2(parts):
    top = jnp.max(parts, axis=0)
    return top + jnp.log2(jnp.sum(jnp.exp2(parts - top[None]), axis=0))


def send(out_ref, square):
    out_ref[...] = jnp.broadcast_to(square[None], (16, 8, 128))


def terms(lanes):
    high = lanes.astype(jnp.bfloat16)
    rest = lanes - high.astype(jnp.float32)
    low = rest.astype(jnp.bfloat16)
    zeros = jnp.zeros((14, ROWS), jnp.bfloat16)
    return jnp.concatenate([high, low, zeros], axis=0)


def down(row):
    return jnp.transpose(jnp.broadcast_to(row, (128, 128)))[:, :1]


def across(column):
    return jnp.transpose(jnp.broadcast_to(column, (128, 128)))[:1, :]


def square_sums(block):
    wide = block.astype(jnp.float32)
    return jnp.sum(wide * wide, axis=1, keepdims=True)


def scores_kernel(data_ref, own_ref, other_ref, score_ref, out_ref):
    scale = LOG2E / EPSILON
    data_norms = jnp.concatenate(
        [square_sums(data_ref[pl.ds(128 * k, 128), :]) for k in range(8)], axis=0
    )
    rows = []
    for k in range(4):
        source = own_ref if k < 2 else other_ref
        noise = source[pl.ds(256 * (k % 2), 256), :]
        noise_norms = jnp.concatenate(
            [across(square_sums(noise[:128])), across(square_sums(noise[128:]))], axis=1
        )
        products = lax.dot_general(
            data_ref[...], noise, (((1,), (1,)), ((), ())), preferred_element_type=jnp.float32
        )
        scores = (2.0 * products - (data_norms + noise_norms)) * scale
        score_ref[:, pl.ds(256 * k, 256)] = scores
        top = jnp.max(scores, axis=0, keepdims=True)
        total = jnp.sum(jnp.exp2(scores - top), axis=0, keepdims=True)
        rows.append(top + jnp.log2(total))
    send(out_ref, own_first(to_square(jnp.concatenate(rows, axis=1))))


def columns_kernel(score_ref, in_ref, dual_ref, out_ref):
    dual = own_first(LOG2_MASS - lse2(in_ref[...]))
    dual_ref[...] = dual
    along = to_lanes(dual)
    rows = []
    for k in range(8):
        shifted = score_ref[pl.ds(128 * k, 128), :] + along
        top = jnp.max(shifted, axis=1, keepdims=True)
        total = jnp.sum(jnp.exp2(shifted - top), axis=1, keepdims=True)
        rows.append(across(top + jnp.log2(total)))
    send(out_ref, jnp.concatenate(rows, axis=0))


def plan_kernel(score_ref, dual_ref, in_ref, plan_ref, out_ref):
    along = to_lanes(dual_ref[...])
    dual = LOG2_MASS - lse2(in_ref[...])
    sums = jnp.zeros((1, ROWS), jnp.float32)
    for k in range(8):
        part = pl.ds(128 * k, 128)
        lifted = down(dual[k : k + 1, :] - LOG2_MASS)
        plan = jnp.exp2(score_ref[part, :] + along + lifted)
        plan_ref[part, :] = plan.astype(jnp.bfloat16)
        sums = sums + jnp.sum(plan, axis=0, keepdims=True)
    send(out_ref, own_first(to_square(sums)))


def column_sums_kernel(plan_ref, in_ref, out_ref):
    scale = own_first(1.0 / jnp.sum(in_ref[...], axis=0))
    sums = lax.dot_general(
        terms(to_lanes(scale)),
        plan_ref[...],
        (((1,), (1,)), ((), ())),
        preferred_element_type=jnp.float32,
    )
    send(out_ref, to_square(sums[0:1, :] + sums[1:2, :]))


def row_sums_kernel(plan_ref, in_ref, out_ref):
    scale = 1.0 / jnp.sum(in_ref[...], axis=0)
    sums = jnp.dot(terms(to_lanes(scale)), plan_ref[...], preferred_element_type=jnp.float32)
    send(out_ref, own_first(to_square(sums[0:1, :] + sums[1:2, :])))


def targets_kernel(plan_ref, in_ref, data_ref, own_ref, other_ref, out_ref, weight_ref):
    scale = 1.0 / jnp.sum(in_ref[...], axis=0)
    sums = jnp.zeros((1, ROWS), jnp.float32)
    for k in range(8):
        part = pl.ds(128 * k, 128)
        weights = plan_ref[part, :].astype(jnp.float32) * down(scale[k : k + 1, :])
        weight_ref[part, :] = weights.astype(jnp.bfloat16)
        sums = sums + jnp.sum(weights, axis=0, keepdims=True)
    send(out_ref, own_first(to_square(sums)))
    for k in range(4):
        partial = lax.dot_general(
            weight_ref[:, pl.ds(256 * k, 256)],
            data_ref[...],
            (((0,), (0,)), ((), ())),
            preferred_element_type=jnp.float32,
        ).astype(jnp.bfloat16)
        home = own_ref if k < 2 else other_ref
        home[pl.ds(256 * (k % 2), 256), :] = partial


SQUARE = jax.ShapeDtypeStruct((8, 128), jnp.float32)
COPIES = jax.ShapeDtypeStruct((16, 8, 128), jnp.float32)


def in_vmem(rows, dtype):
    return pltpu.VMEM((rows, 1024), dtype)


def run(kernel, outs, *args, flops=0, scratch=()):
    return pl.pallas_call(
        kernel,
        out_shape=outs,
        in_specs=[pl.BlockSpec(memory_space=pltpu.VMEM)] * len(args),
        out_specs=jax.tree.map(lambda _: pl.BlockSpec(memory_space=pltpu.VMEM), outs),
        scratch_shapes=scratch,
        compiler_params=pltpu.CompilerParams(vmem_limit_bytes=40 * 1024 * 1024),
        cost_estimate=pl.CostEstimate(flops=flops, bytes_accessed=4 << 20, transcendentals=0),
    )(*args)


def keep(a):
    return pltpu.with_memory_space_constraint(a, pltpu.VMEM)


def per_device(noise_latents, data_latents):
    piece = noise_latents.shape[0]
    core, z = lax.axis_index("core"), lax.axis_index("z")

    columns = spread(
        jnp.broadcast_to(data_latents[None], (16,) + data_latents.shape), COL_GROUP
    ).reshape(ROWS, WIDTH)
    own_rows = gather_z(noise_latents).reshape(ROWS // 2, WIDTH)
    other_rows = swap_core(own_rows)

    scores, parts = run(
        scores_kernel, (in_vmem(ROWS, jnp.float32), COPIES), columns, own_rows, other_rows
    )
    scores = keep(scores)
    row_dual, parts = run(columns_kernel, (SQUARE, COPIES), scores, spread(parts, ROW_GROUP))
    plan, parts = run(
        plan_kernel,
        (in_vmem(ROWS, jnp.bfloat16), COPIES),
        scores,
        row_dual,
        spread(parts, COL_GROUP),
    )
    plan = keep(plan)
    parts = run(column_sums_kernel, COPIES, plan, spread(parts, ROW_GROUP))
    parts = run(row_sums_kernel, COPIES, plan, spread(parts, COL_GROUP))
    parts = run(column_sums_kernel, COPIES, plan, spread(parts, ROW_GROUP))
    half = jax.ShapeDtypeStruct((ROWS // 2, WIDTH), jnp.bfloat16)
    own_half, other_half, parts = run(
        targets_kernel,
        (half, half, COPIES),
        plan,
        spread(parts, COL_GROUP),
        columns,
        scratch=[pltpu.VMEM((ROWS, ROWS), jnp.bfloat16)],
    )
    row_total = jnp.sum(spread(parts, ROW_GROUP), axis=0).reshape(16, piece)

    own_half = added(own_half, swap_core(other_half)).reshape(8, piece, WIDTH)
    summed_up = scatter_z(own_half)
    target = summed_up / pick(row_total, core * 8 + z)[:, None]
    return (target - noise_latents.astype(jnp.float32)).astype(jnp.bfloat16)


def solution(mesh):
    fine = Mesh(mesh.devices.reshape(SIZES), AXES)
    rows = P(AXES, None)
    return jax.shard_map(
        per_device, mesh=fine, in_specs=(rows, rows), out_specs=rows, check_vma=False
    )
```

time: 190 us -> 159 us (0.84)
  other arithmetic: 26 us -> 1.35 us
  Pallas kernels: 0 us -> 11.1 us
  matrix products: 8.71 us -> 0 us
  local copies, waits for them, and re-layouts: 10.6 us -> 5.05 us
  waiting for transfers between devices: 39.5 us -> 36.4 us
    reduce_sum x16 -> x1, other arithmetic: 15.5 us -> 0.02 us  [per_device(): row_total = jnp.sum(spread(parts, ROW_GROUP), axis=0).reshape(16, piece)]
    pallas_call x0 -> x7, Pallas kernels: none -> 11.1 us  [run(): pl.pallas_call(kernel, out_shape=outs, in_specs=[pl.BlockSpec(memory_spac...]
    dot_general x2 -> x0, matrix products: 8.71 us -> none  [the longest x1 4.52 us: per_device(): partial = jnp.dot(weights, columns, preferred_element_type=jnp.float32)]
    exp x1 -> x0, other arithmetic: 5 us -> none  [per_device(): jnp.exp((row_dual[:, None] + column_dual[None, :] - cost) / epsilon - log...]
    unnamed x10 -> x6, local copies, waits for them, and re-layouts: 5.16 us -> 2.22 us
    reduce_max x3 -> x0, other arithmetic: 2.85 us -> none  [log_sum_exp(): top = jnp.max(values, axis=axis)]
    ppermute x14, waiting for transfers between devices: 24.5 us -> 22 us  [shift_z(): lax.ppermute(a, AXES, device_pairs(lambda x, yh, c, yl, z: (x, yh, c, yl,...]
  transfers between devices with their start and end apart: 18 -> 18, of which waited for: 10 -> 10; matrix products, arithmetic and copies ran while one was open for 4% -> 2% of each run, Pallas kernels for 0% -> 0%
where the time goes in v3:
time: 159 us; the launch traced here: 157 us
  blocking collectives  68.9 us (43%)
  waiting for transfers between devices  36.4 us (23%)
  starting transfers between devices  33.6 us (21%)
  Pallas kernels  11.1 us (7%)
  local copies, waits for them, and re-layouts  5.05 us (3%)
    all_to_all x6, blocking collectives, spread(): return lax.all_to_all(copies, group, 0, 0)  68.9 us
    ppermute x14, starting transfers between devices, shift_z(): lax.ppermute(a, AXES, device_pairs(lambda x, yh, c, yl, z: (x, yh, c, yl,...  22.4 us
    ppermute x14, waiting for transfers between devices, shift_z(): lax.ppermute(a, AXES, device_pairs(lambda x, yh, c, yl, z: (x, yh, c, yl,...  22 us
    all_to_all x2, starting transfers between devices, spread(): return lax.all_to_all(copies, group, 0, 0)  11.1 us
    pallas_call x7, Pallas kernels, run(): pl.pallas_call(kernel, out_shape=outs, in_specs=[pl.BlockSpec(memory_spac...  11.1 us
    all_to_all x2, waiting for transfers between devices, spread(): return lax.all_to_all(copies, group, 0, 0)  8.88 us
    ppermute x2, waiting for transfers between devices, swap_core(): lax.ppermute(a, AXES, device_pairs(lambda x, yh, c, yl, z: (x, yh, 1 - c,...  5.51 us
  transfers between devices with their start and end apart: 18, of which 10 were waited for; matrix products, arithmetic and copies ran while one was open for 2% of the time, Pallas kernels for 0%

profile of v3, /device:TPU:2, one launch (start us, length us, event | category | flops | bytes accessed | tf_op | source)
XLA Modules:
  0.0 156.7 jit_solution(17351600649682810001)
XLA Ops:
  1.9 3.9 %collective-permute-start.1 = (bf16[64,1024]{1,0:T(8,128)(2,1)}, bf16[64,1024]{1,0:T(8,128)(2,1)S(1)}, u32[]{:S(2)}, u32[]{:S(2)}) collective-permute-start(bf16[64,1024]{1,0:T(8,128)(2,1)} %param.2), channel_id=1, source_target_pairs={{0,7},{1,0},{2,1},{3,2},{4,3},{5,4},{6,5},{7,6},{8,15},{9,8},{10,9... | collective-permute-start | bytes 393224 | tf_op jit(solution)/shard_map/ppermute | solution.py:46
  5.9 2.5 %broadcast_in_dim.35 = bf16[16,64,1024]{2,1,0:T(8,128)(2,1)} broadcast(bf16[64,1024]{1,0:T(8,128)(2,1)} %param.3), dimensions={1,2} | broadcast | bytes 2228224 | tf_op jit(solution)/shard_map/broadcast_in_dim | solution.py:255
  8.4 7.6 %all-to-all-start = ((bf16[16,64,1024]{2,1,0:T(8,128)(2,1)}), bf16[16,64,1024]{2,1,0:T(8,128)(2,1)S(1)}, u32[]{:S(2)}, u32[]{:S(2)}) async-start(bf16[16,64,1024]{2,1,0:T(8,128)(2,1)} %broadcast_in_dim.35), calls=%async_computation | async-start | bytes 4194304 | tf_op jit(solution)/shard_map/all_to_all | solution.py:54
  16.2 3.2 %collective-permute-start.3 = (bf16[64,1024]{1,0:T(8,128)(2,1)S(1)}, bf16[64,1024]{1,0:T(8,128)(2,1)S(1)}, u32[]{:S(2)}, u32[]{:S(2)}) collective-permute-start(bf16[64,1024]{1,0:T(8,128)(2,1)S(1)} %collective-permute-done.1), channel_id=1, source_target_pairs={{0,7},{1,0},{2,1},{3,2},{4,3},{5,4},{6,5},{7,6},{8,15},{9,8},{10,9... | collective-permute-start | bytes 393224 | tf_op jit(solution)/shard_map/ppermute | solution.py:46
  19.5 2.9 %collective-permute-done.2 = bf16[64,1024]{1,0:T(8,128)(2,1)S(1)} collective-permute-done((bf16[64,1024]{1,0:T(8,128)(2,1)S(1)}, bf16[64,1024]{1,0:T(8,128)(2,1)S(1)}, u32[]{:S(2)}, u32[]{:S(2)}) %collective-permute-start.2) | collective-permute-done | bytes 131104 | tf_op jit(solution)/shard_map/ppermute | solution.py:46
  22.4 3.2 %collective-permute-start.5 = (bf16[64,1024]{1,0:T(8,128)(2,1)S(1)}, bf16[64,1024]{1,0:T(8,128)(2,1)S(1)}, u32[]{:S(2)}, u32[]{:S(2)}) collective-permute-start(bf16[64,1024]{1,0:T(8,128)(2,1)S(1)} %collective-permute-done.3), channel_id=1, source_target_pairs={{0,7},{1,0},{2,1},{3,2},{4,3},{5,4},{6,5},{7,6},{8,15},{9,8},{10,9... | collective-permute-start | bytes 393224 | tf_op jit(solution)/shard_map/ppermute | solution.py:46
  25.7 2.9 %collective-permute-done.4 = bf16[64,1024]{1,0:T(8,128)(2,1)S(1)} collective-permute-done((bf16[64,1024]{1,0:T(8,128)(2,1)S(1)}, bf16[64,1024]{1,0:T(8,128)(2,1)S(1)}, u32[]{:S(2)}, u32[]{:S(2)}) %collective-permute-start.4) | collective-permute-done | bytes 131104 | tf_op jit(solution)/shard_map/ppermute | solution.py:46
  28.6 6.1 %collective-permute-done.6 = bf16[64,1024]{1,0:T(8,128)(2,1)S(1)} collective-permute-done((bf16[64,1024]{1,0:T(8,128)(2,1)S(1)}, bf16[64,1024]{1,0:T(8,128)(2,1)S(1)}, u32[]{:S(2)}, u32[]{:S(2)}) %collective-permute-start.6) | collective-permute-done | bytes 131104 | tf_op jit(solution)/shard_map/ppermute | solution.py:46
  34.9 2.6 %collective-permute-done.7.other_ref = bf16[512,1024]{1,0:T(8,128)(2,1)S(1)} collective-permute-done((bf16[512,1024]{1,0:T(8,128)(2,1)S(1)}, bf16[512,1024]{1,0:T(8,128)(2,1)S(1)}, u32[]{:S(2)}, u32[]{:S(2)}) %collective-permute-start.7) | collective-permute-done | bytes 1048608 | tf_op jit(solution)/shard_map/ppermute | solution.py:50
  38.5 4.3 %all-to-all-done = bf16[16,64,1024]{2,1,0:T(8,128)(2,1)S(1)} async-done(((bf16[16,64,1024]{2,1,0:T(8,128)(2,1)}), bf16[16,64,1024]{2,1,0:T(8,128)(2,1)S(1)}, u32[]{:S(2)}, u32[]{:S(2)}) %all-to-all-start) | async-done | bytes 2097184 | tf_op jit(solution)/shard_map/all_to_all | solution.py:54
  44.1 3.4 %shard_map.28 = (f32[1024,1024]{1,0:T(8,128)S(1)}, f32[16,8,128]{2,1,0:T(8,128)S(1)}) custom-call(bf16[1024,1024]{1,0:T(8,128)(2,1)S(1)} %bitcast.43, bf16[512,1024]{1,0:T(8,128)(2,1)S(1)} %bitcast.46, bf16[512,1024]{1,0:T(8,128)(2,1)S(1)} %copy-done.1), custom_call_target="tpu_custom_call" | custom-call | bytes 4194304 | tf_op jit(solution)/shard_map/pallas_call | solution.py:235
  47.4 13.4 %all_to_all.40.in_ref = f32[16,8,128]{2,1,0:T(8,128)S(1)} all-to-all(f32[16,8,128]{2,1,0:T(8,128)S(1)} %get-tuple-element.15), channel_id=1, replica_groups=mesh['x'=4,'yh'=2,'core'=2,'yl'=2,'z'=8] {'core','z'}, dimensions={0} | all-to-all | bytes 131072 | tf_op jit(solution)/shard_map/all_to_all | solution.py:54
  62.0 12.7 %all_to_all.41.in_ref = f32[16,8,128]{2,1,0:T(8,128)S(1)} all-to-all(f32[16,8,128]{2,1,0:T(8,128)S(1)} %get-tuple-element.17), channel_id=1, replica_groups=mesh['x'=4,'yh'=2,'core'=2,'yl'=2,'z'=8] {'x','yh','yl'}, dimensions={0} | all-to-all | bytes 131072 | tf_op jit(solution)/shard_map/all_to_all | solution.py:54
  75.6 10.5 %all_to_all.42.in_ref = f32[16,8,128]{2,1,0:T(8,128)S(1)} all-to-all(f32[16,8,128]{2,1,0:T(8,128)S(1)} %get-tuple-element.19), channel_id=1, replica_groups=mesh['x'=4,'yh'=2,'core'=2,'yl'=2,'z'=8] {'core','z'}, dimensions={0} | all-to-all | bytes 131072 | tf_op jit(solution)/shard_map/all_to_all | solution.py:54
  86.8 10.9 %all_to_all.43.in_ref = f32[16,8,128]{2,1,0:T(8,128)S(1)} all-to-all(f32[16,8,128]{2,1,0:T(8,128)S(1)} %shard_map.31), channel_id=1, replica_groups=mesh['x'=4,'yh'=2,'core'=2,'yl'=2,'z'=8] {'x','yh','yl'}, dimensions={0} | all-to-all | bytes 131072 | tf_op jit(solution)/shard_map/all_to_all | solution.py:54
  98.0 10.5 %all_to_all.44.in_ref = f32[16,8,128]{2,1,0:T(8,128)S(1)} all-to-all(f32[16,8,128]{2,1,0:T(8,128)S(1)} %shard_map.32), channel_id=1, replica_groups=mesh['x'=4,'yh'=2,'core'=2,'yl'=2,'z'=8] {'core','z'}, dimensions={0} | all-to-all | bytes 131072 | tf_op jit(solution)/shard_map/all_to_all | solution.py:54
  109.2 10.9 %all_to_all.45.in_ref = f32[16,8,128]{2,1,0:T(8,128)S(1)} all-to-all(f32[16,8,128]{2,1,0:T(8,128)S(1)} %shard_map.33), channel_id=1, replica_groups=mesh['x'=4,'yh'=2,'core'=2,'yl'=2,'z'=8] {'x','yh','yl'}, dimensions={0} | all-to-all | bytes 131072 | tf_op jit(solution)/shard_map/all_to_all | solution.py:54
  120.1 4.0 %shard_map.34 = (bf16[512,1024]{1,0:T(8,128)(2,1)S(1)}, bf16[512,1024]{1,0:T(8,128)(2,1)}, f32[16,8,128]{2,1,0:T(8,128)}) custom-call(bf16[1024,1024]{1,0:T(8,128)(2,1)S(1)} %get-tuple-element.18.plan_ref, f32[16,8,128]{2,1,0:T(8,128)S(1)} %all_to_all.45.in_ref, bf16[1024,1024]{1,0:T(8,128)(2,1)S(1)} %bitcast.44), custom_call_target="tpu_custom_call" | custom-call | bytes 4194304 | tf_op jit(solution)/shard_map/pallas_call | solution.py:235
  124.1 2.9 %collective-permute-done.8 = bf16[512,1024]{1,0:T(8,128)(2,1)S(1)} collective-permute-done((bf16[512,1024]{1,0:T(8,128)(2,1)}, bf16[512,1024]{1,0:T(8,128)(2,1)S(1)}, u32[]{:S(2)}, u32[]{:S(2)}) %collective-permute-start.8) | collective-permute-done | bytes 1048608 | tf_op jit(solution)/shard_map/ppermute | solution.py:50
  130.7 3.5 %collective-permute-done.9 = bf16[64,1024]{1,0:T(8,128)(2,1)S(1)} collective-permute-done((bf16[64,1024]{1,0:T(8,128)(2,1)S(1)}, bf16[64,1024]{1,0:T(8,128)(2,1)S(1)}, u32[]{:S(2)}, u32[]{:S(2)}) %collective-permute-start.9) | collective-permute-done | bytes 131104 | tf_op jit(solution)/shard_map/ppermute | solution.py:46
  134.4 6.2 %collective-permute-done.10 = bf16[64,1024]{1,0:T(8,128)(2,1)S(1)} collective-permute-done((bf16[64,1024]{1,0:T(8,128)(2,1)S(1)}, bf16[64,1024]{1,0:T(8,128)(2,1)S(1)}, u32[]{:S(2)}, u32[]{:S(2)}) %collective-permute-start.10) | collective-permute-done | bytes 131104 | tf_op jit(solution)/shard_map/ppermute | solution.py:46
  140.7 3.2 %collective-permute-start.14 = (bf16[64,1024]{1,0:T(8,128)(2,1)S(1)}, bf16[64,1024]{1,0:T(8,128)(2,1)S(1)}, u32[]{:S(2)}, u32[]{:S(2)}) collective-permute-start(bf16[64,1024]{1,0:T(8,128)(2,1)S(1)} %get-tuple-element.26), channel_id=1, source_target_pairs={{0,7},{1,0},{2,1},{3,2},{4,3},{5,4},{6,5},{7,6},{8,15},{9,8},{10,9... | collective-permute-start | bytes 393224 | tf_op jit(solution)/shard_map/ppermute | solution.py:46
  143.9 3.5 %all-to-all-start.7 = ((f32[16,8,128]{2,1,0:T(8,128)}), f32[16,8,128]{2,1,0:T(8,128)S(1)}, u32[]{:S(2)}, u32[]{:S(2)}) async-start(f32[16,8,128]{2,1,0:T(8,128)} %get-tuple-element.22), calls=%async_computation.7 | async-start | bytes 131072 | tf_op jit(solution)/shard_map/all_to_all | solution.py:54
  150.8 4.5 %all-to-all-done.7 = f32[16,8,128]{2,1,0:T(8,128)S(1)} async-done(((f32[16,8,128]{2,1,0:T(8,128)}), f32[16,8,128]{2,1,0:T(8,128)S(1)}, u32[]{:S(2)}, u32[]{:S(2)}) %all-to-all-start.7) | async-done | bytes 65568 | tf_op jit(solution)/shard_map/all_to_all | solution.py:54
  (50 shorter events, 17.0 us)
Async XLA Ops:
  0.0 16.1 %collective-permute-start = (bf16[64,1024]{1,0:T(8,128)(2,1)}, bf16[64,1024]{1,0:T(8,128)(2,1)S(1)}, u32[]{:S(2)}, u32[]{:S(2)}) collective-permute-start(bf16[64,1024]{1,0:T(8,128)(2,1)} %param.2), channel_id=1, source_target_pairs={{0,1},{1,2},{2,3},{3,4},{4,5},{5,6},{6,7},{7,0},{8,9},{9,10},{10,1... | collective-permute-start | bytes 393224 | tf_op jit(solution)/shard_map/ppermute | solution.py:46
  1.9 14.3 %collective-permute-start.1 = (bf16[64,1024]{1,0:T(8,128)(2,1)}, bf16[64,1024]{1,0:T(8,128)(2,1)S(1)}, u32[]{:S(2)}, u32[]{:S(2)}) collective-permute-start(bf16[64,1024]{1,0:T(8,128)(2,1)} %param.2), channel_id=1, source_target_pairs={{0,7},{1,0},{2,1},{3,2},{4,3},{5,4},{6,5},{7,6},{8,15},{9,8},{10,9... | collective-permute-start | bytes 393224 | tf_op jit(solution)/shard_map/ppermute | solution.py:46
  8.4 7.7 %copy-start.2 = (bf16[64,1024]{1,0:T(8,128)(2,1)S(1)}, bf16[64,1024]{1,0:T(8,128)(2,1)}, u32[]{:S(2)}) copy-start(bf16[64,1024]{1,0:T(8,128)(2,1)} %param.2) | copy-start | bytes 393220
  8.4 34.5 %all-to-all-start = ((bf16[16,64,1024]{2,1,0:T(8,128)(2,1)}), bf16[16,64,1024]{2,1,0:T(8,128)(2,1)S(1)}, u32[]{:S(2)}, u32[]{:S(2)}) async-start(bf16[16,64,1024]{2,1,0:T(8,128)(2,1)} %broadcast_in_dim.35), calls=%async_computation | async-start | bytes 4194304 | tf_op jit(solution)/shard_map/all_to_all | solution.py:54
  16.1 6.3 %collective-permute-start.2 = (bf16[64,1024]{1,0:T(8,128)(2,1)S(1)}, bf16[64,1024]{1,0:T(8,128)(2,1)S(1)}, u32[]{:S(2)}, u32[]{:S(2)}) collective-permute-start(bf16[64,1024]{1,0:T(8,128)(2,1)S(1)} %collective-permute-done), channel_id=1, source_target_pairs={{0,1},{1,2},{2,3},{3,4},{4,5},{5,6},{6,7},{7,0},{8,9},{9,10},{10,1... | collective-permute-start | bytes 393224 | tf_op jit(solution)/shard_map/ppermute | solution.py:46
  16.2 6.2 %collective-permute-start.3 = (bf16[64,1024]{1,0:T(8,128)(2,1)S(1)}, bf16[64,1024]{1,0:T(8,128)(2,1)S(1)}, u32[]{:S(2)}, u32[]{:S(2)}) collective-permute-start(bf16[64,1024]{1,0:T(8,128)(2,1)S(1)} %collective-permute-done.1), channel_id=1, source_target_pairs={{0,7},{1,0},{2,1},{3,2},{4,3},{5,4},{6,5},{7,6},{8,15},{9,8},{10,9... | collective-permute-start | bytes 393224 | tf_op jit(solution)/shard_map/ppermute | solution.py:46
  22.4 6.2 %collective-permute-start.4 = (bf16[64,1024]{1,0:T(8,128)(2,1)S(1)}, bf16[64,1024]{1,0:T(8,128)(2,1)S(1)}, u32[]{:S(2)}, u32[]{:S(2)}) collective-permute-start(bf16[64,1024]{1,0:T(8,128)(2,1)S(1)} %collective-permute-done.2), channel_id=1, source_target_pairs={{0,1},{1,2},{2,3},{3,4},{4,5},{5,6},{6,7},{7,0},{8,9},{9,10},{10,1... | collective-permute-start | bytes 393224 | tf_op jit(solution)/shard_map/ppermute | solution.py:46
  22.4 6.2 %collective-permute-start.5 = (bf16[64,1024]{1,0:T(8,128)(2,1)S(1)}, bf16[64,1024]{1,0:T(8,128)(2,1)S(1)}, u32[]{:S(2)}, u32[]{:S(2)}) collective-permute-start(bf16[64,1024]{1,0:T(8,128)(2,1)S(1)} %collective-permute-done.3), channel_id=1, source_target_pairs={{0,7},{1,0},{2,1},{3,2},{4,3},{5,4},{6,5},{7,6},{8,15},{9,8},{10,9... | collective-permute-start | bytes 393224 | tf_op jit(solution)/shard_map/ppermute | solution.py:46
  28.6 6.2 %collective-permute-start.6 = (bf16[64,1024]{1,0:T(8,128)(2,1)S(1)}, bf16[64,1024]{1,0:T(8,128)(2,1)S(1)}, u32[]{:S(2)}, u32[]{:S(2)}) collective-permute-start(bf16[64,1024]{1,0:T(8,128)(2,1)S(1)} %collective-permute-done.4), channel_id=1, source_target_pairs={{0,1},{1,2},{2,3},{3,4},{4,5},{5,6},{6,7},{7,0},{8,9},{9,10},{10,1... | collective-permute-start | bytes 393224 | tf_op jit(solution)/shard_map/ppermute | solution.py:46
  34.8 2.7 %collective-permute-start.7 = (bf16[512,1024]{1,0:T(8,128)(2,1)S(1)}, bf16[512,1024]{1,0:T(8,128)(2,1)S(1)}, u32[]{:S(2)}, u32[]{:S(2)}) collective-permute-start(bf16[512,1024]{1,0:T(8,128)(2,1)S(1)} %bitcast.45), channel_id=1, source_target_pairs={{0,16},{1,17},{2,18},{3,19},{4,20},{5,21},{6,22},{7,23},{8,24},{9,... | collective-permute-start | bytes 3145736 | tf_op jit(solution)/shard_map/ppermute | solution.py:50
  37.5 1.0 copy-start
  42.8 1.2 copy-start.1
  124.1 2.9 %collective-permute-start.8 = (bf16[512,1024]{1,0:T(8,128)(2,1)}, bf16[512,1024]{1,0:T(8,128)(2,1)S(1)}, u32[]{:S(2)}, u32[]{:S(2)}) collective-permute-start(bf16[512,1024]{1,0:T(8,128)(2,1)} %get-tuple-element.21), channel_id=1, source_target_pairs={{0,16},{1,17},{2,18},{3,19},{4,20},{5,21},{6,22},{7,23},{8,24},{9,... | collective-permute-start | bytes 3145736 | tf_op jit(solution)/shard_map/ppermute | solution.py:50
  127.4 6.8 %collective-permute-start.9 = (bf16[64,1024]{1,0:T(8,128)(2,1)S(1)}, bf16[64,1024]{1,0:T(8,128)(2,1)S(1)}, u32[]{:S(2)}, u32[]{:S(2)}) collective-permute-start(bf16[64,1024]{1,0:T(8,128)(2,1)S(1)} %get-tuple-element.27), channel_id=1, source_target_pairs={{0,1},{1,2},{2,3},{3,4},{4,5},{5,6},{6,7},{7,0},{8,9},{9,10},{10,1... | collective-permute-start | bytes 393224 | tf_op jit(solution)/shard_map/ppermute | solution.py:46
  128.4 5.9 %collective-permute-start.13 = (bf16[64,1024]{1,0:T(8,128)(2,1)S(1)}, bf16[64,1024]{1,0:T(8,128)(2,1)S(1)}, u32[]{:S(2)}, u32[]{:S(2)}) collective-permute-start(bf16[64,1024]{1,0:T(8,128)(2,1)S(1)} %get-tuple-element.28), channel_id=1, source_target_pairs={{0,7},{1,0},{2,1},{3,2},{4,3},{5,4},{6,5},{7,6},{8,15},{9,8},{10,9... | collective-permute-start | bytes 393224 | tf_op jit(solution)/shard_map/ppermute | solution.py:46
  134.3 6.3 %collective-permute-start.10 = (bf16[64,1024]{1,0:T(8,128)(2,1)S(1)}, bf16[64,1024]{1,0:T(8,128)(2,1)S(1)}, u32[]{:S(2)}, u32[]{:S(2)}) collective-permute-start(bf16[64,1024]{1,0:T(8,128)(2,1)S(1)} %fusion.7), channel_id=1, source_target_pairs={{0,1},{1,2},{2,3},{3,4},{4,5},{5,6},{6,7},{7,0},{8,9},{9,10},{10,1... | collective-permute-start | bytes 393224 | tf_op jit(solution)/shard_map/ppermute | solution.py:46
  140.6 6.8 %collective-permute-start.11 = (bf16[64,1024]{1,0:T(8,128)(2,1)S(1)}, bf16[64,1024]{1,0:T(8,128)(2,1)S(1)}, u32[]{:S(2)}, u32[]{:S(2)}) collective-permute-start(bf16[64,1024]{1,0:T(8,128)(2,1)S(1)} %get-tuple-element.25), channel_id=1, source_target_pairs={{0,1},{1,2},{2,3},{3,4},{4,5},{5,6},{6,7},{7,0},{8,9},{9,10},{10,1... | collective-permute-start | bytes 393224 | tf_op jit(solution)/shard_map/ppermute | solution.py:46
  140.7 6.7 %collective-permute-start.14 = (bf16[64,1024]{1,0:T(8,128)(2,1)S(1)}, bf16[64,1024]{1,0:T(8,128)(2,1)S(1)}, u32[]{:S(2)}, u32[]{:S(2)}) collective-permute-start(bf16[64,1024]{1,0:T(8,128)(2,1)S(1)} %get-tuple-element.26), channel_id=1, source_target_pairs={{0,7},{1,0},{2,1},{3,2},{4,3},{5,4},{6,5},{7,6},{8,15},{9,8},{10,9... | collective-permute-start | bytes 393224 | tf_op jit(solution)/shard_map/ppermute | solution.py:46
  143.9 11.5 %all-to-all-start.7 = ((f32[16,8,128]{2,1,0:T(8,128)}), f32[16,8,128]{2,1,0:T(8,128)S(1)}, u32[]{:S(2)}, u32[]{:S(2)}) async-start(f32[16,8,128]{2,1,0:T(8,128)} %get-tuple-element.22), calls=%async_computation.7 | async-start | bytes 131072 | tf_op jit(solution)/shard_map/all_to_all | solution.py:54
  147.5 8.4 %collective-permute-start.12 = (bf16[64,1024]{1,0:T(8,128)(2,1)S(1)}, bf16[64,1024]{1,0:T(8,128)(2,1)S(1)}, u32[]{:S(2)}, u32[]{:S(2)}) collective-permute-start(bf16[64,1024]{1,0:T(8,128)(2,1)S(1)} %get-tuple-element.23), channel_id=1, source_target_pairs={{0,1},{1,2},{2,3},{3,4},{4,5},{5,6},{6,7},{7,0},{8,9},{9,10},{10,1... | collective-permute-start | bytes 393224 | tf_op jit(solution)/shard_map/ppermute | solution.py:46
  149.4 6.5 %collective-permute-start.15 = (bf16[64,1024]{1,0:T(8,128)(2,1)S(1)}, bf16[64,1024]{1,0:T(8,128)(2,1)S(1)}, u32[]{:S(2)}, u32[]{:S(2)}) collective-permute-start(bf16[64,1024]{1,0:T(8,128)(2,1)S(1)} %get-tuple-element.24), channel_id=1, source_target_pairs={{0,7},{1,0},{2,1},{3,2},{4,3},{5,4},{6,5},{7,6},{8,15},{9,8},{10,9... | collective-permute-start | bytes 393224 | tf_op jit(solution)/shard_map/ppermute | solution.py:46

commit v4 on v3

v4 whole, which is shorter than its diff:
```python
import functools
import math

import jax
import jax.numpy as jnp
from jax import lax
from jax.experimental import pallas as pl
from jax.experimental.pallas import tpu as pltpu
from jax.sharding import Mesh
from jax.sharding import PartitionSpec as P

WIDTH = 1024
ROWS = 1024
eps_factor = 0.3

AXES = ("x", "yh", "core", "yl", "z")
SIZES = (4, 2, 2, 2, 8)
ROW_GROUP = ("core", "z")
COL_GROUP = ("x", "yh", "yl")

EPSILON = eps_factor * math.sqrt(WIDTH)
LOG2E = math.log2(math.e)
LOG2_MASS = -math.log2(16384)


PIECE = 64
BLOCK = 2 * PIECE
TAIL = 16
FAR = PIECE + TAIL
FULL = BLOCK + TAIL


def number(place):
    index = 0
    for size, at in zip(SIZES, place):
        index = index * size + at % size
    return index


def moved(a, move):
    pairs = []
    for x in range(4):
        for y in range(4):
            for core in range(2):
                for z in range(8):
                    tx, ty, tcore, tz = move(x, y, core, z)
                    source = (x, y // 2, core, y % 2, z)
                    pairs.append((number(source), number((tx, ty // 2, tcore, ty % 2, tz))))
    return lax.ppermute(a, AXES, pairs)


def swap_core(a):
    return moved(a, lambda x, y, core, z: (x, y, 1 - core, z))


def shift_z(a):
    return moved(a, lambda x, y, core, z: (x, y, core, z + 1 - 2 * core))


def swap_x(a, flips):
    return moved(a, lambda x, y, core, z: (x ^ flips[core], y, core, z))


def swap_y(a, flips):
    return moved(a, lambda x, y, core, z: (x, y ^ flips[core], core, z))


def spread(copies, group):
    return lax.all_to_all(copies, group, 0, 0)


def gather_columns(data):
    core, x = lax.axis_index("core"), lax.axis_index("x")
    yh, yl = lax.axis_index("yh"), lax.axis_index("yl")
    x0, x1 = x % 2, x // 2
    along_x = [
        (swap_x, (1, 3), jnp.where(core == 0, x0, x1)),
        (swap_x, (3, 1), jnp.where(core == 0, x1, x0 ^ x1)),
    ]
    along_y = [
        (swap_y, (1, 3), jnp.where(core == 0, yl, yh)),
        (swap_y, (3, 1), jnp.where(core == 0, yh, yl ^ yh)),
    ]
    parts = [data[: PIECE // 2], data[PIECE // 2 :]]
    for step in range(4):
        plans = (along_x + along_y)[step], (along_y + along_x)[step]
        received = [swap(part, flips) for part, (swap, flips, _) in zip(parts, plans)]
        parts = [
            jnp.where(
                at == 0,
                jnp.concatenate([part, other], axis=0),
                jnp.concatenate([other, part], axis=0),
            )
            for part, other, (_, _, at) in zip(parts, received, plans)
        ]
    return parts


def gather_rows(noise):
    beside = swap_core(noise)
    blocks = [jnp.concatenate([noise, beside], axis=0)]
    for step in range(3):
        blocks.append(shift_z(blocks[-1]))
    far = shift_z(blocks[-1][:PIECE])
    others = swap_core(jnp.concatenate(blocks[1:] + [far], axis=0))
    return [noise, beside] + blocks[1:] + [far, others]


def to_lanes(square):
    return jnp.concatenate([square[k : k + 1, :] for k in range(8)], axis=1)


def to_square(lanes):
    return jnp.concatenate([lanes[:, 128 * k : 128 * k + 128] for k in range(8)], axis=0)


def own_first(square):
    swapped = jnp.concatenate([square[:, PIECE:], square[:, :PIECE]], axis=1)
    return jnp.where(lax.axis_index("core") == 0, square, swapped)


def lse2(parts):
    top = jnp.max(parts, axis=0)
    return top + jnp.log2(jnp.sum(jnp.exp2(parts - top[None]), axis=0))


def send(out_ref, square):
    out_ref[...] = jnp.broadcast_to(square[None], (16, 8, 128))


def terms(lanes):
    high = lanes.astype(jnp.bfloat16)
    rest = lanes - high.astype(jnp.float32)
    low = rest.astype(jnp.bfloat16)
    zeros = jnp.zeros((14, ROWS), jnp.bfloat16)
    return jnp.concatenate([high, low, zeros], axis=0)


def down(row):
    return jnp.transpose(jnp.broadcast_to(row, (128, 128)))[:, :1]


def across(column):
    return jnp.transpose(jnp.broadcast_to(column, (128, 128)))[:1, :]


def square_sums(block):
    wide = block.astype(jnp.float32)
    return jnp.sum(wide * wide, axis=1, keepdims=True)


def along_z(steps):
    return jnp.bitwise_and(lax.axis_index("z") + (1 - 2 * lax.axis_index("core")) * steps, 7)


def flipped(block):
    return jnp.concatenate([block[PIECE:], block[:PIECE]], axis=0)


def scores_kernel(
    data0, data1, own, beside, near1, near2, near3, far, others, score_ref, out_ref, lse_ref
):
    scale = LOG2E / EPSILON
    pairs = [
        (0, 4, jnp.concatenate([own[...], beside[...], far[...], others[pl.ds(3 * BLOCK, PIECE), :]], axis=0))
    ]
    for k, near in ((1, near1), (2, near2), (3, near3)):
        other = flipped(others[pl.ds((k - 1) * BLOCK, BLOCK), :])
        pairs.append((-k, k, jnp.concatenate([near[...], other], axis=0)))
    data_norms = [
        jnp.concatenate([square_sums(data[pl.ds(128 * k, 128), :]) for k in range(4)], axis=0)
        for data in (data0, data1)
    ]
    for first, second, noise in pairs:
        noise_norms = jnp.concatenate(
            [across(square_sums(noise[:BLOCK])), across(square_sums(noise[BLOCK:]))], axis=1
        )
        halves = []
        for data, norms in zip((data0, data1), data_norms):
            products = lax.dot_general(
                data[...], noise, (((1,), (1,)), ((), ())), preferred_element_type=jnp.float32
            )
            halves.append((2.0 * products - (norms + noise_norms)) * scale)
        top = jnp.maximum(
            jnp.max(halves[0], axis=0, keepdims=True), jnp.max(halves[1], axis=0, keepdims=True)
        )
        total = jnp.sum(jnp.exp2(halves[0] - top), axis=0, keepdims=True) + jnp.sum(
            jnp.exp2(halves[1] - top), axis=0, keepdims=True
        )
        row = top + jnp.log2(total)
        for side, steps in enumerate((first, second)):
            at = along_z(steps)
            lanes = slice(BLOCK * side, BLOCK * side + BLOCK)
            lse_ref[pl.ds(at, 1), :] = row[:, lanes]
            for h in range(2):
                score_ref[pl.ds(512 * h, 512), pl.ds(pl.multiple_of(at * 128, 128), 128)] = halves[h][:, lanes]
    send(out_ref, own_first(lse_ref[...]))


def columns_kernel(score_ref, in_ref, dual_ref, out_ref):
    dual = own_first(LOG2_MASS - lse2(in_ref[...]))
    dual_ref[...] = dual
    along = to_lanes(dual)
    rows = []
    for k in range(8):
        shifted = score_ref[pl.ds(128 * k, 128), :] + along
        top = jnp.max(shifted, axis=1, keepdims=True)
        total = jnp.sum(jnp.exp2(shifted - top), axis=1, keepdims=True)
        rows.append(across(top + jnp.log2(total)))
    send(out_ref, jnp.concatenate(rows, axis=0))


def plan_kernel(score_ref, dual_ref, in_ref, plan_ref, out_ref):
    along = to_lanes(dual_ref[...])
    dual = LOG2_MASS - lse2(in_ref[...])
    sums = jnp.zeros((1, ROWS), jnp.float32)
    for k in range(8):
        part = pl.ds(128 * k, 128)
        lifted = down(dual[k : k + 1, :] - LOG2_MASS)
        plan = jnp.exp2(score_ref[part, :] + along + lifted)
        plan_ref[part, :] = plan.astype(jnp.bfloat16)
        sums = sums + jnp.sum(plan, axis=0, keepdims=True)
    send(out_ref, own_first(to_square(sums)))


def column_sums_kernel(plan_ref, in_ref, out_ref):
    scale = own_first(1.0 / jnp.sum(in_ref[...], axis=0))
    sums = lax.dot_general(
        terms(to_lanes(scale)),
        plan_ref[...],
        (((1,), (1,)), ((), ())),
        preferred_element_type=jnp.float32,
    )
    send(out_ref, to_square(sums[0:1, :] + sums[1:2, :]))


def row_sums_kernel(plan_ref, in_ref, out_ref):
    scale = 1.0 / jnp.sum(in_ref[...], axis=0)
    sums = jnp.dot(terms(to_lanes(scale)), plan_ref[...], preferred_element_type=jnp.float32)
    send(out_ref, own_first(to_square(sums[0:1, :] + sums[1:2, :])))


def packed(total):
    high = total.astype(jnp.bfloat16)
    low = (total - high.astype(jnp.float32)).astype(jnp.bfloat16)
    zeros = jnp.zeros((TAIL - 2, 128), jnp.bfloat16)
    narrow = jnp.concatenate([high, low, zeros], axis=0)
    return jnp.concatenate([narrow, jnp.zeros((TAIL, WIDTH - 128), jnp.bfloat16)], axis=1)


def unpacked(tail):
    return tail[0:1, :128].astype(jnp.float32) + tail[1:2, :128].astype(jnp.float32)


def halves_turned(total):
    return jnp.concatenate([total[:, PIECE:], total[:, :PIECE]], axis=1)


def targets_kernel(plan_ref, in_ref, data0, data1, mine_ref, give_ref, weight_ref, sum_ref):
    scale = 1.0 / jnp.sum(in_ref[...], axis=0)
    sums = jnp.zeros((1, ROWS), jnp.float32)
    for k in range(8):
        part = pl.ds(128 * k, 128)
        weights = plan_ref[part, :].astype(jnp.float32) * down(scale[k : k + 1, :])
        weight_ref[part, :] = weights.astype(jnp.bfloat16)
        sums = sums + jnp.sum(weights, axis=0, keepdims=True)
    sum_ref[...] = to_square(sums)

    def partial(first, second):
        at = [along_z(first), along_z(second)]
        weights = jnp.concatenate(
            [weight_ref[:, pl.ds(pl.multiple_of(k * 128, 128), 128)] for k in at], axis=1
        )
        out = 0.0
        for h, data in enumerate((data0, data1)):
            out = out + lax.dot_general(
                weights[512 * h : 512 * h + 512],
                data[...],
                (((0,), (0,)), ((), ())),
                preferred_element_type=jnp.float32,
            )
        return out.astype(jnp.bfloat16), [sum_ref[pl.ds(k, 1), :] for k in at]

    for k in (1, 2, 3):
        out, (mine, give) = partial(k, -k)
        start = (k - 1) * FULL
        mine_ref[pl.ds(start, BLOCK), :] = out[:BLOCK]
        mine_ref[pl.ds(start + BLOCK, TAIL), :] = packed(mine)
        give_ref[pl.ds(start, BLOCK), :] = flipped(out[BLOCK:])
        give_ref[pl.ds(start + BLOCK, TAIL), :] = packed(halves_turned(give))
    out, totals = partial(4, 0)
    for side in range(2):
        start = 3 * FULL + side * FAR
        rows = out[side * BLOCK : side * BLOCK + BLOCK]
        mine_ref[pl.ds(start, PIECE), :] = rows[:PIECE]
        mine_ref[pl.ds(start + PIECE, TAIL), :] = packed(totals[side])
        give_ref[pl.ds(start, PIECE), :] = rows[PIECE:]
        give_ref[pl.ds(start + PIECE, TAIL), :] = packed(halves_turned(totals[side]))


def summed(a, b, rows):
    body = a[:rows].astype(jnp.float32) + b[:rows].astype(jnp.float32)
    tail = packed(unpacked(a[rows:]) + unpacked(b[rows:]))
    return jnp.concatenate([body.astype(jnp.bfloat16), tail], axis=0)


def cores_kernel(mine_ref, got_ref, b1_ref, b2_ref, b3_ref, far_ref, home_ref):
    for k, out in enumerate((b1_ref, b2_ref, b3_ref)):
        part = pl.ds(k * FULL, FULL)
        out[...] = summed(mine_ref[part, :], got_ref[part, :], BLOCK)
    for k, out in enumerate((far_ref, home_ref)):
        part = pl.ds(3 * FULL + k * FAR, FAR)
        out[...] = summed(mine_ref[part, :], got_ref[part, :], PIECE)


def far_kernel(block_ref, far_ref, out_ref):
    block, far = block_ref[...], far_ref[...]
    out_ref[pl.ds(0, PIECE), :] = (
        block[:PIECE].astype(jnp.float32) + far[:PIECE].astype(jnp.float32)
    ).astype(jnp.bfloat16)
    out_ref[pl.ds(PIECE, PIECE), :] = block[PIECE:BLOCK]
    first = lax.broadcasted_iota(jnp.int32, (1, 128), 1) < PIECE
    more = jnp.where(first, unpacked(far[PIECE:]), 0.0)
    out_ref[pl.ds(BLOCK, TAIL), :] = packed(unpacked(block[BLOCK:]) + more)


def block_kernel(block_ref, more_ref, out_ref):
    out_ref[...] = summed(block_ref[...], more_ref[...], BLOCK)


def velocity_kernel(last_ref, home_ref, other_ref, noise_ref, out_ref):
    last, home, other = last_ref[...], home_ref[...], other_ref[...]
    body = last[:PIECE].astype(jnp.float32) + home[:PIECE].astype(jnp.float32)
    body = body + other[:PIECE].astype(jnp.float32)
    total = unpacked(last[BLOCK:]) + unpacked(home[PIECE:]) + halves_turned(unpacked(other[PIECE:]))
    target = body / down(total)[:PIECE]
    out_ref[...] = (target - noise_ref[...].astype(jnp.float32)).astype(jnp.bfloat16)


SQUARE = jax.ShapeDtypeStruct((8, 128), jnp.float32)
COPIES = jax.ShapeDtypeStruct((16, 8, 128), jnp.float32)


def in_vmem(rows, dtype):
    return pltpu.VMEM((rows, 1024), dtype)


def run(kernel, outs, *args, flops=0, scratch=()):
    return pl.pallas_call(
        kernel,
        out_shape=outs,
        in_specs=[pl.BlockSpec(memory_space=pltpu.VMEM)] * len(args),
        out_specs=jax.tree.map(lambda _: pl.BlockSpec(memory_space=pltpu.VMEM), outs),
        scratch_shapes=scratch,
        compiler_params=pltpu.CompilerParams(vmem_limit_bytes=40 * 1024 * 1024),
        cost_estimate=pl.CostEstimate(flops=flops, bytes_accessed=4 << 20, transcendentals=0),
    )(*args)


def keep(a):
    return pltpu.with_memory_space_constraint(a, pltpu.VMEM)


def rows_of(count):
    return jax.ShapeDtypeStruct((count, WIDTH), jnp.bfloat16)


def per_device(noise_latents, data_latents):
    columns = gather_columns(data_latents)
    rows = gather_rows(noise_latents)

    scores, parts = run(
        scores_kernel,
        (in_vmem(ROWS, jnp.float32), COPIES),
        *columns,
        *rows,
        scratch=[pltpu.VMEM((8, 128), jnp.float32)],
    )
    scores = keep(scores)
    row_dual, parts = run(columns_kernel, (SQUARE, COPIES), scores, spread(parts, ROW_GROUP))
    plan, parts = run(
        plan_kernel,
        (in_vmem(ROWS, jnp.bfloat16), COPIES),
        scores,
        row_dual,
        spread(parts, COL_GROUP),
    )
    plan = keep(plan)
    parts = run(column_sums_kernel, COPIES, plan, spread(parts, ROW_GROUP))
    parts = run(row_sums_kernel, COPIES, plan, spread(parts, COL_GROUP))
    parts = run(column_sums_kernel, COPIES, plan, spread(parts, ROW_GROUP))
    count = 3 * FULL + 2 * FAR
    mine, give = run(
        targets_kernel,
        (rows_of(count), rows_of(count)),
        plan,
        spread(parts, COL_GROUP),
        *columns,
        scratch=[pltpu.VMEM((ROWS, ROWS), jnp.bfloat16), pltpu.VMEM((8, 128), jnp.float32)],
    )
    b1, b2, b3, far, home = run(
        cores_kernel,
        (rows_of(FULL), rows_of(FULL), rows_of(FULL), rows_of(FAR), rows_of(FAR)),
        mine,
        swap_core(give),
    )
    moving = run(far_kernel, rows_of(FULL), b3, shift_z(far))
    moving = run(block_kernel, rows_of(FULL), b2, shift_z(moving))
    moving = run(block_kernel, rows_of(FULL), b1, shift_z(moving))
    last = shift_z(moving)
    other = swap_core(last[PIECE:])
    return run(velocity_kernel, rows_of(PIECE), last, home, other, noise_latents)


def solution(mesh):
    fine = Mesh(mesh.devices.reshape(SIZES), AXES)
    rows = P(AXES, None)
    return jax.shard_map(
        per_device, mesh=fine, in_specs=(rows, rows), out_specs=rows, check_vma=False
    )
```

time: 159 us -> 171 us (1.075)
  waiting for transfers between devices: 36.4 us -> 61.7 us
  starting transfers between devices: 33.6 us -> 18.1 us
  local copies, waits for them, and re-layouts: 5.05 us -> 0.91 us
  blocking collectives: 68.9 us -> 72.5 us
    ppermute x16 -> x20, waiting for transfers between devices: 27.5 us -> 61.7 us  [moved(): return lax.ppermute(a, AXES, pairs)]
    all_to_all x2 -> x0, starting transfers between devices: 11.1 us -> none  [spread(): return lax.all_to_all(copies, group, 0, 0)]
    all_to_all x2 -> x0, waiting for transfers between devices: 8.88 us -> none  [spread(): return lax.all_to_all(copies, group, 0, 0)]
    ppermute x16 -> x20, starting transfers between devices: 22.5 us -> 18.1 us  [moved(): return lax.ppermute(a, AXES, pairs)]
    all_to_all x6, blocking collectives: 68.9 us -> 72.5 us  [spread(): return lax.all_to_all(copies, group, 0, 0)]
    broadcast_in_dim x2 -> x0, local copies, waits for them, and re-layouts: 2.61 us -> none  [the longest x1 2.5 us: per_device(): jnp.broadcast_to(data_latents[None], (16,) + data_latents.shape)]
    unnamed x6 -> x2, local copies, waits for them, and re-layouts: 2.22 us -> 0.01 us
    pallas_call x7 -> x12, Pallas kernels: 11.1 us -> 12.3 us  [run(): pl.pallas_call(kernel, out_shape=outs, in_specs=[pl.BlockSpec(memory_spac...]
  transfers between devices with their start and end apart: 18 -> 20, of which waited for: 10 -> 16; matrix products, arithmetic and copies ran while one was open for 2% -> 1% of each run, Pallas kernels for 0% -> 0%
where the time goes in v4:
time: 171 us; the launch traced here: 168 us
  blocking collectives  72.5 us (42%)
  waiting for transfers between devices  61.7 us (36%)
  starting transfers between devices  18.1 us (11%)
  Pallas kernels  12.3 us (7%)
  other arithmetic  2.33 us (1%)
    all_to_all x6, blocking collectives, spread(): return lax.all_to_all(copies, group, 0, 0)  72.5 us
    ppermute x20, waiting for transfers between devices, moved(): return lax.ppermute(a, AXES, pairs)  61.7 us
    ppermute x20, starting transfers between devices, moved(): return lax.ppermute(a, AXES, pairs)  18.1 us
    pallas_call x12, Pallas kernels, run(): pl.pallas_call(kernel, out_shape=outs, in_specs=[pl.BlockSpec(memory_spac...  12.3 us
  transfers between devices with their start and end apart: 20, of which 16 were waited for; matrix products, arithmetic and copies ran while one was open for 1% of the time, Pallas kernels for 0%

profile of v4, /device:TPU:2, one launch (start us, length us, event | category | flops | bytes accessed | tf_op | source)
XLA Modules:
  0.0 168.1 jit_solution(7368020718958518559)
XLA Ops:
  2.5 2.0 %collective-permute-start.9 = (bf16[128,1024]{1,0:T(8,128)(2,1)S(1)}, bf16[128,1024]{1,0:T(8,128)(2,1)S(1)}, u32[]{:S(2)}, u32[]{:S(2)}) collective-permute-start(bf16[128,1024]{1,0:T(8,128)(2,1)S(1)} %pad_maximum_fusion.1), channel_id=1, source_target_pairs={{0,1},{1,2},{2,3},{3,4},{4,5},{5,6},{6,7},{7,0},{16,23},{17,16},{1... | collective-permute-start | bytes 786440 | tf_op jit(solution)/shard_map/ppermute | solution.py:49
  4.5 8.3 %collective-permute-done.9.near1 = bf16[128,1024]{1,0:T(8,128)(2,1)S(1)} collective-permute-done((bf16[128,1024]{1,0:T(8,128)(2,1)S(1)}, bf16[128,1024]{1,0:T(8,128)(2,1)S(1)}, u32[]{:S(2)}, u32[]{:S(2)}) %collective-permute-start.9) | collective-permute-done | bytes 262176 | tf_op jit(solution)/shard_map/ppermute | solution.py:49
  14.3 6.1 %collective-permute-done.10.near2 = bf16[128,1024]{1,0:T(8,128)(2,1)S(1)} collective-permute-done((bf16[128,1024]{1,0:T(8,128)(2,1)S(1)}, bf16[128,1024]{1,0:T(8,128)(2,1)S(1)}, u32[]{:S(2)}, u32[]{:S(2)}) %collective-permute-start.10) | collective-permute-done | bytes 262176 | tf_op jit(solution)/shard_map/ppermute | solution.py:49
  22.0 1.6 collective-permute-start.1
  24.7 3.1 %collective-permute-start.5 = (bf16[64,1024]{1,0:T(8,128)(2,1)S(1)}, bf16[64,1024]{1,0:T(8,128)(2,1)S(1)}, u32[]{:S(2)}, u32[]{:S(2)}) collective-permute-start(bf16[64,1024]{1,0:T(8,128)(2,1)S(1)} %maximum_select_fusion.7), channel_id=1, source_target_pairs={{0,40},{1,41},{2,42},{3,43},{4,44},{5,45},{6,46},{7,47},{16,24},{1... | collective-permute-start | bytes 393224 | tf_op jit(solution)/shard_map/ppermute | solution.py:49
  28.1 1.7 collective-permute-start.2
  31.8 2.4 %collective-permute-done.12.far = bf16[64,1024]{1,0:T(8,128)(2,1)S(1)} collective-permute-done((bf16[64,1024]{1,0:T(8,128)(2,1)S(1)}, bf16[64,1024]{1,0:T(8,128)(2,1)S(1)}, u32[]{:S(2)}, u32[]{:S(2)}) %collective-permute-start.12) | collective-permute-done | bytes 131104 | tf_op jit(solution)/shard_map/ppermute | solution.py:49
  34.7 3.1 %collective-permute-start.3 = (bf16[256,1024]{1,0:T(8,128)(2,1)S(1)}, bf16[256,1024]{1,0:T(8,128)(2,1)S(1)}, u32[]{:S(2)}, u32[]{:S(2)}) collective-permute-start(bf16[256,1024]{1,0:T(8,128)(2,1)S(1)} %maximum_select_fusion.2), channel_id=1, source_target_pairs={{0,40},{1,41},{2,42},{3,43},{4,44},{5,45},{6,46},{7,47},{16,24},{1... | collective-permute-start | bytes 1572872 | tf_op jit(solution)/shard_map/ppermute | solution.py:49
  38.0 1.8 %collective-permute-start.7 = (bf16[256,1024]{1,0:T(8,128)(2,1)S(1)}, bf16[256,1024]{1,0:T(8,128)(2,1)S(1)}, u32[]{:S(2)}, u32[]{:S(2)}) collective-permute-start(bf16[256,1024]{1,0:T(8,128)(2,1)S(1)} %maximum_select_fusion.3), channel_id=1, source_target_pairs={{0,192},{1,193},{2,194},{3,195},{4,196},{5,197},{6,198},{7,199},{1... | collective-permute-start | bytes 1572872 | tf_op jit(solution)/shard_map/ppermute | solution.py:49
  39.7 5.5 %collective-permute-done.3 = bf16[256,1024]{1,0:T(8,128)(2,1)S(1)} collective-permute-done((bf16[256,1024]{1,0:T(8,128)(2,1)S(1)}, bf16[256,1024]{1,0:T(8,128)(2,1)S(1)}, u32[]{:S(2)}, u32[]{:S(2)}) %collective-permute-start.3) | collective-permute-done | bytes 524320 | tf_op jit(solution)/shard_map/ppermute | solution.py:49
  45.7 1.7 %collective-permute-done.7 = bf16[256,1024]{1,0:T(8,128)(2,1)S(1)} collective-permute-done((bf16[256,1024]{1,0:T(8,128)(2,1)S(1)}, bf16[256,1024]{1,0:T(8,128)(2,1)S(1)}, u32[]{:S(2)}, u32[]{:S(2)}) %collective-permute-start.7) | collective-permute-done | bytes 524320 | tf_op jit(solution)/shard_map/ppermute | solution.py:49
  47.9 3.8 %shard_map.28 = (f32[1024,1024]{1,0:T(8,128)S(1)}, f32[16,8,128]{2,1,0:T(8,128)S(1)}) custom-call(bf16[512,1024]{1,0:T(8,128)(2,1)S(1)} %maximum_select_fusion.data0, bf16[512,1024]{1,0:T(8,128)(2,1)S(1)} %maximum_select_fusion.1.data1, bf16[64,1024]{1,0:T(8,128)(2,1)S(1)} %copy-done, bf16[64,1024]{1,0:T(8,128)(2,1)S(1)} %collective-permute-done.8.beside, ...), custom_call_target="tpu_custom_call" | custom-call | bytes 4194304 | tf_op jit(solution)/shard_map/pallas_call | solution.py:349
  51.7 14.7 %all_to_all.30.in_ref = f32[16,8,128]{2,1,0:T(8,128)S(1)} all-to-all(f32[16,8,128]{2,1,0:T(8,128)S(1)} %get-tuple-element.19), channel_id=1, replica_groups=mesh['x'=4,'yh'=2,'core'=2,'yl'=2,'z'=8] {'core','z'}, dimensions={0} | all-to-all | bytes 131072 | tf_op jit(solution)/shard_map/all_to_all | solution.py:69
  67.6 15.1 %all_to_all.31.in_ref = f32[16,8,128]{2,1,0:T(8,128)S(1)} all-to-all(f32[16,8,128]{2,1,0:T(8,128)S(1)} %get-tuple-element.21), channel_id=1, replica_groups=mesh['x'=4,'yh'=2,'core'=2,'yl'=2,'z'=8] {'x','yh','yl'}, dimensions={0} | all-to-all | bytes 131072 | tf_op jit(solution)/shard_map/all_to_all | solution.py:69
  83.6 10.5 %all_to_all.32.in_ref = f32[16,8,128]{2,1,0:T(8,128)S(1)} all-to-all(f32[16,8,128]{2,1,0:T(8,128)S(1)} %get-tuple-element.23), channel_id=1, replica_groups=mesh['x'=4,'yh'=2,'core'=2,'yl'=2,'z'=8] {'core','z'}, dimensions={0} | all-to-all | bytes 131072 | tf_op jit(solution)/shard_map/all_to_all | solution.py:69
  94.8 10.9 %all_to_all.33.in_ref = f32[16,8,128]{2,1,0:T(8,128)S(1)} all-to-all(f32[16,8,128]{2,1,0:T(8,128)S(1)} %shard_map.31), channel_id=1, replica_groups=mesh['x'=4,'yh'=2,'core'=2,'yl'=2,'z'=8] {'x','yh','yl'}, dimensions={0} | all-to-all | bytes 131072 | tf_op jit(solution)/shard_map/all_to_all | solution.py:69
  106.2 10.5 %all_to_all.34.in_ref = f32[16,8,128]{2,1,0:T(8,128)S(1)} all-to-all(f32[16,8,128]{2,1,0:T(8,128)S(1)} %shard_map.32), channel_id=1, replica_groups=mesh['x'=4,'yh'=2,'core'=2,'yl'=2,'z'=8] {'core','z'}, dimensions={0} | all-to-all | bytes 131072 | tf_op jit(solution)/shard_map/all_to_all | solution.py:69
  117.4 10.9 %all_to_all.35.in_ref = f32[16,8,128]{2,1,0:T(8,128)S(1)} all-to-all(f32[16,8,128]{2,1,0:T(8,128)S(1)} %shard_map.33), channel_id=1, replica_groups=mesh['x'=4,'yh'=2,'core'=2,'yl'=2,'z'=8] {'x','yh','yl'}, dimensions={0} | all-to-all | bytes 131072 | tf_op jit(solution)/shard_map/all_to_all | solution.py:69
  128.2 3.2 %shard_map.34 = (bf16[592,1024]{1,0:T(8,128)(2,1)S(1)}, bf16[592,1024]{1,0:T(8,128)(2,1)S(1)}) custom-call(bf16[1024,1024]{1,0:T(8,128)(2,1)S(1)} %get-tuple-element.22.plan_ref, f32[16,8,128]{2,1,0:T(8,128)S(1)} %all_to_all.35.in_ref, bf16[512,1024]{1,0:T(8,128)(2,1)S(1)} %maximum_select_fusion.data0, bf16[512,1024]{1,0:T(8,128)(2,1)S(1)} %maximum_select_fusion.1.data1), custom_call_target="tpu_custom_call" | custom-call | bytes 4194304 | tf_op jit(solution)/shard_map/pallas_call | solution.py:349
  131.8 2.9 %collective-permute-done.14.got_ref = bf16[592,1024]{1,0:T(8,128)(2,1)S(1)} collective-permute-done((bf16[592,1024]{1,0:T(8,128)(2,1)S(1)}, bf16[592,1024]{1,0:T(8,128)(2,1)S(1)}, u32[]{:S(2)}, u32[]{:S(2)}) %collective-permute-start.14) | collective-permute-done | bytes 1212448 | tf_op jit(solution)/shard_map/ppermute | solution.py:49
  135.9 5.6 %collective-permute-done.15.far_ref = bf16[80,1024]{1,0:T(8,128)(2,1)S(1)} collective-permute-done((bf16[80,1024]{1,0:T(8,128)(2,1)S(1)}, bf16[80,1024]{1,0:T(8,128)(2,1)S(1)}, u32[]{:S(2)}, u32[]{:S(2)}) %collective-permute-start.15) | collective-permute-done | bytes 163872 | tf_op jit(solution)/shard_map/ppermute | solution.py:49
  141.6 7.9 %collective-permute-done.16.more_ref = bf16[144,1024]{1,0:T(8,128)(2,1)S(1)} collective-permute-done((bf16[144,1024]{1,0:T(8,128)(2,1)S(1)}, bf16[144,1024]{1,0:T(8,128)(2,1)S(1)}, u32[]{:S(2)}, u32[]{:S(2)}) %collective-permute-start.16) | collective-permute-done | bytes 294944 | tf_op jit(solution)/shard_map/ppermute | solution.py:49
  149.7 7.9 %collective-permute-done.17.more_ref = bf16[144,1024]{1,0:T(8,128)(2,1)S(1)} collective-permute-done((bf16[144,1024]{1,0:T(8,128)(2,1)S(1)}, bf16[144,1024]{1,0:T(8,128)(2,1)S(1)}, u32[]{:S(2)}, u32[]{:S(2)}) %collective-permute-start.17) | collective-permute-done | bytes 294944 | tf_op jit(solution)/shard_map/ppermute | solution.py:49
  157.8 7.9 %collective-permute-done.18.last_ref = bf16[144,1024]{1,0:T(8,128)(2,1)S(1)} collective-permute-done((bf16[144,1024]{1,0:T(8,128)(2,1)S(1)}, bf16[144,1024]{1,0:T(8,128)(2,1)S(1)}, u32[]{:S(2)}, u32[]{:S(2)}) %collective-permute-start.18) | collective-permute-done | bytes 294944 | tf_op jit(solution)/shard_map/ppermute | solution.py:49
  (49 shorter events, 19.0 us)
Async XLA Ops:
  0.0 1.6 collective-permute-start.8
  2.5 10.3 %collective-permute-start.9 = (bf16[128,1024]{1,0:T(8,128)(2,1)S(1)}, bf16[128,1024]{1,0:T(8,128)(2,1)S(1)}, u32[]{:S(2)}, u32[]{:S(2)}) collective-permute-start(bf16[128,1024]{1,0:T(8,128)(2,1)S(1)} %pad_maximum_fusion.1), channel_id=1, source_target_pairs={{0,1},{1,2},{2,3},{3,4},{4,5},{5,6},{6,7},{7,0},{16,23},{17,16},{1... | collective-permute-start | bytes 786440 | tf_op jit(solution)/shard_map/ppermute | solution.py:49
  12.8 7.6 %collective-permute-start.10 = (bf16[128,1024]{1,0:T(8,128)(2,1)S(1)}, bf16[128,1024]{1,0:T(8,128)(2,1)S(1)}, u32[]{:S(2)}, u32[]{:S(2)}) collective-permute-start(bf16[128,1024]{1,0:T(8,128)(2,1)S(1)} %collective-permute-done.9.near1), channel_id=1, source_target_pairs={{0,1},{1,2},{2,3},{3,4},{4,5},{5,6},{6,7},{7,0},{16,23},{17,16},{1... | collective-permute-start | bytes 786440 | tf_op jit(solution)/shard_map/ppermute | solution.py:49
  13.7 8.3 %collective-permute-start = (bf16[32,1024]{1,0:T(8,128)(2,1)S(1)}, bf16[32,1024]{1,0:T(8,128)(2,1)S(1)}, u32[]{:S(2)}, u32[]{:S(2)}) collective-permute-start(bf16[32,1024]{1,0:T(8,128)(2,1)S(1)} %get-tuple-element.32), channel_id=1, source_target_pairs={{0,64},{1,65},{2,66},{3,67},{4,68},{5,69},{6,70},{7,71},{16,208},{... | collective-permute-start | bytes 196616 | tf_op jit(solution)/shard_map/ppermute | solution.py:49
  20.4 7.6 %collective-permute-start.11 = (bf16[128,1024]{1,0:T(8,128)(2,1)S(1)}, bf16[128,1024]{1,0:T(8,128)(2,1)S(1)}, u32[]{:S(2)}, u32[]{:S(2)}) collective-permute-start(bf16[128,1024]{1,0:T(8,128)(2,1)S(1)} %collective-permute-done.10.near2), channel_id=1, source_target_pairs={{0,1},{1,2},{2,3},{3,4},{4,5},{5,6},{6,7},{7,0},{16,23},{17,16},{1... | collective-permute-start | bytes 786440 | tf_op jit(solution)/shard_map/ppermute | solution.py:49
  20.4 4.3 %collective-permute-start.4 = (bf16[32,1024]{1,0:T(8,128)(2,1)S(1)}, bf16[32,1024]{1,0:T(8,128)(2,1)S(1)}, u32[]{:S(2)}, u32[]{:S(2)}) collective-permute-start(bf16[32,1024]{1,0:T(8,128)(2,1)S(1)} %get-tuple-element.31), channel_id=1, source_target_pairs={{0,8},{1,9},{2,10},{3,11},{4,12},{5,13},{6,14},{7,15},{16,56},{17,... | collective-permute-start | bytes 196616 | tf_op jit(solution)/shard_map/ppermute | solution.py:49
  22.0 6.1 %collective-permute-start.1 = (bf16[64,1024]{1,0:T(8,128)(2,1)S(1)}, bf16[64,1024]{1,0:T(8,128)(2,1)S(1)}, u32[]{:S(2)}, u32[]{:S(2)}) collective-permute-start(bf16[64,1024]{1,0:T(8,128)(2,1)S(1)} %maximum_select_fusion.6), channel_id=1, source_target_pairs={{0,192},{1,193},{2,194},{3,195},{4,196},{5,197},{6,198},{7,199},{1... | collective-permute-start | bytes 393224 | tf_op jit(solution)/shard_map/ppermute | solution.py:49
  24.7 6.3 %collective-permute-start.5 = (bf16[64,1024]{1,0:T(8,128)(2,1)S(1)}, bf16[64,1024]{1,0:T(8,128)(2,1)S(1)}, u32[]{:S(2)}, u32[]{:S(2)}) collective-permute-start(bf16[64,1024]{1,0:T(8,128)(2,1)S(1)} %maximum_select_fusion.7), channel_id=1, source_target_pairs={{0,40},{1,41},{2,42},{3,43},{4,44},{5,45},{6,46},{7,47},{16,24},{1... | collective-permute-start | bytes 393224 | tf_op jit(solution)/shard_map/ppermute | solution.py:49
  27.9 6.3 %collective-permute-start.12 = (bf16[64,1024]{1,0:T(8,128)(2,1)S(1)}, bf16[64,1024]{1,0:T(8,128)(2,1)S(1)}, u32[]{:S(2)}, u32[]{:S(2)}) collective-permute-start(bf16[64,1024]{1,0:T(8,128)(2,1)S(1)} %slice.16), channel_id=1, source_target_pairs={{0,1},{1,2},{2,3},{3,4},{4,5},{5,6},{6,7},{7,0},{16,23},{17,16},{1... | collective-permute-start | bytes 393224 | tf_op jit(solution)/shard_map/ppermute | solution.py:49
  28.1 6.5 %collective-permute-start.2 = (bf16[128,1024]{1,0:T(8,128)(2,1)S(1)}, bf16[128,1024]{1,0:T(8,128)(2,1)S(1)}, u32[]{:S(2)}, u32[]{:S(2)}) collective-permute-start(bf16[128,1024]{1,0:T(8,128)(2,1)S(1)} %maximum_select_fusion.4), channel_id=1, source_target_pairs={{0,8},{1,9},{2,10},{3,11},{4,12},{5,13},{6,14},{7,15},{16,56},{17,... | collective-permute-start | bytes 786440 | tf_op jit(solution)/shard_map/ppermute | solution.py:49
  31.0 6.8 %collective-permute-start.6 = (bf16[128,1024]{1,0:T(8,128)(2,1)S(1)}, bf16[128,1024]{1,0:T(8,128)(2,1)S(1)}, u32[]{:S(2)}, u32[]{:S(2)}) collective-permute-start(bf16[128,1024]{1,0:T(8,128)(2,1)S(1)} %maximum_select_fusion.5), channel_id=1, source_target_pairs={{0,64},{1,65},{2,66},{3,67},{4,68},{5,69},{6,70},{7,71},{16,208},{... | collective-permute-start | bytes 786440 | tf_op jit(solution)/shard_map/ppermute | solution.py:49
  34.3 13.6 %collective-permute-start.13 = (bf16[448,1024]{1,0:T(8,128)(2,1)S(1)}, bf16[448,1024]{1,0:T(8,128)(2,1)S(1)}, u32[]{:S(2)}, u32[]{:S(2)}) collective-permute-start(bf16[448,1024]{1,0:T(8,128)(2,1)S(1)} %pad_maximum_fusion), channel_id=1, source_target_pairs={{0,16},{1,17},{2,18},{3,19},{4,20},{5,21},{6,22},{7,23},{16,0},{17... | collective-permute-start | bytes 2752520 | tf_op jit(solution)/shard_map/ppermute | solution.py:49
  34.7 10.5 %collective-permute-start.3 = (bf16[256,1024]{1,0:T(8,128)(2,1)S(1)}, bf16[256,1024]{1,0:T(8,128)(2,1)S(1)}, u32[]{:S(2)}, u32[]{:S(2)}) collective-permute-start(bf16[256,1024]{1,0:T(8,128)(2,1)S(1)} %maximum_select_fusion.2), channel_id=1, source_target_pairs={{0,40},{1,41},{2,42},{3,43},{4,44},{5,45},{6,46},{7,47},{16,24},{1... | collective-permute-start | bytes 1572872 | tf_op jit(solution)/shard_map/ppermute | solution.py:49
  37.9 10.0 %copy-start = (bf16[64,1024]{1,0:T(8,128)(2,1)S(1)}, bf16[64,1024]{1,0:T(8,128)(2,1)}, u32[]{:S(2)}) copy-start(bf16[64,1024]{1,0:T(8,128)(2,1)} %noise_ref.1) | copy-start | bytes 393220
  38.0 9.4 %collective-permute-start.7 = (bf16[256,1024]{1,0:T(8,128)(2,1)S(1)}, bf16[256,1024]{1,0:T(8,128)(2,1)S(1)}, u32[]{:S(2)}, u32[]{:S(2)}) collective-permute-start(bf16[256,1024]{1,0:T(8,128)(2,1)S(1)} %maximum_select_fusion.3), channel_id=1, source_target_pairs={{0,192},{1,193},{2,194},{3,195},{4,196},{5,197},{6,198},{7,199},{1... | collective-permute-start | bytes 1572872 | tf_op jit(solution)/shard_map/ppermute | solution.py:49
  131.4 3.2 %collective-permute-start.14 = (bf16[592,1024]{1,0:T(8,128)(2,1)S(1)}, bf16[592,1024]{1,0:T(8,128)(2,1)S(1)}, u32[]{:S(2)}, u32[]{:S(2)}) collective-permute-start(bf16[592,1024]{1,0:T(8,128)(2,1)S(1)} %get-tuple-element.25), channel_id=1, source_target_pairs={{0,16},{1,17},{2,18},{3,19},{4,20},{5,21},{6,22},{7,23},{16,0},{17... | collective-permute-start | bytes 3637256 | tf_op jit(solution)/shard_map/ppermute | solution.py:49
  134.9 6.6 %collective-permute-start.15 = (bf16[80,1024]{1,0:T(8,128)(2,1)S(1)}, bf16[80,1024]{1,0:T(8,128)(2,1)S(1)}, u32[]{:S(2)}, u32[]{:S(2)}) collective-permute-start(bf16[80,1024]{1,0:T(8,128)(2,1)S(1)} %get-tuple-element.29), channel_id=1, source_target_pairs={{0,1},{1,2},{2,3},{3,4},{4,5},{5,6},{6,7},{7,0},{16,23},{17,16},{1... | collective-permute-start | bytes 491528 | tf_op jit(solution)/shard_map/ppermute | solution.py:49
  141.5 8.0 %collective-permute-start.16 = (bf16[144,1024]{1,0:T(8,128)(2,1)S(1)}, bf16[144,1024]{1,0:T(8,128)(2,1)S(1)}, u32[]{:S(2)}, u32[]{:S(2)}) collective-permute-start(bf16[144,1024]{1,0:T(8,128)(2,1)S(1)} %shard_map.36), channel_id=1, source_target_pairs={{0,1},{1,2},{2,3},{3,4},{4,5},{5,6},{6,7},{7,0},{16,23},{17,16},{1... | collective-permute-start | bytes 884744 | tf_op jit(solution)/shard_map/ppermute | solution.py:49
  149.6 8.0 %collective-permute-start.17 = (bf16[144,1024]{1,0:T(8,128)(2,1)S(1)}, bf16[144,1024]{1,0:T(8,128)(2,1)S(1)}, u32[]{:S(2)}, u32[]{:S(2)}) collective-permute-start(bf16[144,1024]{1,0:T(8,128)(2,1)S(1)} %shard_map.37), channel_id=1, source_target_pairs={{0,1},{1,2},{2,3},{3,4},{4,5},{5,6},{6,7},{7,0},{16,23},{17,16},{1... | collective-permute-start | bytes 884744 | tf_op jit(solution)/shard_map/ppermute | solution.py:49
  157.7 8.0 %collective-permute-start.18 = (bf16[144,1024]{1,0:T(8,128)(2,1)S(1)}, bf16[144,1024]{1,0:T(8,128)(2,1)S(1)}, u32[]{:S(2)}, u32[]{:S(2)}) collective-permute-start(bf16[144,1024]{1,0:T(8,128)(2,1)S(1)} %shard_map.38), channel_id=1, source_target_pairs={{0,1},{1,2},{2,3},{3,4},{4,5},{5,6},{6,7},{7,0},{16,23},{17,16},{1... | collective-permute-start | bytes 884744 | tf_op jit(solution)/shard_map/ppermute | solution.py:49
  165.7 1.5 collective-permute-start.19

commit v5 on v4

v5 whole, which is shorter than its diff:
```python
import functools
import math

import jax
import jax.numpy as jnp
from jax import lax
from jax.experimental import pallas as pl
from jax.experimental.pallas import tpu as pltpu
from jax.sharding import Mesh
from jax.sharding import PartitionSpec as P

WIDTH = 1024
ROWS = 1024
eps_factor = 0.3

AXES = ("x", "yh", "core", "yl", "z")
SIZES = (4, 2, 2, 2, 8)
ROW_GROUP = ("core", "z")
COL_GROUP = ("x", "yh", "yl")

EPSILON = eps_factor * math.sqrt(WIDTH)
LOG2E = math.log2(math.e)
LOG2_MASS = -math.log2(16384)


PIECE = 64
BLOCK = 2 * PIECE
TAIL = 16
UNIT = PIECE + TAIL


def number(place):
    index = 0
    for size, at in zip(SIZES, place):
        index = index * size + at % size
    return index


def moved(a, move):
    pairs = []
    for x in range(4):
        for y in range(4):
            for core in range(2):
                for z in range(8):
                    tx, ty, tcore, tz = move(x, y, core, z)
                    source = (x, y // 2, core, y % 2, z)
                    pairs.append((number(source), number((tx, ty // 2, tcore, ty % 2, tz))))
    return lax.ppermute(a, AXES, pairs)


def swap_core(a):
    return moved(a, lambda x, y, core, z: (x, y, 1 - core, z))


def shift_z(a):
    return moved(a, lambda x, y, core, z: (x, y, core, z + 1 - 2 * core))


def swap_x(a, flips):
    return moved(a, lambda x, y, core, z: (x ^ flips[core], y, core, z))


def swap_y(a, flips):
    return moved(a, lambda x, y, core, z: (x, y ^ flips[core], core, z))


def spread(copies, group):
    return lax.all_to_all(copies, group, 0, 0)


def side(position):
    core = lax.axis_index("core")
    low, high = position
    return jnp.where(core == 0, low, high), jnp.where(core == 0, high, low ^ high)


def sides():
    x = lax.axis_index("x")
    along_x = side((x % 2, x // 2))
    along_y = side((lax.axis_index("yl"), lax.axis_index("yh")))
    return along_x + along_y, along_y + along_x


def doubled(part, other, at):
    return jnp.where(
        at == 0,
        jnp.concatenate([part, other], axis=0),
        jnp.concatenate([other, part], axis=0),
    )


def gather(noise, data):
    first, second = (1, 3), (3, 1)
    moves = [(swap_x, first), (swap_x, second), (swap_y, first), (swap_y, second)]
    moves = moves, moves[2:] + moves[:2]
    parts = [data[: PIECE // 2], data[PIECE // 2 :]]
    straight, beside = [noise], []
    for step in range(3):
        received = [swap(part, flips) for part, (swap, flips) in zip(parts, [m[step] for m in moves])]
        near = shift_z(straight[-1])
        by = swap_core(noise) if step == 0 else shift_z(beside[-1])
        *received, near, by = lax.optimization_barrier((*received, near, by))
        straight.append(near)
        beside.append(by)
        parts = [
            doubled(part, other, at[step]) for part, other, at in zip(parts, received, sides())
        ]
    pieces = []
    for part, m in zip(parts, moves):
        swap, flips = m[3]
        pieces.append([part, swap(part[:BLOCK], flips), swap(part[BLOCK:], flips)])
    beside.append(shift_z(beside[-1]))
    straight.append(shift_z(straight[-1]))
    early = swap_core(jnp.concatenate([straight[1], beside[1], straight[2], beside[2], straight[3]], axis=0))
    late = swap_core(jnp.concatenate([beside[3], straight[4]], axis=0))
    rows = [noise, beside[0], straight[1], beside[1], straight[2], beside[2]]
    return pieces[0] + pieces[1], rows + [straight[3], beside[3], straight[4], early, late]


def to_lanes(square):
    return jnp.concatenate([square[k : k + 1, :] for k in range(8)], axis=1)


def to_square(lanes):
    return jnp.concatenate([lanes[:, 128 * k : 128 * k + 128] for k in range(8)], axis=0)


def own_first(square):
    swapped = jnp.concatenate([square[:, PIECE:], square[:, :PIECE]], axis=1)
    return jnp.where(lax.axis_index("core") == 0, square, swapped)


def lse2(parts):
    top = jnp.max(parts, axis=0)
    return top + jnp.log2(jnp.sum(jnp.exp2(parts - top[None]), axis=0))


def send(out_ref, square):
    out_ref[...] = jnp.broadcast_to(square[None], (16, 8, 128))


def terms(lanes):
    high = lanes.astype(jnp.bfloat16)
    rest = lanes - high.astype(jnp.float32)
    low = rest.astype(jnp.bfloat16)
    zeros = jnp.zeros((14, ROWS), jnp.bfloat16)
    return jnp.concatenate([high, low, zeros], axis=0)


def down(row):
    return jnp.transpose(jnp.broadcast_to(row, (128, 128)))[:, :1]


def across(column):
    return jnp.transpose(jnp.broadcast_to(column, (128, 128)))[:1, :]


def square_sums(block):
    wide = block.astype(jnp.float32)
    return jnp.sum(wide * wide, axis=1, keepdims=True)


def along_z(steps):
    return jnp.bitwise_and(lax.axis_index("z") + (1 - 2 * lax.axis_index("core")) * steps, 7)


def flipped(block):
    return jnp.concatenate([block[PIECE:], block[:PIECE]], axis=0)


def places():
    starts = []
    for h, at in enumerate(sides()):
        own = 512 * h + 256 * at[3]
        other = 512 * h + 256 - 256 * at[3]
        starts += [own, other, other + BLOCK]
    return [pl.multiple_of(start, BLOCK) for start in starts]


def scores_kernel(d0, d1, d2, d3, d4, d5, n0, b0, n1, b1, n2, b2, n3, b3, n4, early, late, *outs):
    score_ref, out_ref, lse_ref = outs
    scale = LOG2E / EPSILON
    swapped = [early[pl.ds(PIECE * k, PIECE), :] for k in range(5)]
    swapped += [late[pl.ds(PIECE * k, PIECE), :] for k in range(2)]
    pairs = [
        (0, 4, [n0[...], b0[...], n4[...], swapped[6]]),
        (-1, 1, [n1[...], b1[...], swapped[1], swapped[0]]),
        (-2, 2, [n2[...], b2[...], swapped[3], swapped[2]]),
        (-3, 3, [n3[...], b3[...], swapped[5], swapped[4]]),
    ]
    pieces = list(zip((d0, d1, d2, d3, d4, d5), places()))
    data_norms = [
        jnp.concatenate(
            [square_sums(data[pl.ds(at, 128), :]) for at in range(0, data.shape[0], 128)], axis=0
        )
        for data, _ in pieces
    ]
    for first, second, shards in pairs:
        noise = jnp.concatenate(shards, axis=0)
        noise_norms = jnp.concatenate(
            [across(square_sums(noise[:BLOCK])), across(square_sums(noise[BLOCK:]))], axis=1
        )
        found = []
        for (data, _), norms in zip(pieces, data_norms):
            products = lax.dot_general(
                data[...], noise, (((1,), (1,)), ((), ())), preferred_element_type=jnp.float32
            )
            found.append((2.0 * products - (norms + noise_norms)) * scale)
        top = functools.reduce(
            jnp.maximum, [jnp.max(scores, axis=0, keepdims=True) for scores in found]
        )
        total = sum(jnp.sum(jnp.exp2(scores - top), axis=0, keepdims=True) for scores in found)
        row = top + jnp.log2(total)
        for half, steps in enumerate((first, second)):
            at = along_z(steps)
            lanes = slice(BLOCK * half, BLOCK * half + BLOCK)
            lse_ref[pl.ds(at, 1), :] = row[:, lanes]
            columns = pl.ds(pl.multiple_of(at * 128, 128), 128)
            for scores, (data, start) in zip(found, pieces):
                score_ref[pl.ds(start, data.shape[0]), columns] = scores[:, lanes]
    send(out_ref, own_first(lse_ref[...]))


def columns_kernel(score_ref, in_ref, dual_ref, out_ref):
    dual = own_first(LOG2_MASS - lse2(in_ref[...]))
    dual_ref[...] = dual
    along = to_lanes(dual)
    rows = []
    for k in range(8):
        shifted = score_ref[pl.ds(128 * k, 128), :] + along
        top = jnp.max(shifted, axis=1, keepdims=True)
        total = jnp.sum(jnp.exp2(shifted - top), axis=1, keepdims=True)
        rows.append(across(top + jnp.log2(total)))
    send(out_ref, jnp.concatenate(rows, axis=0))


def plan_kernel(score_ref, dual_ref, in_ref, plan_ref, out_ref):
    along = to_lanes(dual_ref[...])
    dual = LOG2_MASS - lse2(in_ref[...])
    sums = jnp.zeros((1, ROWS), jnp.float32)
    for k in range(8):
        part = pl.ds(128 * k, 128)
        lifted = down(dual[k : k + 1, :] - LOG2_MASS)
        plan = jnp.exp2(score_ref[part, :] + along + lifted)
        plan_ref[part, :] = plan.astype(jnp.bfloat16)
        sums = sums + jnp.sum(plan, axis=0, keepdims=True)
    send(out_ref, own_first(to_square(sums)))


def column_sums_kernel(plan_ref, in_ref, out_ref):
    scale = own_first(1.0 / jnp.sum(in_ref[...], axis=0))
    sums = lax.dot_general(
        terms(to_lanes(scale)),
        plan_ref[...],
        (((1,), (1,)), ((), ())),
        preferred_element_type=jnp.float32,
    )
    send(out_ref, to_square(sums[0:1, :] + sums[1:2, :]))


def row_sums_kernel(plan_ref, in_ref, out_ref):
    scale = 1.0 / jnp.sum(in_ref[...], axis=0)
    sums = jnp.dot(terms(to_lanes(scale)), plan_ref[...], preferred_element_type=jnp.float32)
    send(out_ref, own_first(to_square(sums[0:1, :] + sums[1:2, :])))


def packed(total):
    high = total.astype(jnp.bfloat16)
    low = (total - high.astype(jnp.float32)).astype(jnp.bfloat16)
    zeros = jnp.zeros((TAIL - 2, 128), jnp.bfloat16)
    narrow = jnp.concatenate([high, low, zeros], axis=0)
    return jnp.concatenate([narrow, jnp.zeros((TAIL, WIDTH - 128), jnp.bfloat16)], axis=1)


def unpacked(tail):
    return tail[0:1, :128].astype(jnp.float32) + tail[1:2, :128].astype(jnp.float32)


def halves_turned(total):
    return jnp.concatenate([total[:, PIECE:], total[:, :PIECE]], axis=1)


def give_unit(ref, index, rows, total):
    ref[pl.ds(index * UNIT, PIECE), :] = rows
    ref[pl.ds(index * UNIT + PIECE, TAIL), :] = packed(total)


def share(mine, give, index, rows, total):
    give_unit(mine, index, rows[:PIECE], total)
    give_unit(give, index, rows[PIECE:], halves_turned(total))


def whole(ref, index, rows, total, turned):
    parts = [(rows[:PIECE], total), (rows[PIECE:], halves_turned(total))]
    for k, (part, sums) in enumerate(parts[::-1] if turned else parts):
        give_unit(ref, index + k, part, sums)


def pair_targets(weight_ref, sum_ref, pieces, first, second):
    at = [along_z(first), along_z(second)]
    lanes = [pl.ds(pl.multiple_of(k * 128, 128), 128) for k in at]
    out = 0.0
    for data, start in pieces:
        rows = pl.ds(start, data.shape[0])
        weights = jnp.concatenate([weight_ref[rows, part] for part in lanes], axis=1)
        out = out + lax.dot_general(
            weights, data[...], (((0,), (0,)), ((), ())), preferred_element_type=jnp.float32
        )
    out = out.astype(jnp.bfloat16)
    return (out[:BLOCK], sum_ref[pl.ds(at[0], 1), :]), (out[BLOCK:], sum_ref[pl.ds(at[1], 1), :])


def early_targets_kernel(plan_ref, in_ref, d0, d1, d2, d3, d4, d5, *outs):
    weight_ref, sum_ref, mine, give = outs
    scale = 1.0 / jnp.sum(in_ref[...], axis=0)
    sums = jnp.zeros((1, ROWS), jnp.float32)
    for k in range(8):
        part = pl.ds(128 * k, 128)
        weights = plan_ref[part, :].astype(jnp.float32) * down(scale[k : k + 1, :])
        weight_ref[part, :] = weights.astype(jnp.bfloat16)
        sums = sums + jnp.sum(weights, axis=0, keepdims=True)
    sum_ref[...] = to_square(sums)
    pieces = list(zip((d0, d1, d2, d3, d4, d5), places()))
    far, third = pair_targets(weight_ref, sum_ref, pieces, 4, -3)
    share(mine, give, 0, *far)
    whole(give, 1, *third, True)


def late_targets_kernel(weight_ref, sum_ref, d0, d1, d2, d3, d4, d5, mine, give):
    pieces = list(zip((d0, d1, d2, d3, d4, d5), places()))
    two, one = pair_targets(weight_ref, sum_ref, pieces, -2, -1)
    whole(give, 0, *two, True)
    whole(give, 2, *one, True)
    home, third = pair_targets(weight_ref, sum_ref, pieces, 0, 3)
    give_unit(mine, 6, home[0][:PIECE], home[1])
    give_unit(give, 4, home[0][PIECE:], halves_turned(home[1]))
    whole(mine, 0, *third, False)
    two, one = pair_targets(weight_ref, sum_ref, pieces, 2, 1)
    whole(mine, 2, *two, False)
    whole(mine, 4, *one, False)


def summed(a, b):
    body = a[:PIECE].astype(jnp.float32) + b[:PIECE].astype(jnp.float32)
    tail = packed(unpacked(a[PIECE:]) + unpacked(b[PIECE:]))
    return jnp.concatenate([body.astype(jnp.bfloat16), tail], axis=0)


def unit(ref, index):
    return ref[pl.ds(index * UNIT, UNIT), :]


def start_kernel(far, late, got, far_ref, third0_ref, third1_ref):
    far_ref[...] = summed(far[...], unit(got, 0))
    third0_ref[...] = summed(unit(late, 0), unit(got, 1))
    third1_ref[...] = summed(unit(late, 1), unit(got, 2))


def rest_kernel(late, got, *outs):
    for k, out in enumerate(outs):
        out[...] = summed(unit(late, 2 + k), unit(got, k))


def unit_kernel(a_ref, b_ref, out_ref):
    out_ref[...] = summed(a_ref[...], b_ref[...])


def velocity_kernel(last_ref, home_ref, other_ref, noise_ref, out_ref):
    last, home, other = last_ref[...], home_ref[...], other_ref[...]
    body = last[:PIECE].astype(jnp.float32) + home[:PIECE].astype(jnp.float32)
    body = body + other[:PIECE].astype(jnp.float32)
    total = unpacked(last[PIECE:]) + unpacked(home[PIECE:]) + unpacked(other[PIECE:])
    target = body / down(total)[:PIECE]
    out_ref[...] = (target - noise_ref[...].astype(jnp.float32)).astype(jnp.bfloat16)


SQUARE = jax.ShapeDtypeStruct((8, 128), jnp.float32)
COPIES = jax.ShapeDtypeStruct((16, 8, 128), jnp.float32)


def in_vmem(rows, dtype):
    return pltpu.VMEM((rows, 1024), dtype)


def run(kernel, outs, *args, flops=0, scratch=()):
    return pl.pallas_call(
        kernel,
        out_shape=outs,
        in_specs=[pl.BlockSpec(memory_space=pltpu.VMEM)] * len(args),
        out_specs=jax.tree.map(lambda _: pl.BlockSpec(memory_space=pltpu.VMEM), outs),
        scratch_shapes=scratch,
        compiler_params=pltpu.CompilerParams(vmem_limit_bytes=40 * 1024 * 1024),
        cost_estimate=pl.CostEstimate(flops=flops, bytes_accessed=4 << 20, transcendentals=0),
    )(*args)


def keep(a):
    return pltpu.with_memory_space_constraint(a, pltpu.VMEM)


def units(count):
    return jax.ShapeDtypeStruct((count * UNIT, WIDTH), jnp.bfloat16)


def per_device(noise_latents, data_latents):
    columns, rows = gather(noise_latents, data_latents)

    scores, parts = run(
        scores_kernel,
        (in_vmem(ROWS, jnp.float32), COPIES),
        *columns,
        *rows,
        scratch=[pltpu.VMEM((8, 128), jnp.float32)],
    )
    scores = keep(scores)
    row_dual, parts = run(columns_kernel, (SQUARE, COPIES), scores, spread(parts, ROW_GROUP))
    plan, parts = run(
        plan_kernel,
        (in_vmem(ROWS, jnp.bfloat16), COPIES),
        scores,
        row_dual,
        spread(parts, COL_GROUP),
    )
    plan = keep(plan)
    parts = run(column_sums_kernel, COPIES, plan, spread(parts, ROW_GROUP))
    parts = run(row_sums_kernel, COPIES, plan, spread(parts, COL_GROUP))
    parts = run(column_sums_kernel, COPIES, plan, spread(parts, ROW_GROUP))

    weights, sums, far, give = run(
        early_targets_kernel,
        (in_vmem(ROWS, jnp.bfloat16), SQUARE, units(1), units(3)),
        plan,
        spread(parts, COL_GROUP),
        *columns,
    )
    got = swap_core(give)
    late, give = run(late_targets_kernel, (units(7), units(5)), keep(weights), sums, *columns)
    got_late = swap_core(give)
    far, third0, third1 = run(start_kernel, (units(1),) * 3, far, late, got)
    straight, beside = shift_z(far), shift_z(third1)
    two0, two1, one0, one1, home = run(rest_kernel, (units(1),) * 5, late, got_late)

    straight = shift_z(run(unit_kernel, units(1), third0, straight))
    beside = shift_z(run(unit_kernel, units(1), two1, beside))
    straight = shift_z(run(unit_kernel, units(1), two0, straight))
    beside = shift_z(run(unit_kernel, units(1), one1, beside))
    straight = shift_z(run(unit_kernel, units(1), one0, straight))
    other = swap_core(beside)
    velocity = jax.ShapeDtypeStruct((PIECE, WIDTH), jnp.bfloat16)
    return run(velocity_kernel, velocity, straight, home, other, noise_latents)


def solution(mesh):
    fine = Mesh(mesh.devices.reshape(SIZES), AXES)
    rows = P(AXES, None)
    return jax.shard_map(
        per_device, mesh=fine, in_specs=(rows, rows), out_specs=rows, check_vma=False
    )
```

time: 171 us -> 160 us (0.936); the launches traced: 168 us -> 159 us
  waiting for transfers between devices: 61.7 us -> 48 us
  starting transfers between devices: 18.1 us -> 27.6 us
  blocking collectives: 72.5 us -> 66.9 us
  Pallas kernels: 12.3 us -> 15 us
  other arithmetic: 2.33 us -> 0.42 us
    ppermute x20 -> x30, waiting for transfers between devices: 61.7 us -> 48 us  [moved(): return lax.ppermute(a, AXES, pairs)]
    ppermute x20 -> x30, starting transfers between devices: 18.1 us -> 27.6 us  [moved(): return lax.ppermute(a, AXES, pairs)]
    all_to_all x6, blocking collectives: 72.5 us -> 66.9 us  [spread(): return lax.all_to_all(copies, group, 0, 0)]
    pallas_call x12 -> x16, Pallas kernels: 12.3 us -> 15 us  [run(): pl.pallas_call(kernel, out_shape=outs, in_specs=[pl.BlockSpec(memory_spac...]
  transfers between devices with their start and end apart: 20 -> 30, of which waited for: 16 -> 21; matrix products, arithmetic and copies ran while one was open for 1% -> 1% of each run, Pallas kernels for 0% -> 0%
where the time goes in v5:
time: 160 us; the launch traced here: 159 us
  blocking collectives  66.9 us (42%)
  waiting for transfers between devices  48 us (30%)
  starting transfers between devices  27.6 us (17%)
  Pallas kernels  15 us (9%)
    all_to_all x6, blocking collectives, spread(): return lax.all_to_all(copies, group, 0, 0)  66.9 us
    ppermute x30, waiting for transfers between devices, moved(): return lax.ppermute(a, AXES, pairs)  48 us
    ppermute x30, starting transfers between devices, moved(): return lax.ppermute(a, AXES, pairs)  27.6 us
    pallas_call x16, Pallas kernels, run(): pl.pallas_call(kernel, out_shape=outs, in_specs=[pl.BlockSpec(memory_spac...  15 us
  transfers between devices with their start and end apart: 30, of which 21 were waited for; matrix products, arithmetic and copies ran while one was open for 1% of the time, Pallas kernels for 0%

profile of v5, /device:TPU:2, one launch (start us, length us, event | category | flops | bytes accessed | tf_op | source)
XLA Modules:
  0.0 159.2 jit_solution(14349347249621112072)
XLA Ops:
  0.0 1.9 %collective-permute-start.2 = (bf16[64,1024]{1,0:T(8,128)(2,1)}, bf16[64,1024]{1,0:T(8,128)(2,1)S(1)}, u32[]{:S(2)}, u32[]{:S(2)}) collective-permute-start(bf16[64,1024]{1,0:T(8,128)(2,1)} %noise_ref.1), channel_id=1, source_target_pairs={{0,1},{1,2},{2,3},{3,4},{4,5},{5,6},{6,7},{7,0},{16,23},{17,16},{1... | collective-permute-start | bytes 393224 | tf_op jit(solution)/shard_map/ppermute | solution.py:48
  5.0 2.2 %collective-permute-done.1 = bf16[32,1024]{1,0:T(8,128)(2,1)S(1)} collective-permute-done((bf16[32,1024]{1,0:T(8,128)(2,1)S(1)}, bf16[32,1024]{1,0:T(8,128)(2,1)S(1)}, u32[]{:S(2)}, u32[]{:S(2)}) %collective-permute-start.1) | collective-permute-done | bytes 65568 | tf_op jit(solution)/shard_map/ppermute | solution.py:48
  9.0 3.1 %collective-permute-start.5 = (bf16[64,1024]{1,0:T(8,128)(2,1)S(1)}, bf16[64,1024]{1,0:T(8,128)(2,1)S(1)}, u32[]{:S(2)}, u32[]{:S(2)}) collective-permute-start(bf16[64,1024]{1,0:T(8,128)(2,1)S(1)} %maximum_select_fusion.5), channel_id=1, source_target_pairs={{0,40},{1,41},{2,42},{3,43},{4,44},{5,45},{6,46},{7,47},{16,24},{1... | collective-permute-start | bytes 393224 | tf_op jit(solution)/shard_map/ppermute | solution.py:48
  14.6 1.9 %collective-permute-start.6 = (bf16[64,1024]{1,0:T(8,128)(2,1)S(1)}, bf16[64,1024]{1,0:T(8,128)(2,1)S(1)}, u32[]{:S(2)}, u32[]{:S(2)}) collective-permute-start(bf16[64,1024]{1,0:T(8,128)(2,1)S(1)} %collective-permute-done.2.n1), channel_id=1, source_target_pairs={{0,1},{1,2},{2,3},{3,4},{4,5},{5,6},{6,7},{7,0},{16,23},{17,16},{1... | collective-permute-start | bytes 393224 | tf_op jit(solution)/shard_map/ppermute | solution.py:48
  17.2 2.7 %collective-permute-done.7.b1 = bf16[64,1024]{1,0:T(8,128)(2,1)S(1)} collective-permute-done((bf16[64,1024]{1,0:T(8,128)(2,1)S(1)}, bf16[64,1024]{1,0:T(8,128)(2,1)S(1)}, u32[]{:S(2)}, u32[]{:S(2)}) %collective-permute-start.7) | collective-permute-done | bytes 131104 | tf_op jit(solution)/shard_map/ppermute | solution.py:48
  21.4 1.9 %collective-permute-start.9 = (bf16[128,1024]{1,0:T(8,128)(2,1)S(1)}, bf16[128,1024]{1,0:T(8,128)(2,1)S(1)}, u32[]{:S(2)}, u32[]{:S(2)}) collective-permute-start(bf16[128,1024]{1,0:T(8,128)(2,1)S(1)} %maximum_select_fusion.3), channel_id=1, source_target_pairs={{0,64},{1,65},{2,66},{3,67},{4,68},{5,69},{6,70},{7,71},{16,208},{... | collective-permute-start | bytes 786440 | tf_op jit(solution)/shard_map/ppermute | solution.py:48
  25.0 2.4 %collective-permute-start.11 = (bf16[64,1024]{1,0:T(8,128)(2,1)S(1)}, bf16[64,1024]{1,0:T(8,128)(2,1)S(1)}, u32[]{:S(2)}, u32[]{:S(2)}) collective-permute-start(bf16[64,1024]{1,0:T(8,128)(2,1)S(1)} %collective-permute-done.7.b1), channel_id=1, source_target_pairs={{0,1},{1,2},{2,3},{3,4},{4,5},{5,6},{6,7},{7,0},{16,23},{17,16},{1... | collective-permute-start | bytes 393224 | tf_op jit(solution)/shard_map/ppermute | solution.py:48
  27.5 2.5 %collective-permute-done.10.n3 = bf16[64,1024]{1,0:T(8,128)(2,1)S(1)} collective-permute-done((bf16[64,1024]{1,0:T(8,128)(2,1)S(1)}, bf16[64,1024]{1,0:T(8,128)(2,1)S(1)}, u32[]{:S(2)}, u32[]{:S(2)}) %collective-permute-start.10) | collective-permute-done | bytes 131104 | tf_op jit(solution)/shard_map/ppermute | solution.py:48
  34.4 2.0 %collective-permute-start.14 = (bf16[128,1024]{1,0:T(8,128)(2,1)S(1)}, bf16[128,1024]{1,0:T(8,128)(2,1)S(1)}, u32[]{:S(2)}, u32[]{:S(2)}) collective-permute-start(bf16[128,1024]{1,0:T(8,128)(2,1)S(1)} %get-tuple-element.70), channel_id=1, source_target_pairs={{0,192},{1,193},{2,194},{3,195},{4,196},{5,197},{6,198},{7,199},{1... | collective-permute-start | bytes 786440 | tf_op jit(solution)/shard_map/ppermute | solution.py:48
  40.9 2.6 %collective-permute-done.14.d4 = bf16[128,1024]{1,0:T(8,128)(2,1)S(1)} collective-permute-done((bf16[128,1024]{1,0:T(8,128)(2,1)S(1)}, bf16[128,1024]{1,0:T(8,128)(2,1)S(1)}, u32[]{:S(2)}, u32[]{:S(2)}) %collective-permute-start.14) | collective-permute-done | bytes 262176 | tf_op jit(solution)/shard_map/ppermute | solution.py:48
  45.2 2.8 %collective-permute-done.12.d1 = bf16[128,1024]{1,0:T(8,128)(2,1)S(1)} collective-permute-done((bf16[128,1024]{1,0:T(8,128)(2,1)S(1)}, bf16[128,1024]{1,0:T(8,128)(2,1)S(1)}, u32[]{:S(2)}, u32[]{:S(2)}) %collective-permute-start.12) | collective-permute-done | bytes 262176 | tf_op jit(solution)/shard_map/ppermute | solution.py:48
  48.0 5.2 %shard_map.28 = (f32[1024,1024]{1,0:T(8,128)S(1)}, f32[16,8,128]{2,1,0:T(8,128)S(1)}) custom-call(bf16[256,1024]{1,0:T(8,128)(2,1)S(1)} %maximum_select_fusion.d0, bf16[128,1024]{1,0:T(8,128)(2,1)S(1)} %collective-permute-done.12.d1, bf16[128,1024]{1,0:T(8,128)(2,1)S(1)} %collective-permute-done.13.d2, bf16[256,1024]{1,0:T(8,128)(2,1)S(1)} %maximum_select_fusion.1.d3, ...), custom_call_target="tpu_custom_call" | custom-call | bytes 4194304 | tf_op jit(solution)/shard_map/pallas_call | solution.py:386
  53.2 14.7 %all_to_all.30.in_ref = f32[16,8,128]{2,1,0:T(8,128)S(1)} all-to-all(f32[16,8,128]{2,1,0:T(8,128)S(1)} %get-tuple-element.50), channel_id=1, replica_groups=mesh['x'=4,'yh'=2,'core'=2,'yl'=2,'z'=8] {'core','z'}, dimensions={0} | all-to-all | bytes 131072 | tf_op jit(solution)/shard_map/all_to_all | solution.py:68
  69.1 9.4 %all_to_all.31.in_ref = f32[16,8,128]{2,1,0:T(8,128)S(1)} all-to-all(f32[16,8,128]{2,1,0:T(8,128)S(1)} %get-tuple-element.52), channel_id=1, replica_groups=mesh['x'=4,'yh'=2,'core'=2,'yl'=2,'z'=8] {'x','yh','yl'}, dimensions={0} | all-to-all | bytes 131072 | tf_op jit(solution)/shard_map/all_to_all | solution.py:68
  79.5 10.5 %all_to_all.32.in_ref = f32[16,8,128]{2,1,0:T(8,128)S(1)} all-to-all(f32[16,8,128]{2,1,0:T(8,128)S(1)} %get-tuple-element.54), channel_id=1, replica_groups=mesh['x'=4,'yh'=2,'core'=2,'yl'=2,'z'=8] {'core','z'}, dimensions={0} | all-to-all | bytes 131072 | tf_op jit(solution)/shard_map/all_to_all | solution.py:68
  90.7 10.9 %all_to_all.33.in_ref = f32[16,8,128]{2,1,0:T(8,128)S(1)} all-to-all(f32[16,8,128]{2,1,0:T(8,128)S(1)} %shard_map.31), channel_id=1, replica_groups=mesh['x'=4,'yh'=2,'core'=2,'yl'=2,'z'=8] {'x','yh','yl'}, dimensions={0} | all-to-all | bytes 131072 | tf_op jit(solution)/shard_map/all_to_all | solution.py:68
  102.0 10.5 %all_to_all.34.in_ref = f32[16,8,128]{2,1,0:T(8,128)S(1)} all-to-all(f32[16,8,128]{2,1,0:T(8,128)S(1)} %shard_map.32), channel_id=1, replica_groups=mesh['x'=4,'yh'=2,'core'=2,'yl'=2,'z'=8] {'core','z'}, dimensions={0} | all-to-all | bytes 131072 | tf_op jit(solution)/shard_map/all_to_all | solution.py:68
  113.2 10.9 %all_to_all.35.in_ref = f32[16,8,128]{2,1,0:T(8,128)S(1)} all-to-all(f32[16,8,128]{2,1,0:T(8,128)S(1)} %shard_map.33), channel_id=1, replica_groups=mesh['x'=4,'yh'=2,'core'=2,'yl'=2,'z'=8] {'x','yh','yl'}, dimensions={0} | all-to-all | bytes 131072 | tf_op jit(solution)/shard_map/all_to_all | solution.py:68
  125.9 2.7 %shard_map.35 = (bf16[560,1024]{1,0:T(8,128)(2,1)S(1)}, bf16[400,1024]{1,0:T(8,128)(2,1)S(1)}) custom-call(bf16[1024,1024]{1,0:T(8,128)(2,1)S(1)} %get-tuple-element.55.weight_ref, f32[8,128]{1,0:T(8,128)S(1)} %get-tuple-element.56.sum_ref, bf16[256,1024]{1,0:T(8,128)(2,1)S(1)} %maximum_select_fusion.d0, bf16[128,1024]{1,0:T(8,128)(2,1)S(1)} %collective-permute-done.12.d1, ...), custom_call_target="tpu_custom_call" | custom-call | bytes 4194304 | tf_op jit(solution)/shard_map/pallas_call | solution.py:386
  129.2 2.5 %collective-permute-done.21.got = bf16[240,1024]{1,0:T(8,128)(2,1)S(1)} collective-permute-done((bf16[240,1024]{1,0:T(8,128)(2,1)S(1)}, bf16[240,1024]{1,0:T(8,128)(2,1)S(1)}, u32[]{:S(2)}, u32[]{:S(2)}) %collective-permute-start.21) | collective-permute-done | bytes 491552 | tf_op jit(solution)/shard_map/ppermute | solution.py:48
  133.5 4.9 %collective-permute-done.22.b_ref = bf16[80,1024]{1,0:T(8,128)(2,1)S(1)} collective-permute-done((bf16[80,1024]{1,0:T(8,128)(2,1)S(1)}, bf16[80,1024]{1,0:T(8,128)(2,1)S(1)}, u32[]{:S(2)}, u32[]{:S(2)}) %collective-permute-start.22) | collective-permute-done | bytes 163872 | tf_op jit(solution)/shard_map/ppermute | solution.py:48
  140.3 4.8 %collective-permute-done.23.b_ref = bf16[80,1024]{1,0:T(8,128)(2,1)S(1)} collective-permute-done((bf16[80,1024]{1,0:T(8,128)(2,1)S(1)}, bf16[80,1024]{1,0:T(8,128)(2,1)S(1)}, u32[]{:S(2)}, u32[]{:S(2)}) %collective-permute-start.23) | collective-permute-done | bytes 163872 | tf_op jit(solution)/shard_map/ppermute | solution.py:48
  146.9 4.8 %collective-permute-done.24.b_ref = bf16[80,1024]{1,0:T(8,128)(2,1)S(1)} collective-permute-done((bf16[80,1024]{1,0:T(8,128)(2,1)S(1)}, bf16[80,1024]{1,0:T(8,128)(2,1)S(1)}, u32[]{:S(2)}, u32[]{:S(2)}) %collective-permute-start.24) | collective-permute-done | bytes 163872 | tf_op jit(solution)/shard_map/ppermute | solution.py:48
  153.5 4.9 %collective-permute-done.25.last_ref = bf16[80,1024]{1,0:T(8,128)(2,1)S(1)} collective-permute-done((bf16[80,1024]{1,0:T(8,128)(2,1)S(1)}, bf16[80,1024]{1,0:T(8,128)(2,1)S(1)}, u32[]{:S(2)}, u32[]{:S(2)}) %collective-permute-start.25) | collective-permute-done | bytes 163872 | tf_op jit(solution)/shard_map/ppermute | solution.py:48
  (75 shorter events, 36.2 us)
Async XLA Ops:
  0.0 8.7 %collective-permute-start.3 = (bf16[64,1024]{1,0:T(8,128)(2,1)}, bf16[64,1024]{1,0:T(8,128)(2,1)S(1)}, u32[]{:S(2)}, u32[]{:S(2)}) collective-permute-start(bf16[64,1024]{1,0:T(8,128)(2,1)} %noise_ref.1), channel_id=1, source_target_pairs={{0,16},{1,17},{2,18},{3,19},{4,20},{5,21},{6,22},{7,23},{16,0},{17... | collective-permute-start | bytes 393224 | tf_op jit(solution)/shard_map/ppermute | solution.py:48
  0.0 9.0 %collective-permute-start.2 = (bf16[64,1024]{1,0:T(8,128)(2,1)}, bf16[64,1024]{1,0:T(8,128)(2,1)S(1)}, u32[]{:S(2)}, u32[]{:S(2)}) collective-permute-start(bf16[64,1024]{1,0:T(8,128)(2,1)} %noise_ref.1), channel_id=1, source_target_pairs={{0,1},{1,2},{2,3},{3,4},{4,5},{5,6},{6,7},{7,0},{16,23},{17,16},{1... | collective-permute-start | bytes 393224 | tf_op jit(solution)/shard_map/ppermute | solution.py:48
  9.0 7.4 %collective-permute-start.5 = (bf16[64,1024]{1,0:T(8,128)(2,1)S(1)}, bf16[64,1024]{1,0:T(8,128)(2,1)S(1)}, u32[]{:S(2)}, u32[]{:S(2)}) collective-permute-start(bf16[64,1024]{1,0:T(8,128)(2,1)S(1)} %maximum_select_fusion.5), channel_id=1, source_target_pairs={{0,40},{1,41},{2,42},{3,43},{4,44},{5,45},{6,46},{7,47},{16,24},{1... | collective-permute-start | bytes 393224 | tf_op jit(solution)/shard_map/ppermute | solution.py:48
  14.6 6.8 %collective-permute-start.6 = (bf16[64,1024]{1,0:T(8,128)(2,1)S(1)}, bf16[64,1024]{1,0:T(8,128)(2,1)S(1)}, u32[]{:S(2)}, u32[]{:S(2)}) collective-permute-start(bf16[64,1024]{1,0:T(8,128)(2,1)S(1)} %collective-permute-done.2.n1), channel_id=1, source_target_pairs={{0,1},{1,2},{2,3},{3,4},{4,5},{5,6},{6,7},{7,0},{16,23},{17,16},{1... | collective-permute-start | bytes 393224 | tf_op jit(solution)/shard_map/ppermute | solution.py:48
  21.4 10.0 %collective-permute-start.9 = (bf16[128,1024]{1,0:T(8,128)(2,1)S(1)}, bf16[128,1024]{1,0:T(8,128)(2,1)S(1)}, u32[]{:S(2)}, u32[]{:S(2)}) collective-permute-start(bf16[128,1024]{1,0:T(8,128)(2,1)S(1)} %maximum_select_fusion.3), channel_id=1, source_target_pairs={{0,64},{1,65},{2,66},{3,67},{4,68},{5,69},{6,70},{7,71},{16,208},{... | collective-permute-start | bytes 786440 | tf_op jit(solution)/shard_map/ppermute | solution.py:48
  23.3 8.0 %collective-permute-start.8 = (bf16[128,1024]{1,0:T(8,128)(2,1)S(1)}, bf16[128,1024]{1,0:T(8,128)(2,1)S(1)}, u32[]{:S(2)}, u32[]{:S(2)}) collective-permute-start(bf16[128,1024]{1,0:T(8,128)(2,1)S(1)} %maximum_select_fusion.2), channel_id=1, source_target_pairs={{0,8},{1,9},{2,10},{3,11},{4,12},{5,13},{6,14},{7,15},{16,56},{17,... | collective-permute-start | bytes 786440 | tf_op jit(solution)/shard_map/ppermute | solution.py:48
  23.7 6.3 %collective-permute-start.10 = (bf16[64,1024]{1,0:T(8,128)(2,1)S(1)}, bf16[64,1024]{1,0:T(8,128)(2,1)S(1)}, u32[]{:S(2)}, u32[]{:S(2)}) collective-permute-start(bf16[64,1024]{1,0:T(8,128)(2,1)S(1)} %collective-permute-done.6.n2), channel_id=1, source_target_pairs={{0,1},{1,2},{2,3},{3,4},{4,5},{5,6},{6,7},{7,0},{16,23},{17,16},{1... | collective-permute-start | bytes 393224 | tf_op jit(solution)/shard_map/ppermute | solution.py:48
  25.0 6.4 %collective-permute-start.11 = (bf16[64,1024]{1,0:T(8,128)(2,1)S(1)}, bf16[64,1024]{1,0:T(8,128)(2,1)S(1)}, u32[]{:S(2)}, u32[]{:S(2)}) collective-permute-start(bf16[64,1024]{1,0:T(8,128)(2,1)S(1)} %collective-permute-done.7.b1), channel_id=1, source_target_pairs={{0,1},{1,2},{2,3},{3,4},{4,5},{5,6},{6,7},{7,0},{16,23},{17,16},{1... | collective-permute-start | bytes 393224 | tf_op jit(solution)/shard_map/ppermute | solution.py:48
  31.4 6.2 %collective-permute-start.16 = (bf16[64,1024]{1,0:T(8,128)(2,1)S(1)}, bf16[64,1024]{1,0:T(8,128)(2,1)S(1)}, u32[]{:S(2)}, u32[]{:S(2)}) collective-permute-start(bf16[64,1024]{1,0:T(8,128)(2,1)S(1)} %collective-permute-done.11.b2), channel_id=1, source_target_pairs={{0,1},{1,2},{2,3},{3,4},{4,5},{5,6},{6,7},{7,0},{16,23},{17,16},{1... | collective-permute-start | bytes 393224 | tf_op jit(solution)/shard_map/ppermute | solution.py:48
  32.4 6.6 %collective-permute-start.17 = (bf16[64,1024]{1,0:T(8,128)(2,1)S(1)}, bf16[64,1024]{1,0:T(8,128)(2,1)S(1)}, u32[]{:S(2)}, u32[]{:S(2)}) collective-permute-start(bf16[64,1024]{1,0:T(8,128)(2,1)S(1)} %collective-permute-done.10.n3), channel_id=1, source_target_pairs={{0,1},{1,2},{2,3},{3,4},{4,5},{5,6},{6,7},{7,0},{16,23},{17,16},{1... | collective-permute-start | bytes 393224 | tf_op jit(solution)/shard_map/ppermute | solution.py:48
  34.0 13.9 %collective-permute-start.18 = (bf16[320,1024]{1,0:T(8,128)(2,1)S(1)}, bf16[320,1024]{1,0:T(8,128)(2,1)S(1)}, u32[]{:S(2)}, u32[]{:S(2)}) collective-permute-start(bf16[320,1024]{1,0:T(8,128)(2,1)S(1)} %constant_dynamic-update-slice_fusion), channel_id=1, source_target_pairs={{0,16},{1,17},{2,18},{3,19},{4,20},{5,21},{6,22},{7,23},{16,0},{17... | collective-permute-start | bytes 1966088 | tf_op jit(solution)/shard_map/ppermute | solution.py:48
  34.3 6.5 %collective-permute-start.15 = (bf16[128,1024]{1,0:T(8,128)(2,1)S(1)}, bf16[128,1024]{1,0:T(8,128)(2,1)S(1)}, u32[]{:S(2)}, u32[]{:S(2)}) collective-permute-start(bf16[128,1024]{1,0:T(8,128)(2,1)S(1)} %get-tuple-element.69), channel_id=1, source_target_pairs={{0,192},{1,193},{2,194},{3,195},{4,196},{5,197},{6,198},{7,199},{1... | collective-permute-start | bytes 786440 | tf_op jit(solution)/shard_map/ppermute | solution.py:48
  34.4 9.2 %collective-permute-start.14 = (bf16[128,1024]{1,0:T(8,128)(2,1)S(1)}, bf16[128,1024]{1,0:T(8,128)(2,1)S(1)}, u32[]{:S(2)}, u32[]{:S(2)}) collective-permute-start(bf16[128,1024]{1,0:T(8,128)(2,1)S(1)} %get-tuple-element.70), channel_id=1, source_target_pairs={{0,192},{1,193},{2,194},{3,195},{4,196},{5,197},{6,198},{7,199},{1... | collective-permute-start | bytes 786440 | tf_op jit(solution)/shard_map/ppermute | solution.py:48
  37.6 7.6 %collective-permute-start.13 = (bf16[128,1024]{1,0:T(8,128)(2,1)S(1)}, bf16[128,1024]{1,0:T(8,128)(2,1)S(1)}, u32[]{:S(2)}, u32[]{:S(2)}) collective-permute-start(bf16[128,1024]{1,0:T(8,128)(2,1)S(1)} %get-tuple-element.71), channel_id=1, source_target_pairs={{0,40},{1,41},{2,42},{3,43},{4,44},{5,45},{6,46},{7,47},{16,24},{1... | collective-permute-start | bytes 786440 | tf_op jit(solution)/shard_map/ppermute | solution.py:48
  39.0 9.0 %collective-permute-start.12 = (bf16[128,1024]{1,0:T(8,128)(2,1)S(1)}, bf16[128,1024]{1,0:T(8,128)(2,1)S(1)}, u32[]{:S(2)}, u32[]{:S(2)}) collective-permute-start(bf16[128,1024]{1,0:T(8,128)(2,1)S(1)} %get-tuple-element.72), channel_id=1, source_target_pairs={{0,40},{1,41},{2,42},{3,43},{4,44},{5,45},{6,46},{7,47},{16,24},{1... | collective-permute-start | bytes 786440 | tf_op jit(solution)/shard_map/ppermute | solution.py:48
  40.8 7.1 %collective-permute-start.19 = (bf16[128,1024]{1,0:T(8,128)(2,1)S(1)}, bf16[128,1024]{1,0:T(8,128)(2,1)S(1)}, u32[]{:S(2)}, u32[]{:S(2)}) collective-permute-start(bf16[128,1024]{1,0:T(8,128)(2,1)S(1)} %pad_maximum_fusion), channel_id=1, source_target_pairs={{0,16},{1,17},{2,18},{3,19},{4,20},{5,21},{6,22},{7,23},{16,0},{17... | collective-permute-start | bytes 786440 | tf_op jit(solution)/shard_map/ppermute | solution.py:48
  128.6 10.0 %collective-permute-start.20 = (bf16[400,1024]{1,0:T(8,128)(2,1)S(1)}, bf16[400,1024]{1,0:T(8,128)(2,1)S(1)}, u32[]{:S(2)}, u32[]{:S(2)}) collective-permute-start(bf16[400,1024]{1,0:T(8,128)(2,1)S(1)} %get-tuple-element.58), channel_id=1, source_target_pairs={{0,16},{1,17},{2,18},{3,19},{4,20},{5,21},{6,22},{7,23},{16,0},{17... | collective-permute-start | bytes 2457608 | tf_op jit(solution)/shard_map/ppermute | solution.py:48
  131.8 6.6 %collective-permute-start.22 = (bf16[80,1024]{1,0:T(8,128)(2,1)S(1)}, bf16[80,1024]{1,0:T(8,128)(2,1)S(1)}, u32[]{:S(2)}, u32[]{:S(2)}) collective-permute-start(bf16[80,1024]{1,0:T(8,128)(2,1)S(1)} %get-tuple-element.64), channel_id=1, source_target_pairs={{0,1},{1,2},{2,3},{3,4},{4,5},{5,6},{6,7},{7,0},{16,23},{17,16},{1... | collective-permute-start | bytes 491528 | tf_op jit(solution)/shard_map/ppermute | solution.py:48
  132.9 7.3 %collective-permute-start.26 = (bf16[80,1024]{1,0:T(8,128)(2,1)S(1)}, bf16[80,1024]{1,0:T(8,128)(2,1)S(1)}, u32[]{:S(2)}, u32[]{:S(2)}) collective-permute-start(bf16[80,1024]{1,0:T(8,128)(2,1)S(1)} %get-tuple-element.68), channel_id=1, source_target_pairs={{0,1},{1,2},{2,3},{3,4},{4,5},{5,6},{6,7},{7,0},{16,23},{17,16},{1... | collective-permute-start | bytes 491528 | tf_op jit(solution)/shard_map/ppermute | solution.py:48
  138.4 6.6 %collective-permute-start.23 = (bf16[80,1024]{1,0:T(8,128)(2,1)S(1)}, bf16[80,1024]{1,0:T(8,128)(2,1)S(1)}, u32[]{:S(2)}, u32[]{:S(2)}) collective-permute-start(bf16[80,1024]{1,0:T(8,128)(2,1)S(1)} %shard_map.38), channel_id=1, source_target_pairs={{0,1},{1,2},{2,3},{3,4},{4,5},{5,6},{6,7},{7,0},{16,23},{17,16},{1... | collective-permute-start | bytes 491528 | tf_op jit(solution)/shard_map/ppermute | solution.py:48
  140.2 6.6 %collective-permute-start.27 = (bf16[80,1024]{1,0:T(8,128)(2,1)S(1)}, bf16[80,1024]{1,0:T(8,128)(2,1)S(1)}, u32[]{:S(2)}, u32[]{:S(2)}) collective-permute-start(bf16[80,1024]{1,0:T(8,128)(2,1)S(1)} %shard_map.41), channel_id=1, source_target_pairs={{0,1},{1,2},{2,3},{3,4},{4,5},{5,6},{6,7},{7,0},{16,23},{17,16},{1... | collective-permute-start | bytes 491528 | tf_op jit(solution)/shard_map/ppermute | solution.py:48
  145.1 6.6 %collective-permute-start.24 = (bf16[80,1024]{1,0:T(8,128)(2,1)S(1)}, bf16[80,1024]{1,0:T(8,128)(2,1)S(1)}, u32[]{:S(2)}, u32[]{:S(2)}) collective-permute-start(bf16[80,1024]{1,0:T(8,128)(2,1)S(1)} %shard_map.39), channel_id=1, source_target_pairs={{0,1},{1,2},{2,3},{3,4},{4,5},{5,6},{6,7},{7,0},{16,23},{17,16},{1... | collective-permute-start | bytes 491528 | tf_op jit(solution)/shard_map/ppermute | solution.py:48
  146.9 6.6 %collective-permute-start.28 = (bf16[80,1024]{1,0:T(8,128)(2,1)S(1)}, bf16[80,1024]{1,0:T(8,128)(2,1)S(1)}, u32[]{:S(2)}, u32[]{:S(2)}) collective-permute-start(bf16[80,1024]{1,0:T(8,128)(2,1)S(1)} %shard_map.42), channel_id=1, source_target_pairs={{0,1},{1,2},{2,3},{3,4},{4,5},{5,6},{6,7},{7,0},{16,23},{17,16},{1... | collective-permute-start | bytes 491528 | tf_op jit(solution)/shard_map/ppermute | solution.py:48
  151.8 6.6 %collective-permute-start.25 = (bf16[80,1024]{1,0:T(8,128)(2,1)S(1)}, bf16[80,1024]{1,0:T(8,128)(2,1)S(1)}, u32[]{:S(2)}, u32[]{:S(2)}) collective-permute-start(bf16[80,1024]{1,0:T(8,128)(2,1)S(1)} %shard_map.40), channel_id=1, source_target_pairs={{0,1},{1,2},{2,3},{3,4},{4,5},{5,6},{6,7},{7,0},{16,23},{17,16},{1... | collective-permute-start | bytes 491528 | tf_op jit(solution)/shard_map/ppermute | solution.py:48
  (7 other events, 41.8 us)

commit v6 on v3

--- a/solution.py
+++ b/solution.py
@@ -11,6 +11,8 @@
 
 WIDTH = 1024
 ROWS = 1024
+PIECE = 64
+SENT = WIDTH + 128
 eps_factor = 0.3
 
 AXES = ("x", "yh", "core", "yl", "z")
@@ -56,14 +58,6 @@
 
 def put(whole, part, at):
     return lax.dynamic_update_index_in_dim(whole, part, at, 0)
-
-
-def pick(whole, at):
-    return lax.dynamic_index_in_dim(whole, at, 0, False)
-
-
-def added(a, b):
-    return (a.astype(jnp.float32) + b.astype(jnp.float32)).astype(jnp.bfloat16)
 
 
 def gather_z(part):
@@ -77,21 +71,6 @@
             left = shift_z(left, -1)
             whole = put(whole, left, jnp.bitwise_and(z + k, 7))
     return whole
-
-
-def scatter_z(parts):
-    z = lax.axis_index("z")
-
-    def own(offset):
-        return pick(parts, jnp.bitwise_and(z + offset, 7))
-
-    right, left = shift_z(own(4), 1), shift_z(own(5), -1)
-    for k in (3, 2, 1):
-        right = shift_z(added(right, own(k)), 1)
-        if k > 1:
-            left = shift_z(added(left, own(9 - k)), -1)
-    last = [a.astype(jnp.float32) for a in (right, left, own(0))]
-    return last[0] + last[1] + last[2]
 
 
 def to_lanes(square):
@@ -203,24 +182,74 @@
     send(out_ref, own_first(to_square(sums[0:1, :] + sums[1:2, :])))
 
 
-def targets_kernel(plan_ref, in_ref, data_ref, own_ref, other_ref, out_ref, weight_ref):
+def copies_kernel(data_ref, out_ref):
+    for k in range(16):
+        out_ref[k] = data_ref[...]
+
+
+def with_total(body, total):
+    high = total.astype(jnp.bfloat16).astype(jnp.float32)
+    first = lax.broadcasted_iota(jnp.int32, total.shape, 1) < 64
+    tail = jnp.where(first, high, total - high)
+    return jnp.concatenate([body.astype(jnp.bfloat16), tail.astype(jnp.bfloat16)], axis=1)
+
+
+def body_total(sent):
+    tail = sent[:, WIDTH:].astype(jnp.float32)
+    return sent[:, :WIDTH].astype(jnp.float32), tail + pltpu.roll(tail, 64, 1)
+
+
+def summed(a, b):
+    (body_a, total_a), (body_b, total_b) = body_total(a), body_total(b)
+    return with_total(body_a + body_b, total_a + total_b)
+
+
+def half_targets(weight_ref, data_ref, start, out_ref):
+    ones = jnp.ones((ROWS, 128), jnp.bfloat16)
+    for k in range(2):
+        weights = weight_ref[:, pl.ds(start + 256 * k, 256)]
+        found = [
+            lax.dot_general(weights, side, (((0,), (0,)), ((), ())), preferred_element_type=jnp.float32)
+            for side in (data_ref[...], ones)
+        ]
+        out_ref[pl.ds(256 * k, 256), :] = with_total(*found)
+
+
+def other_targets_kernel(plan_ref, in_ref, data_ref, weight_ref, out_ref):
     scale = 1.0 / jnp.sum(in_ref[...], axis=0)
-    sums = jnp.zeros((1, ROWS), jnp.float32)
     for k in range(8):
         part = pl.ds(128 * k, 128)
         weights = plan_ref[part, :].astype(jnp.float32) * down(scale[k : k + 1, :])
         weight_ref[part, :] = weights.astype(jnp.bfloat16)
-        sums = sums + jnp.sum(weights, axis=0, keepdims=True)
-    send(out_ref, own_first(to_square(sums)))
+    half_targets(weight_ref, data_ref, ROWS // 2, out_ref)
+
+
+def own_targets_kernel(weight_ref, data_ref, out_ref):
+    half_targets(weight_ref, data_ref, 0, out_ref)
+
+
+def piece(ref, offset):
+    at = jnp.bitwise_and(lax.axis_index("z") + offset, 7)
+    return ref[pl.ds(pl.multiple_of(at * PIECE, PIECE), PIECE), :]
+
+
+def cores_kernel(own_ref, got_ref, out_ref, right_ref, left_ref):
     for k in range(4):
-        partial = lax.dot_general(
-            weight_ref[:, pl.ds(256 * k, 256)],
-            data_ref[...],
-            (((0,), (0,)), ((), ())),
-            preferred_element_type=jnp.float32,
-        ).astype(jnp.bfloat16)
-        home = own_ref if k < 2 else other_ref
-        home[pl.ds(256 * (k % 2), 256), :] = partial
+        part = pl.ds(128 * k, 128)
+        out_ref[part, :] = summed(own_ref[part, :], got_ref[part, :])
+    right_ref[...] = piece(out_ref, 4)
+    left_ref[...] = piece(out_ref, 5)
+
+
+def pass_kernel(offset, own_ref, got_ref, out_ref):
+    out_ref[...] = summed(piece(own_ref, offset), got_ref[...])
+
+
+def velocity_kernel(own_ref, right_ref, left_ref, noise_ref, out_ref):
+    found = [body_total(a) for a in (piece(own_ref, 0), right_ref[...], left_ref[...])]
+    body, total = (sum(values) for values in zip(*found))
+    target = body / total[:, :1]
+    out_ref[...] = (target - noise_ref[...].astype(jnp.float32)).astype(jnp.bfloat16)
 
 
 SQUARE = jax.ShapeDtypeStruct((8, 128), jnp.float32)
@@ -247,18 +276,24 @@
     return pltpu.with_memory_space_constraint(a, pltpu.VMEM)
 
 
+def sent_rows(count):
+    return pltpu.VMEM((count, SENT), jnp.bfloat16)
+
+
 def per_device(noise_latents, data_latents):
-    piece = noise_latents.shape[0]
-    core, z = lax.axis_index("core"), lax.axis_index("z")
-
-    columns = spread(
-        jnp.broadcast_to(data_latents[None], (16,) + data_latents.shape), COL_GROUP
-    ).reshape(ROWS, WIDTH)
-    own_rows = gather_z(noise_latents).reshape(ROWS // 2, WIDTH)
-    other_rows = swap_core(own_rows)
+    copies = run(copies_kernel, pltpu.VMEM((16, PIECE, WIDTH), jnp.bfloat16), data_latents)
+    copies, noise = lax.optimization_barrier((copies, noise_latents))
+    columns = keep(spread(copies, COL_GROUP).reshape(ROWS, WIDTH))
+    own_rows = gather_z(noise).reshape(ROWS // 2, WIDTH)
+    other_rows = keep(swap_core(own_rows))
 
     scores, parts = run(
-        scores_kernel, (in_vmem(ROWS, jnp.float32), COPIES), columns, own_rows, other_rows
+        scores_kernel,
+        (in_vmem(ROWS, jnp.float32), COPIES),
+        columns,
+        keep(own_rows),
+        other_rows,
+        flops=2 * ROWS * ROWS * WIDTH,
     )
     scores = keep(scores)
     row_dual, parts = run(columns_kernel, (SQUARE, COPIES), scores, spread(parts, ROW_GROUP))
@@ -273,21 +308,38 @@
     parts = run(column_sums_kernel, COPIES, plan, spread(parts, ROW_GROUP))
     parts = run(row_sums_kernel, COPIES, plan, spread(parts, COL_GROUP))
     parts = run(column_sums_kernel, COPIES, plan, spread(parts, ROW_GROUP))
-    half = jax.ShapeDtypeStruct((ROWS // 2, WIDTH), jnp.bfloat16)
-    own_half, other_half, parts = run(
-        targets_kernel,
-        (half, half, COPIES),
+    weights, others = run(
+        other_targets_kernel,
+        (in_vmem(ROWS, jnp.bfloat16), sent_rows(ROWS // 2)),
         plan,
         spread(parts, COL_GROUP),
         columns,
-        scratch=[pltpu.VMEM((ROWS, ROWS), jnp.bfloat16)],
-    )
-    row_total = jnp.sum(spread(parts, ROW_GROUP), axis=0).reshape(16, piece)
-
-    own_half = added(own_half, swap_core(other_half)).reshape(8, piece, WIDTH)
-    summed_up = scatter_z(own_half)
-    target = summed_up / pick(row_total, core * 8 + z)[:, None]
-    return (target - noise_latents.astype(jnp.float32)).astype(jnp.bfloat16)
+        flops=ROWS * ROWS * WIDTH,
+    )
+    got = swap_core(others)
+    own = run(
+        own_targets_kernel,
+        sent_rows(ROWS // 2),
+        keep(weights),
+        columns,
+        flops=ROWS * ROWS * WIDTH,
+    )
+    own, right, left = run(
+        cores_kernel,
+        (sent_rows(ROWS // 2), sent_rows(PIECE), sent_rows(PIECE)),
+        keep(own),
+        keep(got),
+    )
+    own = keep(own)
+    right, left = shift_z(right, 1), shift_z(left, -1)
+    for k in (3, 2, 1):
+        passing = functools.partial(pass_kernel, k)
+        right = shift_z(run(passing, sent_rows(PIECE), own, keep(right)), 1)
+        if k > 1:
+            passing = functools.partial(pass_kernel, 9 - k)
+            left = shift_z(run(passing, sent_rows(PIECE), own, keep(left)), -1)
+    velocity = jax.ShapeDtypeStruct((PIECE, WIDTH), jnp.bfloat16)
+    return run(velocity_kernel, velocity, own, keep(right), keep(left), noise_latents)
 
 
 def solution(mesh):

time: 159 us -> 152 us (0.956); the launches traced: 157 us -> 152 us
  starting transfers between devices: 33.6 us -> 30.6 us
  Pallas kernels: 11.1 us -> 13.1 us
    ppermute x14, waiting for transfers between devices: 22 us -> 30.8 us  [shift_z(): lax.ppermute(a, AXES, device_pairs(lambda x, yh, c, yl, z: (x, yh, c, yl,...]
    all_to_all x2 -> x1, waiting for transfers between devices: 8.88 us -> 1.1 us  [spread(): return lax.all_to_all(copies, group, 0, 0)]
    all_to_all x2 -> x1, starting transfers between devices: 11.1 us -> 7.48 us  [spread(): return lax.all_to_all(copies, group, 0, 0)]
    broadcast_in_dim x1 -> x0, local copies, waits for them, and re-layouts: 2.5 us -> none  [per_device(): jnp.broadcast_to(data_latents[None], (16,) + data_latents.shape)]
    unnamed x6 -> x10, local copies, waits for them, and re-layouts: 2.22 us -> 4.45 us
    pallas_call x7 -> x16, Pallas kernels: 11.1 us -> 13.1 us  [run(): pl.pallas_call(kernel, out_shape=outs, in_specs=[pl.BlockSpec(memory_spac...]
    ppermute x2, waiting for transfers between devices: 5.51 us -> 3.91 us  [swap_core(): lax.ppermute(a, AXES, device_pairs(lambda x, yh, c, yl, z: (x, yh, 1 - c,...]
  transfers between devices with their start and end apart: 18 -> 17, of which waited for: 10 -> 10; matrix products, arithmetic and copies ran while one was open for 2% -> 0% of each run, Pallas kernels for 0% -> 1%
where the time goes in v6:
time: 152 us
  blocking collectives  67.7 us (45%)
  waiting for transfers between devices  35.8 us (24%)
  starting transfers between devices  30.6 us (20%)
  Pallas kernels  13.1 us (9%)
  local copies, waits for them, and re-layouts  4.68 us (3%)
    all_to_all x6, blocking collectives, spread(): return lax.all_to_all(copies, group, 0, 0)  67.7 us
    ppermute x14, waiting for transfers between devices, shift_z(): lax.ppermute(a, AXES, device_pairs(lambda x, yh, c, yl, z: (x, yh, c, yl,...  30.8 us
    ppermute x14, starting transfers between devices, shift_z(): lax.ppermute(a, AXES, device_pairs(lambda x, yh, c, yl, z: (x, yh, c, yl,...  23 us
    pallas_call x16, Pallas kernels, run(): pl.pallas_call(kernel, out_shape=outs, in_specs=[pl.BlockSpec(memory_spac...  13.1 us
    all_to_all x1, starting transfers between devices, spread(): return lax.all_to_all(copies, group, 0, 0)  7.48 us
    unnamed x10, local copies, waits for them, and re-layouts  4.45 us
    ppermute x2, waiting for transfers between devices, swap_core(): lax.ppermute(a, AXES, device_pairs(lambda x, yh, c, yl, z: (x, yh, 1 - c,...  3.91 us
  transfers between devices with their start and end apart: 17, of which 10 were waited for; matrix products, arithmetic and copies ran while one was open for 0% of the time, Pallas kernels for 1%

profile of v6, /device:TPU:2, one launch (start us, length us, event | category | flops | bytes accessed | tf_op | source)
XLA Modules:
  0.0 152.1 jit_solution(2517811186257661564)
XLA Ops:
  2.4 5.9 %collective-permute-start.1 = (bf16[64,1024]{1,0:T(8,128)(2,1)S(1)}, bf16[64,1024]{1,0:T(8,128)(2,1)S(1)}, u32[]{:S(2)}, u32[]{:S(2)}) collective-permute-start(bf16[64,1024]{1,0:T(8,128)(2,1)S(1)} %copy-done.1), channel_id=1, source_target_pairs={{0,7},{1,0},{2,1},{3,2},{4,3},{5,4},{6,5},{7,6},{8,15},{9,8},{10,9... | collective-permute-start | bytes 393224 | tf_op jit(solution)/shard_map/ppermute | solution.py:48
  8.2 7.5 %all-to-all-start = ((bf16[16,64,1024]{2,1,0:T(8,128)(2,1)}), bf16[16,64,1024]{2,1,0:T(8,128)(2,1)S(1)}, u32[]{:S(2)}, u32[]{:S(2)}) async-start(bf16[16,64,1024]{2,1,0:T(8,128)(2,1)} %copy-done), calls=%async_computation | async-start | bytes 4194304 | tf_op jit(solution)/shard_map/all_to_all | solution.py:56
  15.9 3.3 %collective-permute-start.3 = (bf16[64,1024]{1,0:T(8,128)(2,1)S(1)}, bf16[64,1024]{1,0:T(8,128)(2,1)S(1)}, u32[]{:S(2)}, u32[]{:S(2)}) collective-permute-start(bf16[64,1024]{1,0:T(8,128)(2,1)S(1)} %collective-permute-done.1), channel_id=1, source_target_pairs={{0,7},{1,0},{2,1},{3,2},{4,3},{5,4},{6,5},{7,6},{8,15},{9,8},{10,9... | collective-permute-start | bytes 393224 | tf_op jit(solution)/shard_map/ppermute | solution.py:48
  19.2 2.5 %collective-permute-done.3 = bf16[64,1024]{1,0:T(8,128)(2,1)S(1)} collective-permute-done((bf16[64,1024]{1,0:T(8,128)(2,1)S(1)}, bf16[64,1024]{1,0:T(8,128)(2,1)S(1)}, u32[]{:S(2)}, u32[]{:S(2)}) %collective-permute-start.3) | collective-permute-done | bytes 131104 | tf_op jit(solution)/shard_map/ppermute | solution.py:48
  21.7 3.7 %collective-permute-start.5 = (bf16[64,1024]{1,0:T(8,128)(2,1)S(1)}, bf16[64,1024]{1,0:T(8,128)(2,1)S(1)}, u32[]{:S(2)}, u32[]{:S(2)}) collective-permute-start(bf16[64,1024]{1,0:T(8,128)(2,1)S(1)} %collective-permute-done.3), channel_id=1, source_target_pairs={{0,7},{1,0},{2,1},{3,2},{4,3},{5,4},{6,5},{7,6},{8,15},{9,8},{10,9... | collective-permute-start | bytes 393224 | tf_op jit(solution)/shard_map/ppermute | solution.py:48
  25.4 6.1 %collective-permute-done.4 = bf16[64,1024]{1,0:T(8,128)(2,1)S(1)} collective-permute-done((bf16[64,1024]{1,0:T(8,128)(2,1)S(1)}, bf16[64,1024]{1,0:T(8,128)(2,1)S(1)}, u32[]{:S(2)}, u32[]{:S(2)}) %collective-permute-start.4) | collective-permute-done | bytes 131104 | tf_op jit(solution)/shard_map/ppermute | solution.py:48
  31.6 6.1 %collective-permute-done.6 = bf16[64,1024]{1,0:T(8,128)(2,1)S(1)} collective-permute-done((bf16[64,1024]{1,0:T(8,128)(2,1)S(1)}, bf16[64,1024]{1,0:T(8,128)(2,1)S(1)}, u32[]{:S(2)}, u32[]{:S(2)}) %collective-permute-start.6) | collective-permute-done | bytes 131104 | tf_op jit(solution)/shard_map/ppermute | solution.py:48
  37.8 2.6 %collective-permute-done.7.other_ref = bf16[512,1024]{1,0:T(8,128)(2,1)S(1)} collective-permute-done((bf16[512,1024]{1,0:T(8,128)(2,1)S(1)}, bf16[512,1024]{1,0:T(8,128)(2,1)S(1)}, u32[]{:S(2)}, u32[]{:S(2)}) %collective-permute-start.7) | collective-permute-done | bytes 1048608 | tf_op jit(solution)/shard_map/ppermute | solution.py:52
  43.8 3.4 %shard_map.29 = (f32[1024,1024]{1,0:T(8,128)S(1)}, f32[16,8,128]{2,1,0:T(8,128)S(1)}) custom-call(bf16[1024,1024]{1,0:T(8,128)(2,1)S(1)} %bitcast.18, bf16[512,1024]{1,0:T(8,128)(2,1)S(1)} %bitcast.22, bf16[512,1024]{1,0:T(8,128)(2,1)S(1)} %copy-done.4), custom_call_target="tpu_custom_call" | custom-call | flops 2147483648 | bytes 4194304 | tf_op jit(solution)/shard_map/pallas_call | solution.py:264
  47.2 12.2 %all_to_all.35.in_ref = f32[16,8,128]{2,1,0:T(8,128)S(1)} all-to-all(f32[16,8,128]{2,1,0:T(8,128)S(1)} %get-tuple-element.21), channel_id=1, replica_groups=mesh['x'=4,'yh'=2,'core'=2,'yl'=2,'z'=8] {'core','z'}, dimensions={0} | all-to-all | bytes 131072 | tf_op jit(solution)/shard_map/all_to_all | solution.py:56
  60.5 12.7 %all_to_all.36.in_ref = f32[16,8,128]{2,1,0:T(8,128)S(1)} all-to-all(f32[16,8,128]{2,1,0:T(8,128)S(1)} %get-tuple-element.23), channel_id=1, replica_groups=mesh['x'=4,'yh'=2,'core'=2,'yl'=2,'z'=8] {'x','yh','yl'}, dimensions={0} | all-to-all | bytes 131072 | tf_op jit(solution)/shard_map/all_to_all | solution.py:56
  74.2 10.5 %all_to_all.37.in_ref = f32[16,8,128]{2,1,0:T(8,128)S(1)} all-to-all(f32[16,8,128]{2,1,0:T(8,128)S(1)} %get-tuple-element.25), channel_id=1, replica_groups=mesh['x'=4,'yh'=2,'core'=2,'yl'=2,'z'=8] {'core','z'}, dimensions={0} | all-to-all | bytes 131072 | tf_op jit(solution)/shard_map/all_to_all | solution.py:56
  85.3 10.9 %all_to_all.38.in_ref = f32[16,8,128]{2,1,0:T(8,128)S(1)} all-to-all(f32[16,8,128]{2,1,0:T(8,128)S(1)} %shard_map.32), channel_id=1, replica_groups=mesh['x'=4,'yh'=2,'core'=2,'yl'=2,'z'=8] {'x','yh','yl'}, dimensions={0} | all-to-all | bytes 131072 | tf_op jit(solution)/shard_map/all_to_all | solution.py:56
  96.6 10.5 %all_to_all.39.in_ref = f32[16,8,128]{2,1,0:T(8,128)S(1)} all-to-all(f32[16,8,128]{2,1,0:T(8,128)S(1)} %shard_map.33), channel_id=1, replica_groups=mesh['x'=4,'yh'=2,'core'=2,'yl'=2,'z'=8] {'core','z'}, dimensions={0} | all-to-all | bytes 131072 | tf_op jit(solution)/shard_map/all_to_all | solution.py:56
  107.8 10.9 %all_to_all.40.in_ref = f32[16,8,128]{2,1,0:T(8,128)S(1)} all-to-all(f32[16,8,128]{2,1,0:T(8,128)S(1)} %shard_map.34), channel_id=1, replica_groups=mesh['x'=4,'yh'=2,'core'=2,'yl'=2,'z'=8] {'x','yh','yl'}, dimensions={0} | all-to-all | bytes 131072 | tf_op jit(solution)/shard_map/all_to_all | solution.py:56
  118.7 2.2 %shard_map.35 = (bf16[1024,1024]{1,0:T(8,128)(2,1)S(1)}, bf16[512,1152]{1,0:T(8,128)(2,1)S(1)}) custom-call(bf16[1024,1024]{1,0:T(8,128)(2,1)S(1)} %get-tuple-element.24.plan_ref, f32[16,8,128]{2,1,0:T(8,128)S(1)} %all_to_all.40.in_ref, bf16[1024,1024]{1,0:T(8,128)(2,1)S(1)} %bitcast.19), custom_call_target="tpu_custom_call" | custom-call | flops 1073741824 | bytes 4194304 | tf_op jit(solution)/shard_map/pallas_call | solution.py:264
  121.0 1.6 %shard_map.36.own_ref = bf16[512,1152]{1,0:T(8,128)(2,1)S(1)} custom-call(bf16[1024,1024]{1,0:T(8,128)(2,1)S(1)} %get-tuple-element.26.weight_ref, bf16[1024,1024]{1,0:T(8,128)(2,1)S(1)} %bitcast.20), custom_call_target="tpu_custom_call" | custom-call | flops 1073741824 | bytes 4194304 | tf_op jit(solution)/shard_map/pallas_call | solution.py:264
  125.4 2.3 %collective-permute-start.13 = (bf16[64,1152]{1,0:T(8,128)(2,1)S(1)}, bf16[64,1152]{1,0:T(8,128)(2,1)S(1)}, u32[]{:S(2)}, u32[]{:S(2)}) collective-permute-start(bf16[64,1152]{1,0:T(8,128)(2,1)S(1)} %get-tuple-element.30), channel_id=1, source_target_pairs={{0,7},{1,0},{2,1},{3,2},{4,3},{5,4},{6,5},{7,6},{8,15},{9,8},{10,9... | collective-permute-start | bytes 442376 | tf_op jit(solution)/shard_map/ppermute | solution.py:48
  127.7 3.9 %collective-permute-done.9.got_ref = bf16[64,1152]{1,0:T(8,128)(2,1)S(1)} collective-permute-done((bf16[64,1152]{1,0:T(8,128)(2,1)S(1)}, bf16[64,1152]{1,0:T(8,128)(2,1)S(1)}, u32[]{:S(2)}, u32[]{:S(2)}) %collective-permute-start.9) | collective-permute-done | bytes 147488 | tf_op jit(solution)/shard_map/ppermute | solution.py:48
  131.9 3.3 %collective-permute-start.14 = (bf16[64,1152]{1,0:T(8,128)(2,1)S(1)}, bf16[64,1152]{1,0:T(8,128)(2,1)S(1)}, u32[]{:S(2)}, u32[]{:S(2)}) collective-permute-start(bf16[64,1152]{1,0:T(8,128)(2,1)S(1)} %shard_map.41), channel_id=1, source_target_pairs={{0,7},{1,0},{2,1},{3,2},{4,3},{5,4},{6,5},{7,6},{8,15},{9,8},{10,9... | collective-permute-start | bytes 442376 | tf_op jit(solution)/shard_map/ppermute | solution.py:48
  135.2 2.9 %collective-permute-done.10.got_ref = bf16[64,1152]{1,0:T(8,128)(2,1)S(1)} collective-permute-done((bf16[64,1152]{1,0:T(8,128)(2,1)S(1)}, bf16[64,1152]{1,0:T(8,128)(2,1)S(1)}, u32[]{:S(2)}, u32[]{:S(2)}) %collective-permute-start.10) | collective-permute-done | bytes 147488 | tf_op jit(solution)/shard_map/ppermute | solution.py:48
  138.5 3.3 %collective-permute-start.15 = (bf16[64,1152]{1,0:T(8,128)(2,1)S(1)}, bf16[64,1152]{1,0:T(8,128)(2,1)S(1)}, u32[]{:S(2)}, u32[]{:S(2)}) collective-permute-start(bf16[64,1152]{1,0:T(8,128)(2,1)S(1)} %shard_map.42), channel_id=1, source_target_pairs={{0,7},{1,0},{2,1},{3,2},{4,3},{5,4},{6,5},{7,6},{8,15},{9,8},{10,9... | collective-permute-start | bytes 442376 | tf_op jit(solution)/shard_map/ppermute | solution.py:48
  141.8 2.9 %collective-permute-done.11.got_ref = bf16[64,1152]{1,0:T(8,128)(2,1)S(1)} collective-permute-done((bf16[64,1152]{1,0:T(8,128)(2,1)S(1)}, bf16[64,1152]{1,0:T(8,128)(2,1)S(1)}, u32[]{:S(2)}, u32[]{:S(2)}) %collective-permute-start.11) | collective-permute-done | bytes 147488 | tf_op jit(solution)/shard_map/ppermute | solution.py:48
  144.9 6.3 %collective-permute-done.12.right_ref = bf16[64,1152]{1,0:T(8,128)(2,1)S(1)} collective-permute-done((bf16[64,1152]{1,0:T(8,128)(2,1)S(1)}, bf16[64,1152]{1,0:T(8,128)(2,1)S(1)}, u32[]{:S(2)}, u32[]{:S(2)}) %collective-permute-start.12) | collective-permute-done | bytes 147488 | tf_op jit(solution)/shard_map/ppermute | solution.py:48
  (51 shorter events, 14.5 us)
Async XLA Ops:
  0.0 0.9 copy-start.2
  0.9 1.5 copy-start.1
  1.0 1.3 copy-start
  2.4 13.5 %collective-permute-start.1 = (bf16[64,1024]{1,0:T(8,128)(2,1)S(1)}, bf16[64,1024]{1,0:T(8,128)(2,1)S(1)}, u32[]{:S(2)}, u32[]{:S(2)}) collective-permute-start(bf16[64,1024]{1,0:T(8,128)(2,1)S(1)} %copy-done.1), channel_id=1, source_target_pairs={{0,7},{1,0},{2,1},{3,2},{4,3},{5,4},{6,5},{7,6},{8,15},{9,8},{10,9... | collective-permute-start | bytes 393224 | tf_op jit(solution)/shard_map/ppermute | solution.py:48
  8.2 11.0 %collective-permute-start = (bf16[64,1024]{1,0:T(8,128)(2,1)S(1)}, bf16[64,1024]{1,0:T(8,128)(2,1)S(1)}, u32[]{:S(2)}, u32[]{:S(2)}) collective-permute-start(bf16[64,1024]{1,0:T(8,128)(2,1)S(1)} %copy-done.1), channel_id=1, source_target_pairs={{0,1},{1,2},{2,3},{3,4},{4,5},{5,6},{6,7},{7,0},{8,9},{9,10},{10,1... | collective-permute-start | bytes 393224 | tf_op jit(solution)/shard_map/ppermute | solution.py:48
  8.2 34.4 %all-to-all-start = ((bf16[16,64,1024]{2,1,0:T(8,128)(2,1)}), bf16[16,64,1024]{2,1,0:T(8,128)(2,1)S(1)}, u32[]{:S(2)}, u32[]{:S(2)}) async-start(bf16[16,64,1024]{2,1,0:T(8,128)(2,1)} %copy-done), calls=%async_computation | async-start | bytes 4194304 | tf_op jit(solution)/shard_map/all_to_all | solution.py:56
  15.9 5.8 %collective-permute-start.3 = (bf16[64,1024]{1,0:T(8,128)(2,1)S(1)}, bf16[64,1024]{1,0:T(8,128)(2,1)S(1)}, u32[]{:S(2)}, u32[]{:S(2)}) collective-permute-start(bf16[64,1024]{1,0:T(8,128)(2,1)S(1)} %collective-permute-done.1), channel_id=1, source_target_pairs={{0,7},{1,0},{2,1},{3,2},{4,3},{5,4},{6,5},{7,6},{8,15},{9,8},{10,9... | collective-permute-start | bytes 393224 | tf_op jit(solution)/shard_map/ppermute | solution.py:48
  19.2 6.2 %collective-permute-start.2 = (bf16[64,1024]{1,0:T(8,128)(2,1)S(1)}, bf16[64,1024]{1,0:T(8,128)(2,1)S(1)}, u32[]{:S(2)}, u32[]{:S(2)}) collective-permute-start(bf16[64,1024]{1,0:T(8,128)(2,1)S(1)} %collective-permute-done), channel_id=1, source_target_pairs={{0,1},{1,2},{2,3},{3,4},{4,5},{5,6},{6,7},{7,0},{8,9},{9,10},{10,1... | collective-permute-start | bytes 393224 | tf_op jit(solution)/shard_map/ppermute | solution.py:48
  21.7 9.9 %collective-permute-start.5 = (bf16[64,1024]{1,0:T(8,128)(2,1)S(1)}, bf16[64,1024]{1,0:T(8,128)(2,1)S(1)}, u32[]{:S(2)}, u32[]{:S(2)}) collective-permute-start(bf16[64,1024]{1,0:T(8,128)(2,1)S(1)} %collective-permute-done.3), channel_id=1, source_target_pairs={{0,7},{1,0},{2,1},{3,2},{4,3},{5,4},{6,5},{7,6},{8,15},{9,8},{10,9... | collective-permute-start | bytes 393224 | tf_op jit(solution)/shard_map/ppermute | solution.py:48
  25.4 6.2 %collective-permute-start.4 = (bf16[64,1024]{1,0:T(8,128)(2,1)S(1)}, bf16[64,1024]{1,0:T(8,128)(2,1)S(1)}, u32[]{:S(2)}, u32[]{:S(2)}) collective-permute-start(bf16[64,1024]{1,0:T(8,128)(2,1)S(1)} %collective-permute-done.2), channel_id=1, source_target_pairs={{0,1},{1,2},{2,3},{3,4},{4,5},{5,6},{6,7},{7,0},{8,9},{9,10},{10,1... | collective-permute-start | bytes 393224 | tf_op jit(solution)/shard_map/ppermute | solution.py:48
  31.5 6.2 %collective-permute-start.6 = (bf16[64,1024]{1,0:T(8,128)(2,1)S(1)}, bf16[64,1024]{1,0:T(8,128)(2,1)S(1)}, u32[]{:S(2)}, u32[]{:S(2)}) collective-permute-start(bf16[64,1024]{1,0:T(8,128)(2,1)S(1)} %collective-permute-done.4), channel_id=1, source_target_pairs={{0,1},{1,2},{2,3},{3,4},{4,5},{5,6},{6,7},{7,0},{8,9},{9,10},{10,1... | collective-permute-start | bytes 393224 | tf_op jit(solution)/shard_map/ppermute | solution.py:48
  37.7 2.7 %collective-permute-start.7 = (bf16[512,1024]{1,0:T(8,128)(2,1)S(1)}, bf16[512,1024]{1,0:T(8,128)(2,1)S(1)}, u32[]{:S(2)}, u32[]{:S(2)}) collective-permute-start(bf16[512,1024]{1,0:T(8,128)(2,1)S(1)} %bitcast.21), channel_id=1, source_target_pairs={{0,16},{1,17},{2,18},{3,19},{4,20},{5,21},{6,22},{7,23},{8,24},{9,... | collective-permute-start | bytes 3145736 | tf_op jit(solution)/shard_map/ppermute | solution.py:52
  40.5 1.0 copy-start.3
  42.6 1.2 copy-start.4
  120.9 2.9 %collective-permute-start.8 = (bf16[512,1152]{1,0:T(8,128)(2,1)S(1)}, bf16[512,1152]{1,0:T(8,128)(2,1)S(1)}, u32[]{:S(2)}, u32[]{:S(2)}) collective-permute-start(bf16[512,1152]{1,0:T(8,128)(2,1)S(1)} %get-tuple-element.27), channel_id=1, source_target_pairs={{0,16},{1,17},{2,18},{3,19},{4,20},{5,21},{6,22},{7,23},{8,24},{9,... | collective-permute-start | bytes 3538952 | tf_op jit(solution)/shard_map/ppermute | solution.py:52
  124.4 7.2 %collective-permute-start.9 = (bf16[64,1152]{1,0:T(8,128)(2,1)S(1)}, bf16[64,1152]{1,0:T(8,128)(2,1)S(1)}, u32[]{:S(2)}, u32[]{:S(2)}) collective-permute-start(bf16[64,1152]{1,0:T(8,128)(2,1)S(1)} %get-tuple-element.29), channel_id=1, source_target_pairs={{0,1},{1,2},{2,3},{3,4},{4,5},{5,6},{6,7},{7,0},{8,9},{9,10},{10,1... | collective-permute-start | bytes 442376 | tf_op jit(solution)/shard_map/ppermute | solution.py:48
  125.4 6.4 %collective-permute-start.13 = (bf16[64,1152]{1,0:T(8,128)(2,1)S(1)}, bf16[64,1152]{1,0:T(8,128)(2,1)S(1)}, u32[]{:S(2)}, u32[]{:S(2)}) collective-permute-start(bf16[64,1152]{1,0:T(8,128)(2,1)S(1)} %get-tuple-element.30), channel_id=1, source_target_pairs={{0,7},{1,0},{2,1},{3,2},{4,3},{5,4},{6,5},{7,6},{8,15},{9,8},{10,9... | collective-permute-start | bytes 442376 | tf_op jit(solution)/shard_map/ppermute | solution.py:48
  131.7 6.4 %collective-permute-start.10 = (bf16[64,1152]{1,0:T(8,128)(2,1)S(1)}, bf16[64,1152]{1,0:T(8,128)(2,1)S(1)}, u32[]{:S(2)}, u32[]{:S(2)}) collective-permute-start(bf16[64,1152]{1,0:T(8,128)(2,1)S(1)} %shard_map.38), channel_id=1, source_target_pairs={{0,1},{1,2},{2,3},{3,4},{4,5},{5,6},{6,7},{7,0},{8,9},{9,10},{10,1... | collective-permute-start | bytes 442376 | tf_op jit(solution)/shard_map/ppermute | solution.py:48
  131.9 6.4 %collective-permute-start.14 = (bf16[64,1152]{1,0:T(8,128)(2,1)S(1)}, bf16[64,1152]{1,0:T(8,128)(2,1)S(1)}, u32[]{:S(2)}, u32[]{:S(2)}) collective-permute-start(bf16[64,1152]{1,0:T(8,128)(2,1)S(1)} %shard_map.41), channel_id=1, source_target_pairs={{0,7},{1,0},{2,1},{3,2},{4,3},{5,4},{6,5},{7,6},{8,15},{9,8},{10,9... | collective-permute-start | bytes 442376 | tf_op jit(solution)/shard_map/ppermute | solution.py:48
  138.3 6.4 %collective-permute-start.11 = (bf16[64,1152]{1,0:T(8,128)(2,1)S(1)}, bf16[64,1152]{1,0:T(8,128)(2,1)S(1)}, u32[]{:S(2)}, u32[]{:S(2)}) collective-permute-start(bf16[64,1152]{1,0:T(8,128)(2,1)S(1)} %shard_map.39), channel_id=1, source_target_pairs={{0,1},{1,2},{2,3},{3,4},{4,5},{5,6},{6,7},{7,0},{8,9},{9,10},{10,1... | collective-permute-start | bytes 442376 | tf_op jit(solution)/shard_map/ppermute | solution.py:48
  138.5 6.4 %collective-permute-start.15 = (bf16[64,1152]{1,0:T(8,128)(2,1)S(1)}, bf16[64,1152]{1,0:T(8,128)(2,1)S(1)}, u32[]{:S(2)}, u32[]{:S(2)}) collective-permute-start(bf16[64,1152]{1,0:T(8,128)(2,1)S(1)} %shard_map.42), channel_id=1, source_target_pairs={{0,7},{1,0},{2,1},{3,2},{4,3},{5,4},{6,5},{7,6},{8,15},{9,8},{10,9... | collective-permute-start | bytes 442376 | tf_op jit(solution)/shard_map/ppermute | solution.py:48
  144.8 6.4 %collective-permute-start.12 = (bf16[64,1152]{1,0:T(8,128)(2,1)S(1)}, bf16[64,1152]{1,0:T(8,128)(2,1)S(1)}, u32[]{:S(2)}, u32[]{:S(2)}) collective-permute-start(bf16[64,1152]{1,0:T(8,128)(2,1)S(1)} %shard_map.40), channel_id=1, source_target_pairs={{0,1},{1,2},{2,3},{3,4},{4,5},{5,6},{6,7},{7,0},{8,9},{9,10},{10,1... | collective-permute-start | bytes 442376 | tf_op jit(solution)/shard_map/ppermute | solution.py:48

commit v7 on v6

--- a/solution.py
+++ b/solution.py
@@ -64,13 +64,13 @@
     z = lax.axis_index("z")
     whole = put(jnp.zeros((8,) + part.shape, part.dtype), part, z)
     right = left = part
-    for k in (1, 2, 3, 4):
-        right = shift_z(right, 1)
+    for k in (1, 2, 3):
+        if k == 3:
+            halves = shift_z(right[: PIECE // 2], 2), shift_z(left[PIECE // 2 :], -2)
+        right, left = shift_z(right, 1), shift_z(left, -1)
         whole = put(whole, right, jnp.bitwise_and(z - k, 7))
-        if k < 4:
-            left = shift_z(left, -1)
-            whole = put(whole, left, jnp.bitwise_and(z + k, 7))
-    return whole
+        whole = put(whole, left, jnp.bitwise_and(z + k, 7))
+    return put(whole, jnp.concatenate(halves, axis=0), jnp.bitwise_and(z + 4, 7))
 
 
 def to_lanes(square):
@@ -116,13 +116,17 @@
     return jnp.sum(wide * wide, axis=1, keepdims=True)
 
 
-def scores_kernel(data_ref, own_ref, other_ref, score_ref, out_ref):
+def scores_kernel(data_ref, own_ref, far_ref, score_ref, out_ref, other_ref, sem):
     scale = LOG2E / EPSILON
+    load = pltpu.make_async_copy(far_ref, other_ref, sem)
+    load.start()
     data_norms = jnp.concatenate(
         [square_sums(data_ref[pl.ds(128 * k, 128), :]) for k in range(8)], axis=0
     )
     rows = []
     for k in range(4):
+        if k == 2:
+            load.wait()
         source = own_ref if k < 2 else other_ref
         noise = source[pl.ds(256 * (k % 2), 256), :]
         noise_norms = jnp.concatenate(
@@ -182,9 +186,12 @@
     send(out_ref, own_first(to_square(sums[0:1, :] + sums[1:2, :])))
 
 
-def copies_kernel(data_ref, out_ref):
-    for k in range(16):
-        out_ref[k] = data_ref[...]
+def copies_kernel(data_ref, out_ref, sems):
+    writes = [pltpu.make_async_copy(data_ref, out_ref.at[k], sems.at[k]) for k in range(16)]
+    for write in writes:
+        write.start()
+    for write in writes:
+        write.wait()
 
 
 def with_total(body, total):
@@ -233,12 +240,22 @@
     return ref[pl.ds(pl.multiple_of(at * PIECE, PIECE), PIECE), :]
 
 
-def cores_kernel(own_ref, got_ref, out_ref, right_ref, left_ref):
+def cores_kernel(own_ref, got_ref, out_ref, right_ref, left_ref, right2_ref, left2_ref):
     for k in range(4):
         part = pl.ds(128 * k, 128)
         out_ref[part, :] = summed(own_ref[part, :], got_ref[part, :])
-    right_ref[...] = piece(out_ref, 4)
+    right_ref[...] = piece(out_ref, 3)
     left_ref[...] = piece(out_ref, 5)
+    far = piece(out_ref, 4)
+    right2_ref[...] = far[: PIECE // 2]
+    left2_ref[...] = far[PIECE // 2 :]
+
+
+def join_kernel(offset, start, own_ref, got_ref, far_ref, out_ref):
+    found = summed(piece(own_ref, offset), got_ref[...])
+    halves = [found[: PIECE // 2], found[PIECE // 2 :]]
+    halves[start] = summed(halves[start], far_ref[...])
+    out_ref[...] = jnp.concatenate(halves, axis=0)
 
 
 def pass_kernel(offset, own_ref, got_ref, out_ref):
@@ -260,12 +277,13 @@
     return pltpu.VMEM((rows, 1024), dtype)
 
 
-def run(kernel, outs, *args, flops=0, scratch=()):
+def run(kernel, outs, *args, flops=0, scratch=(), out_space=pltpu.VMEM, in_hbm=()):
+    spaces = [pltpu.HBM if k in in_hbm else pltpu.VMEM for k in range(len(args))]
     return pl.pallas_call(
         kernel,
         out_shape=outs,
-        in_specs=[pl.BlockSpec(memory_space=pltpu.VMEM)] * len(args),
-        out_specs=jax.tree.map(lambda _: pl.BlockSpec(memory_space=pltpu.VMEM), outs),
+        in_specs=[pl.BlockSpec(memory_space=space) for space in spaces],
+        out_specs=jax.tree.map(lambda _: pl.BlockSpec(memory_space=out_space), outs),
         scratch_shapes=scratch,
         compiler_params=pltpu.CompilerParams(vmem_limit_bytes=40 * 1024 * 1024),
         cost_estimate=pl.CostEstimate(flops=flops, bytes_accessed=4 << 20, transcendentals=0),
@@ -281,11 +299,17 @@
 
 
 def per_device(noise_latents, data_latents):
-    copies = run(copies_kernel, pltpu.VMEM((16, PIECE, WIDTH), jnp.bfloat16), data_latents)
+    copies = run(
+        copies_kernel,
+        pltpu.HBM((16, PIECE, WIDTH), jnp.bfloat16),
+        data_latents,
+        scratch=[pltpu.SemaphoreType.DMA((16,))],
+        out_space=pltpu.HBM,
+    )
     copies, noise = lax.optimization_barrier((copies, noise_latents))
     columns = keep(spread(copies, COL_GROUP).reshape(ROWS, WIDTH))
     own_rows = gather_z(noise).reshape(ROWS // 2, WIDTH)
-    other_rows = keep(swap_core(own_rows))
+    other_rows = pltpu.with_memory_space_constraint(swap_core(own_rows), pltpu.HBM)
 
     scores, parts = run(
         scores_kernel,
@@ -294,6 +318,8 @@
         keep(own_rows),
         other_rows,
         flops=2 * ROWS * ROWS * WIDTH,
+        scratch=[pltpu.VMEM((ROWS // 2, WIDTH), jnp.bfloat16), pltpu.SemaphoreType.DMA],
+        in_hbm=(2,),
     )
     scores = keep(scores)
     row_dual, parts = run(columns_kernel, (SQUARE, COPIES), scores, spread(parts, ROW_GROUP))
@@ -324,20 +350,20 @@
         columns,
         flops=ROWS * ROWS * WIDTH,
     )
-    own, right, left = run(
+    own, right, left, right2, left2 = run(
         cores_kernel,
-        (sent_rows(ROWS // 2), sent_rows(PIECE), sent_rows(PIECE)),
+        tuple(sent_rows(count) for count in (ROWS // 2, PIECE, PIECE, PIECE // 2, PIECE // 2)),
         keep(own),
         keep(got),
     )
     own = keep(own)
     right, left = shift_z(right, 1), shift_z(left, -1)
-    for k in (3, 2, 1):
-        passing = functools.partial(pass_kernel, k)
-        right = shift_z(run(passing, sent_rows(PIECE), own, keep(right)), 1)
-        if k > 1:
-            passing = functools.partial(pass_kernel, 9 - k)
-            left = shift_z(run(passing, sent_rows(PIECE), own, keep(left)), -1)
+    right2, left2 = shift_z(right2, 2), shift_z(left2, -2)
+    joined = sent_rows(PIECE)
+    right = shift_z(run(functools.partial(join_kernel, 2, 0), joined, own, keep(right), keep(right2)), 1)
+    left = shift_z(run(functools.partial(join_kernel, 6, 1), joined, own, keep(left), keep(left2)), -1)
+    right = shift_z(run(functools.partial(pass_kernel, 1), joined, own, keep(right)), 1)
+    left = shift_z(run(functools.partial(pass_kernel, 7), joined, own, keep(left)), -1)
     velocity = jax.ShapeDtypeStruct((PIECE, WIDTH), jnp.bfloat16)
     return run(velocity_kernel, velocity, own, keep(right), keep(left), noise_latents)
 

time: 152 us -> 148 us (0.974)
  waiting for transfers between devices: 35.8 us -> 27 us
  starting transfers between devices: 30.6 us -> 37.2 us
  local copies, waits for them, and re-layouts: 4.68 us -> 1.13 us
  Pallas kernels: 13.1 us -> 14.7 us
    ppermute x14 -> x16, waiting for transfers between devices: 30.8 us -> 19.2 us  [shift_z(): lax.ppermute(a, AXES, device_pairs(lambda x, yh, c, yl, z: (x, yh, c, yl,...]
    ppermute x14 -> x16, starting transfers between devices: 23 us -> 29.5 us  [shift_z(): lax.ppermute(a, AXES, device_pairs(lambda x, yh, c, yl, z: (x, yh, c, yl,...]
    unnamed x10 -> x4, local copies, waits for them, and re-layouts: 4.45 us -> 0.91 us
    all_to_all x1, waiting for transfers between devices: 1.1 us -> 3.84 us  [spread(): return lax.all_to_all(copies, group, 0, 0)]
    pallas_call x16 -> x15, Pallas kernels: 13.1 us -> 14.7 us  [run(): pl.pallas_call(kernel, out_shape=outs, in_specs=[pl.BlockSpec(memory_spac...]
  transfers between devices with their start and end apart: 17 -> 19, of which waited for: 10 -> 9; matrix products, arithmetic and copies ran while one was open for 0% -> 0% of each run, Pallas kernels for 1% -> 1%
where the time goes in v7:
time: 148 us
  blocking collectives  67.7 us (46%)
  starting transfers between devices  37.2 us (25%)
  waiting for transfers between devices  27 us (18%)
  Pallas kernels  14.7 us (10%)
    all_to_all x6, blocking collectives, spread(): return lax.all_to_all(copies, group, 0, 0)  67.7 us
    ppermute x16, starting transfers between devices, shift_z(): lax.ppermute(a, AXES, device_pairs(lambda x, yh, c, yl, z: (x, yh, c, yl,...  29.5 us
    ppermute x16, waiting for transfers between devices, shift_z(): lax.ppermute(a, AXES, device_pairs(lambda x, yh, c, yl, z: (x, yh, c, yl,...  19.2 us
    pallas_call x15, Pallas kernels, run(): pl.pallas_call(kernel, out_shape=outs, in_specs=[pl.BlockSpec(memory_spac...  14.7 us
    all_to_all x1, starting transfers between devices, spread(): return lax.all_to_all(copies, group, 0, 0)  7.48 us
    ppermute x2, waiting for transfers between devices, swap_core(): lax.ppermute(a, AXES, device_pairs(lambda x, yh, c, yl, z: (x, yh, 1 - c,...  4.03 us
    all_to_all x1, waiting for transfers between devices, spread(): return lax.all_to_all(copies, group, 0, 0)  3.84 us
  transfers between devices with their start and end apart: 19, of which 9 were waited for; matrix products, arithmetic and copies ran while one was open for 0% of the time, Pallas kernels for 1%

profile of v7, /device:TPU:2, one launch (start us, length us, event | category | flops | bytes accessed | tf_op | source)
XLA Modules:
  0.0 147.9 jit_solution(4945602696174284458)
XLA Ops:
  2.4 5.9 %collective-permute-start.1 = (bf16[64,1024]{1,0:T(8,128)(2,1)S(1)}, bf16[64,1024]{1,0:T(8,128)(2,1)S(1)}, u32[]{:S(2)}, u32[]{:S(2)}) collective-permute-start(bf16[64,1024]{1,0:T(8,128)(2,1)S(1)} %copy-done), channel_id=1, source_target_pairs={{0,7},{1,0},{2,1},{3,2},{4,3},{5,4},{6,5},{7,6},{8,15},{9,8},{10,9... | collective-permute-start | bytes 393224 | tf_op jit(solution)/shard_map/ppermute | solution.py:48
  8.3 7.5 %all-to-all-start = ((bf16[16,64,1024]{2,1,0:T(8,128)(2,1)}), bf16[16,64,1024]{2,1,0:T(8,128)(2,1)S(1)}, u32[]{:S(2)}, u32[]{:S(2)}) async-start(bf16[16,64,1024]{2,1,0:T(8,128)(2,1)} %shard_map.28), calls=%async_computation | async-start | bytes 4194304 | tf_op jit(solution)/shard_map/all_to_all | solution.py:56
  16.0 3.3 %collective-permute-start.3 = (bf16[64,1024]{1,0:T(8,128)(2,1)S(1)}, bf16[64,1024]{1,0:T(8,128)(2,1)S(1)}, u32[]{:S(2)}, u32[]{:S(2)}) collective-permute-start(bf16[64,1024]{1,0:T(8,128)(2,1)S(1)} %collective-permute-done.1), channel_id=1, source_target_pairs={{0,7},{1,0},{2,1},{3,2},{4,3},{5,4},{6,5},{7,6},{8,15},{9,8},{10,9... | collective-permute-start | bytes 393224 | tf_op jit(solution)/shard_map/ppermute | solution.py:48
  19.3 2.5 %collective-permute-done.3 = bf16[64,1024]{1,0:T(8,128)(2,1)S(1)} collective-permute-done((bf16[64,1024]{1,0:T(8,128)(2,1)S(1)}, bf16[64,1024]{1,0:T(8,128)(2,1)S(1)}, u32[]{:S(2)}, u32[]{:S(2)}) %collective-permute-start.3) | collective-permute-done | bytes 131104 | tf_op jit(solution)/shard_map/ppermute | solution.py:48
  21.8 1.9 %collective-permute-start.7 = (bf16[32,1024]{1,0:T(8,128)(2,1)S(1)}, bf16[32,1024]{1,0:T(8,128)(2,1)S(1)}, u32[]{:S(2)}, u32[]{:S(2)}) collective-permute-start(bf16[32,1024]{1,0:T(8,128)(2,1)S(1)} %slice.9), channel_id=1, source_target_pairs={{0,6},{1,7},{2,0},{3,1},{4,2},{5,3},{6,4},{7,5},{8,14},{9,15},{10,... | collective-permute-start | bytes 196616 | tf_op jit(solution)/shard_map/ppermute | solution.py:48
  25.5 4.2 %collective-permute-start.5 = (bf16[64,1024]{1,0:T(8,128)(2,1)S(1)}, bf16[64,1024]{1,0:T(8,128)(2,1)S(1)}, u32[]{:S(2)}, u32[]{:S(2)}) collective-permute-start(bf16[64,1024]{1,0:T(8,128)(2,1)S(1)} %collective-permute-done.3), channel_id=1, source_target_pairs={{0,7},{1,0},{2,1},{3,2},{4,3},{5,4},{6,5},{7,6},{8,15},{9,8},{10,9... | collective-permute-start | bytes 393224 | tf_op jit(solution)/shard_map/ppermute | solution.py:48
  29.7 6.1 %collective-permute-done.4 = bf16[64,1024]{1,0:T(8,128)(2,1)S(1)} collective-permute-done((bf16[64,1024]{1,0:T(8,128)(2,1)S(1)}, bf16[64,1024]{1,0:T(8,128)(2,1)S(1)}, u32[]{:S(2)}, u32[]{:S(2)}) %collective-permute-start.4) | collective-permute-done | bytes 131104 | tf_op jit(solution)/shard_map/ppermute | solution.py:48
  36.1 2.8 %collective-permute-done.8.far_ref = bf16[512,1024]{1,0:T(8,128)(2,1)} collective-permute-done((bf16[512,1024]{1,0:T(8,128)(2,1)S(1)}, bf16[512,1024]{1,0:T(8,128)(2,1)}, u32[]{:S(2)}, u32[]{:S(2)}) %collective-permute-start.8) | collective-permute-done | bytes 1048608 | tf_op jit(solution)/shard_map/ppermute | solution.py:52
  38.8 3.8 %all-to-all-done = bf16[16,64,1024]{2,1,0:T(8,128)(2,1)S(1)} async-done(((bf16[16,64,1024]{2,1,0:T(8,128)(2,1)}), bf16[16,64,1024]{2,1,0:T(8,128)(2,1)S(1)}, u32[]{:S(2)}, u32[]{:S(2)}) %all-to-all-start) | async-done | bytes 2097184 | tf_op jit(solution)/shard_map/all_to_all | solution.py:56
  42.7 3.7 %shard_map.29 = (f32[1024,1024]{1,0:T(8,128)S(1)}, f32[16,8,128]{2,1,0:T(8,128)S(1)}) custom-call(bf16[1024,1024]{1,0:T(8,128)(2,1)S(1)} %bitcast.20, bf16[512,1024]{1,0:T(8,128)(2,1)S(1)} %bitcast.24, bf16[512,1024]{1,0:T(8,128)(2,1)} %collective-permute-done.8.far_ref), custom_call_target="tpu_custom_call" | custom-call | flops 2147483648 | bytes 4194304 | tf_op jit(solution)/shard_map/pallas_call | solution.py:282
  46.4 12.2 %all_to_all.35.in_ref = f32[16,8,128]{2,1,0:T(8,128)S(1)} all-to-all(f32[16,8,128]{2,1,0:T(8,128)S(1)} %get-tuple-element.23), channel_id=1, replica_groups=mesh['x'=4,'yh'=2,'core'=2,'yl'=2,'z'=8] {'core','z'}, dimensions={0} | all-to-all | bytes 131072 | tf_op jit(solution)/shard_map/all_to_all | solution.py:56
  59.8 12.7 %all_to_all.36.in_ref = f32[16,8,128]{2,1,0:T(8,128)S(1)} all-to-all(f32[16,8,128]{2,1,0:T(8,128)S(1)} %get-tuple-element.25), channel_id=1, replica_groups=mesh['x'=4,'yh'=2,'core'=2,'yl'=2,'z'=8] {'x','yh','yl'}, dimensions={0} | all-to-all | bytes 131072 | tf_op jit(solution)/shard_map/all_to_all | solution.py:56
  73.4 10.5 %all_to_all.37.in_ref = f32[16,8,128]{2,1,0:T(8,128)S(1)} all-to-all(f32[16,8,128]{2,1,0:T(8,128)S(1)} %get-tuple-element.27), channel_id=1, replica_groups=mesh['x'=4,'yh'=2,'core'=2,'yl'=2,'z'=8] {'core','z'}, dimensions={0} | all-to-all | bytes 131072 | tf_op jit(solution)/shard_map/all_to_all | solution.py:56
  84.5 10.9 %all_to_all.38.in_ref = f32[16,8,128]{2,1,0:T(8,128)S(1)} all-to-all(f32[16,8,128]{2,1,0:T(8,128)S(1)} %shard_map.32), channel_id=1, replica_groups=mesh['x'=4,'yh'=2,'core'=2,'yl'=2,'z'=8] {'x','yh','yl'}, dimensions={0} | all-to-all | bytes 131072 | tf_op jit(solution)/shard_map/all_to_all | solution.py:56
  95.8 10.5 %all_to_all.39.in_ref = f32[16,8,128]{2,1,0:T(8,128)S(1)} all-to-all(f32[16,8,128]{2,1,0:T(8,128)S(1)} %shard_map.33), channel_id=1, replica_groups=mesh['x'=4,'yh'=2,'core'=2,'yl'=2,'z'=8] {'core','z'}, dimensions={0} | all-to-all | bytes 131072 | tf_op jit(solution)/shard_map/all_to_all | solution.py:56
  107.0 10.9 %all_to_all.40.in_ref = f32[16,8,128]{2,1,0:T(8,128)S(1)} all-to-all(f32[16,8,128]{2,1,0:T(8,128)S(1)} %shard_map.34), channel_id=1, replica_groups=mesh['x'=4,'yh'=2,'core'=2,'yl'=2,'z'=8] {'x','yh','yl'}, dimensions={0} | all-to-all | bytes 131072 | tf_op jit(solution)/shard_map/all_to_all | solution.py:56
  117.9 2.2 %shard_map.35 = (bf16[1024,1024]{1,0:T(8,128)(2,1)S(1)}, bf16[512,1152]{1,0:T(8,128)(2,1)S(1)}) custom-call(bf16[1024,1024]{1,0:T(8,128)(2,1)S(1)} %get-tuple-element.26.plan_ref, f32[16,8,128]{2,1,0:T(8,128)S(1)} %all_to_all.40.in_ref, bf16[1024,1024]{1,0:T(8,128)(2,1)S(1)} %bitcast.21), custom_call_target="tpu_custom_call" | custom-call | flops 1073741824 | bytes 4194304 | tf_op jit(solution)/shard_map/pallas_call | solution.py:282
  124.6 2.3 %collective-permute-start.14 = (bf16[64,1152]{1,0:T(8,128)(2,1)S(1)}, bf16[64,1152]{1,0:T(8,128)(2,1)S(1)}, u32[]{:S(2)}, u32[]{:S(2)}) collective-permute-start(bf16[64,1152]{1,0:T(8,128)(2,1)S(1)} %get-tuple-element.33), channel_id=1, source_target_pairs={{0,7},{1,0},{2,1},{3,2},{4,3},{5,4},{6,5},{7,6},{8,15},{9,8},{10,9... | collective-permute-start | bytes 442376 | tf_op jit(solution)/shard_map/ppermute | solution.py:48
  126.8 4.1 %collective-permute-start.15 = (bf16[32,1152]{1,0:T(8,128)(2,1)S(1)}, bf16[32,1152]{1,0:T(8,128)(2,1)S(1)}, u32[]{:S(2)}, u32[]{:S(2)}) collective-permute-start(bf16[32,1152]{1,0:T(8,128)(2,1)S(1)} %get-tuple-element.34), channel_id=1, source_target_pairs={{0,6},{1,7},{2,0},{3,1},{4,2},{5,3},{6,4},{7,5},{8,14},{9,15},{10,... | collective-permute-start | bytes 221192 | tf_op jit(solution)/shard_map/ppermute | solution.py:48
  131.0 2.9 %collective-permute-done.11.far_ref = bf16[32,1152]{1,0:T(8,128)(2,1)S(1)} collective-permute-done((bf16[32,1152]{1,0:T(8,128)(2,1)S(1)}, bf16[32,1152]{1,0:T(8,128)(2,1)S(1)}, u32[]{:S(2)}, u32[]{:S(2)}) %collective-permute-start.11) | collective-permute-done | bytes 73760 | tf_op jit(solution)/shard_map/ppermute | solution.py:48
  134.9 2.7 %collective-permute-start.16 = (bf16[64,1152]{1,0:T(8,128)(2,1)S(1)}, bf16[64,1152]{1,0:T(8,128)(2,1)S(1)}, u32[]{:S(2)}, u32[]{:S(2)}) collective-permute-start(bf16[64,1152]{1,0:T(8,128)(2,1)S(1)} %shard_map.40), channel_id=1, source_target_pairs={{0,7},{1,0},{2,1},{3,2},{4,3},{5,4},{6,5},{7,6},{8,15},{9,8},{10,9... | collective-permute-start | bytes 442376 | tf_op jit(solution)/shard_map/ppermute | solution.py:48
  137.6 2.9 %collective-permute-done.12.got_ref = bf16[64,1152]{1,0:T(8,128)(2,1)S(1)} collective-permute-done((bf16[64,1152]{1,0:T(8,128)(2,1)S(1)}, bf16[64,1152]{1,0:T(8,128)(2,1)S(1)}, u32[]{:S(2)}, u32[]{:S(2)}) %collective-permute-start.12) | collective-permute-done | bytes 147488 | tf_op jit(solution)/shard_map/ppermute | solution.py:48
  140.8 3.3 %collective-permute-start.17 = (bf16[64,1152]{1,0:T(8,128)(2,1)S(1)}, bf16[64,1152]{1,0:T(8,128)(2,1)S(1)}, u32[]{:S(2)}, u32[]{:S(2)}) collective-permute-start(bf16[64,1152]{1,0:T(8,128)(2,1)S(1)} %shard_map.41), channel_id=1, source_target_pairs={{0,7},{1,0},{2,1},{3,2},{4,3},{5,4},{6,5},{7,6},{8,15},{9,8},{10,9... | collective-permute-start | bytes 442376 | tf_op jit(solution)/shard_map/ppermute | solution.py:48
  144.1 2.9 %collective-permute-done.13.right_ref = bf16[64,1152]{1,0:T(8,128)(2,1)S(1)} collective-permute-done((bf16[64,1152]{1,0:T(8,128)(2,1)S(1)}, bf16[64,1152]{1,0:T(8,128)(2,1)S(1)}, u32[]{:S(2)}, u32[]{:S(2)}) %collective-permute-start.13) | collective-permute-done | bytes 147488 | tf_op jit(solution)/shard_map/ppermute | solution.py:48
  (50 shorter events, 14.9 us)
Async XLA Ops:
  0.0 0.9 copy-start.1
  0.9 1.5 %copy-start = (bf16[64,1024]{1,0:T(8,128)(2,1)S(1)}, bf16[64,1024]{1,0:T(8,128)(2,1)}, u32[]{:S(2)}) copy-start(bf16[64,1024]{1,0:T(8,128)(2,1)} %noise_ref.1) | copy-start | bytes 393220
  2.4 13.6 %collective-permute-start.1 = (bf16[64,1024]{1,0:T(8,128)(2,1)S(1)}, bf16[64,1024]{1,0:T(8,128)(2,1)S(1)}, u32[]{:S(2)}, u32[]{:S(2)}) collective-permute-start(bf16[64,1024]{1,0:T(8,128)(2,1)S(1)} %copy-done), channel_id=1, source_target_pairs={{0,7},{1,0},{2,1},{3,2},{4,3},{5,4},{6,5},{7,6},{8,15},{9,8},{10,9... | collective-permute-start | bytes 393224 | tf_op jit(solution)/shard_map/ppermute | solution.py:48
  8.3 11.0 %collective-permute-start = (bf16[64,1024]{1,0:T(8,128)(2,1)S(1)}, bf16[64,1024]{1,0:T(8,128)(2,1)S(1)}, u32[]{:S(2)}, u32[]{:S(2)}) collective-permute-start(bf16[64,1024]{1,0:T(8,128)(2,1)S(1)} %copy-done), channel_id=1, source_target_pairs={{0,1},{1,2},{2,3},{3,4},{4,5},{5,6},{6,7},{7,0},{8,9},{9,10},{10,1... | collective-permute-start | bytes 393224 | tf_op jit(solution)/shard_map/ppermute | solution.py:48
  8.3 34.4 %all-to-all-start = ((bf16[16,64,1024]{2,1,0:T(8,128)(2,1)}), bf16[16,64,1024]{2,1,0:T(8,128)(2,1)S(1)}, u32[]{:S(2)}, u32[]{:S(2)}) async-start(bf16[16,64,1024]{2,1,0:T(8,128)(2,1)} %shard_map.28), calls=%async_computation | async-start | bytes 4194304 | tf_op jit(solution)/shard_map/all_to_all | solution.py:56
  16.0 5.8 %collective-permute-start.3 = (bf16[64,1024]{1,0:T(8,128)(2,1)S(1)}, bf16[64,1024]{1,0:T(8,128)(2,1)S(1)}, u32[]{:S(2)}, u32[]{:S(2)}) collective-permute-start(bf16[64,1024]{1,0:T(8,128)(2,1)S(1)} %collective-permute-done.1), channel_id=1, source_target_pairs={{0,7},{1,0},{2,1},{3,2},{4,3},{5,4},{6,5},{7,6},{8,15},{9,8},{10,9... | collective-permute-start | bytes 393224 | tf_op jit(solution)/shard_map/ppermute | solution.py:48
  19.3 6.2 %collective-permute-start.2 = (bf16[64,1024]{1,0:T(8,128)(2,1)S(1)}, bf16[64,1024]{1,0:T(8,128)(2,1)S(1)}, u32[]{:S(2)}, u32[]{:S(2)}) collective-permute-start(bf16[64,1024]{1,0:T(8,128)(2,1)S(1)} %collective-permute-done), channel_id=1, source_target_pairs={{0,1},{1,2},{2,3},{3,4},{4,5},{5,6},{6,7},{7,0},{8,9},{9,10},{10,1... | collective-permute-start | bytes 393224 | tf_op jit(solution)/shard_map/ppermute | solution.py:48
  21.8 14.1 %collective-permute-start.7 = (bf16[32,1024]{1,0:T(8,128)(2,1)S(1)}, bf16[32,1024]{1,0:T(8,128)(2,1)S(1)}, u32[]{:S(2)}, u32[]{:S(2)}) collective-permute-start(bf16[32,1024]{1,0:T(8,128)(2,1)S(1)} %slice.9), channel_id=1, source_target_pairs={{0,6},{1,7},{2,0},{3,1},{4,2},{5,3},{6,4},{7,5},{8,14},{9,15},{10,... | collective-permute-start | bytes 196616 | tf_op jit(solution)/shard_map/ppermute | solution.py:48
  25.5 10.5 %collective-permute-start.6 = (bf16[32,1024]{1,0:T(8,128)(2,1)S(1)}, bf16[32,1024]{1,0:T(8,128)(2,1)S(1)}, u32[]{:S(2)}, u32[]{:S(2)}) collective-permute-start(bf16[32,1024]{1,0:T(8,128)(2,1)S(1)} %slice.8), channel_id=1, source_target_pairs={{0,2},{1,3},{2,4},{3,5},{4,6},{5,7},{6,0},{7,1},{8,10},{9,11},{10,... | collective-permute-start | bytes 196616 | tf_op jit(solution)/shard_map/ppermute | solution.py:48
  25.5 10.4 %collective-permute-start.5 = (bf16[64,1024]{1,0:T(8,128)(2,1)S(1)}, bf16[64,1024]{1,0:T(8,128)(2,1)S(1)}, u32[]{:S(2)}, u32[]{:S(2)}) collective-permute-start(bf16[64,1024]{1,0:T(8,128)(2,1)S(1)} %collective-permute-done.3), channel_id=1, source_target_pairs={{0,7},{1,0},{2,1},{3,2},{4,3},{5,4},{6,5},{7,6},{8,15},{9,8},{10,9... | collective-permute-start | bytes 393224 | tf_op jit(solution)/shard_map/ppermute | solution.py:48
  29.7 6.2 %collective-permute-start.4 = (bf16[64,1024]{1,0:T(8,128)(2,1)S(1)}, bf16[64,1024]{1,0:T(8,128)(2,1)S(1)}, u32[]{:S(2)}, u32[]{:S(2)}) collective-permute-start(bf16[64,1024]{1,0:T(8,128)(2,1)S(1)} %collective-permute-done.2), channel_id=1, source_target_pairs={{0,1},{1,2},{2,3},{3,4},{4,5},{5,6},{6,7},{7,0},{8,9},{9,10},{10,1... | collective-permute-start | bytes 393224 | tf_op jit(solution)/shard_map/ppermute | solution.py:48
  36.0 2.9 %collective-permute-start.8 = (bf16[512,1024]{1,0:T(8,128)(2,1)S(1)}, bf16[512,1024]{1,0:T(8,128)(2,1)}, u32[]{:S(2)}, u32[]{:S(2)}) collective-permute-start(bf16[512,1024]{1,0:T(8,128)(2,1)S(1)} %bitcast.23), channel_id=1, source_target_pairs={{0,16},{1,17},{2,18},{3,19},{4,20},{5,21},{6,22},{7,23},{8,24},{9,... | collective-permute-start | bytes 3145736 | tf_op jit(solution)/shard_map/ppermute | solution.py:52
  120.1 2.9 %collective-permute-start.9 = (bf16[512,1152]{1,0:T(8,128)(2,1)S(1)}, bf16[512,1152]{1,0:T(8,128)(2,1)S(1)}, u32[]{:S(2)}, u32[]{:S(2)}) collective-permute-start(bf16[512,1152]{1,0:T(8,128)(2,1)S(1)} %get-tuple-element.29), channel_id=1, source_target_pairs={{0,16},{1,17},{2,18},{3,19},{4,20},{5,21},{6,22},{7,23},{8,24},{9,... | collective-permute-start | bytes 3538952 | tf_op jit(solution)/shard_map/ppermute | solution.py:52
  123.5 10.4 %collective-permute-start.10 = (bf16[64,1152]{1,0:T(8,128)(2,1)S(1)}, bf16[64,1152]{1,0:T(8,128)(2,1)S(1)}, u32[]{:S(2)}, u32[]{:S(2)}) collective-permute-start(bf16[64,1152]{1,0:T(8,128)(2,1)S(1)} %get-tuple-element.31), channel_id=1, source_target_pairs={{0,1},{1,2},{2,3},{3,4},{4,5},{5,6},{6,7},{7,0},{8,9},{9,10},{10,1... | collective-permute-start | bytes 442376 | tf_op jit(solution)/shard_map/ppermute | solution.py:48
  124.6 10.2 %collective-permute-start.14 = (bf16[64,1152]{1,0:T(8,128)(2,1)S(1)}, bf16[64,1152]{1,0:T(8,128)(2,1)S(1)}, u32[]{:S(2)}, u32[]{:S(2)}) collective-permute-start(bf16[64,1152]{1,0:T(8,128)(2,1)S(1)} %get-tuple-element.33), channel_id=1, source_target_pairs={{0,7},{1,0},{2,1},{3,2},{4,3},{5,4},{6,5},{7,6},{8,15},{9,8},{10,9... | collective-permute-start | bytes 442376 | tf_op jit(solution)/shard_map/ppermute | solution.py:48
  126.8 7.1 %collective-permute-start.11 = (bf16[32,1152]{1,0:T(8,128)(2,1)S(1)}, bf16[32,1152]{1,0:T(8,128)(2,1)S(1)}, u32[]{:S(2)}, u32[]{:S(2)}) collective-permute-start(bf16[32,1152]{1,0:T(8,128)(2,1)S(1)} %get-tuple-element.32), channel_id=1, source_target_pairs={{0,2},{1,3},{2,4},{3,5},{4,6},{5,7},{6,0},{7,1},{8,10},{9,11},{10,... | collective-permute-start | bytes 221192 | tf_op jit(solution)/shard_map/ppermute | solution.py:48
  126.8 7.9 %collective-permute-start.15 = (bf16[32,1152]{1,0:T(8,128)(2,1)S(1)}, bf16[32,1152]{1,0:T(8,128)(2,1)S(1)}, u32[]{:S(2)}, u32[]{:S(2)}) collective-permute-start(bf16[32,1152]{1,0:T(8,128)(2,1)S(1)} %get-tuple-element.34), channel_id=1, source_target_pairs={{0,6},{1,7},{2,0},{3,1},{4,2},{5,3},{6,4},{7,5},{8,14},{9,15},{10,... | collective-permute-start | bytes 221192 | tf_op jit(solution)/shard_map/ppermute | solution.py:48
  134.1 6.4 %collective-permute-start.12 = (bf16[64,1152]{1,0:T(8,128)(2,1)S(1)}, bf16[64,1152]{1,0:T(8,128)(2,1)S(1)}, u32[]{:S(2)}, u32[]{:S(2)}) collective-permute-start(bf16[64,1152]{1,0:T(8,128)(2,1)S(1)} %shard_map.38), channel_id=1, source_target_pairs={{0,1},{1,2},{2,3},{3,4},{4,5},{5,6},{6,7},{7,0},{8,9},{9,10},{10,1... | collective-permute-start | bytes 442376 | tf_op jit(solution)/shard_map/ppermute | solution.py:48
  134.9 5.8 %collective-permute-start.16 = (bf16[64,1152]{1,0:T(8,128)(2,1)S(1)}, bf16[64,1152]{1,0:T(8,128)(2,1)S(1)}, u32[]{:S(2)}, u32[]{:S(2)}) collective-permute-start(bf16[64,1152]{1,0:T(8,128)(2,1)S(1)} %shard_map.40), channel_id=1, source_target_pairs={{0,7},{1,0},{2,1},{3,2},{4,3},{5,4},{6,5},{7,6},{8,15},{9,8},{10,9... | collective-permute-start | bytes 442376 | tf_op jit(solution)/shard_map/ppermute | solution.py:48
  140.6 6.4 %collective-permute-start.13 = (bf16[64,1152]{1,0:T(8,128)(2,1)S(1)}, bf16[64,1152]{1,0:T(8,128)(2,1)S(1)}, u32[]{:S(2)}, u32[]{:S(2)}) collective-permute-start(bf16[64,1152]{1,0:T(8,128)(2,1)S(1)} %shard_map.39), channel_id=1, source_target_pairs={{0,1},{1,2},{2,3},{3,4},{4,5},{5,6},{6,7},{7,0},{8,9},{9,10},{10,1... | collective-permute-start | bytes 442376 | tf_op jit(solution)/shard_map/ppermute | solution.py:48
  140.8 6.2 %collective-permute-start.17 = (bf16[64,1152]{1,0:T(8,128)(2,1)S(1)}, bf16[64,1152]{1,0:T(8,128)(2,1)S(1)}, u32[]{:S(2)}, u32[]{:S(2)}) collective-permute-start(bf16[64,1152]{1,0:T(8,128)(2,1)S(1)} %shard_map.41), channel_id=1, source_target_pairs={{0,7},{1,0},{2,1},{3,2},{4,3},{5,4},{6,5},{7,6},{8,15},{9,8},{10,9... | collective-permute-start | bytes 442376 | tf_op jit(solution)/shard_map/ppermute | solution.py:48

commit v8 on v7

--- a/solution.py
+++ b/solution.py
@@ -56,21 +56,28 @@
     return lax.all_to_all(copies, group, 0, 0)
 
 
-def put(whole, part, at):
-    return lax.dynamic_update_index_in_dim(whole, part, at, 0)
-
-
-def gather_z(part):
-    z = lax.axis_index("z")
-    whole = put(jnp.zeros((8,) + part.shape, part.dtype), part, z)
-    right = left = part
-    for k in (1, 2, 3):
-        if k == 3:
-            halves = shift_z(right[: PIECE // 2], 2), shift_z(left[PIECE // 2 :], -2)
-        right, left = shift_z(right, 1), shift_z(left, -1)
-        whole = put(whole, right, jnp.bitwise_and(z - k, 7))
-        whole = put(whole, left, jnp.bitwise_and(z + k, 7))
-    return put(whole, jnp.concatenate(halves, axis=0), jnp.bitwise_and(z + 4, 7))
+def shift_out(a, by):
+    return lax.ppermute(
+        a, AXES, device_pairs(lambda x, yh, c, yl, z: (x, yh, c, yl, z + by * (1 - 2 * c)))
+    )
+
+
+def gather_z(shard):
+    ahead, behind = [shard], [shard]
+    for step in range(3):
+        if step == 2:
+            far = shift_out(ahead[2], 2)
+        ahead.append(shift_out(ahead[-1], 1))
+        behind.append(shift_out(behind[-1], -1))
+    return ahead[1], behind[1], ahead[2], behind[2], ahead[3], behind[3], far
+
+
+FOUND = (-1, 1, -2, 2, -3, 3, 4)
+
+
+def chip_rows(steps):
+    at = lax.axis_index("z") + steps * (1 - 2 * lax.axis_index("core"))
+    return pl.ds(pl.multiple_of(jnp.bitwise_and(at, 7) * PIECE, PIECE), PIECE)
 
 
 def to_lanes(square):
@@ -194,6 +201,18 @@
         write.wait()
 
 
+def tile_kernel(shard_ref, *refs):
+    sources, (out_ref, sems) = refs[:7], refs[7:]
+    loads = [
+        pltpu.make_async_copy(source, out_ref.at[chip_rows(steps), :], sems.at[k])
+        for k, (source, steps) in enumerate(zip((shard_ref, *sources), (0, *FOUND)))
+    ]
+    for load in loads:
+        load.start()
+    for load in loads:
+        load.wait()
+
+
 def with_total(body, total):
     high = total.astype(jnp.bfloat16).astype(jnp.float32)
     first = lax.broadcasted_iota(jnp.int32, total.shape, 1) < 64
@@ -240,30 +259,39 @@
     return ref[pl.ds(pl.multiple_of(at * PIECE, PIECE), PIECE), :]
 
 
-def cores_kernel(own_ref, got_ref, out_ref, right_ref, left_ref, right2_ref, left2_ref):
-    for k in range(4):
-        part = pl.ds(128 * k, 128)
-        out_ref[part, :] = summed(own_ref[part, :], got_ref[part, :])
-    right_ref[...] = piece(out_ref, 3)
-    left_ref[...] = piece(out_ref, 5)
-    far = piece(out_ref, 4)
+def start_kernel(own_ref, got_ref, right_ref, left_ref, right2_ref, left2_ref):
+    right_ref[...] = summed(piece(own_ref, 3), piece(got_ref, 3))
+    left_ref[...] = summed(piece(own_ref, 5), piece(got_ref, 5))
+    far = summed(piece(own_ref, 4), piece(got_ref, 4))
     right2_ref[...] = far[: PIECE // 2]
     left2_ref[...] = far[PIECE // 2 :]
 
 
+def cores_kernel(own_ref, got_ref, out_ref):
+    for k, steps in enumerate(LATE):
+        out_ref[pl.ds(PIECE * k, PIECE), :] = summed(piece(own_ref, steps), piece(got_ref, steps))
+
+
+LATE = (0, 1, 2, 6, 7)
+
+
+def later(ref, steps):
+    return ref[pl.ds(PIECE * LATE.index(steps), PIECE), :]
+
+
 def join_kernel(offset, start, own_ref, got_ref, far_ref, out_ref):
-    found = summed(piece(own_ref, offset), got_ref[...])
+    found = summed(later(own_ref, offset), got_ref[...])
     halves = [found[: PIECE // 2], found[PIECE // 2 :]]
     halves[start] = summed(halves[start], far_ref[...])
     out_ref[...] = jnp.concatenate(halves, axis=0)
 
 
 def pass_kernel(offset, own_ref, got_ref, out_ref):
-    out_ref[...] = summed(piece(own_ref, offset), got_ref[...])
+    out_ref[...] = summed(later(own_ref, offset), got_ref[...])
 
 
 def velocity_kernel(own_ref, right_ref, left_ref, noise_ref, out_ref):
-    found = [body_total(a) for a in (piece(own_ref, 0), right_ref[...], left_ref[...])]
+    found = [body_total(a) for a in (later(own_ref, 0), right_ref[...], left_ref[...])]
     body, total = (sum(values) for values in zip(*found))
     target = body / total[:, :1]
     out_ref[...] = (target - noise_ref[...].astype(jnp.float32)).astype(jnp.bfloat16)
@@ -305,10 +333,20 @@
         data_latents,
         scratch=[pltpu.SemaphoreType.DMA((16,))],
         out_space=pltpu.HBM,
-    )
-    copies, noise = lax.optimization_barrier((copies, noise_latents))
+        in_hbm=(0,),
+    )
     columns = keep(spread(copies, COL_GROUP).reshape(ROWS, WIDTH))
-    own_rows = gather_z(noise).reshape(ROWS // 2, WIDTH)
+    found = lax.cond(
+        lax.axis_index("x") < 4, gather_z, lambda shard: (jnp.zeros_like(shard),) * 7, noise_latents
+    )
+    own_rows = run(
+        tile_kernel,
+        in_vmem(ROWS // 2, jnp.bfloat16),
+        noise_latents,
+        *found,
+        scratch=[pltpu.SemaphoreType.DMA((8,))],
+        in_hbm=range(8),
+    )
     other_rows = pltpu.with_memory_space_constraint(swap_core(own_rows), pltpu.HBM)
 
     scores, parts = run(
@@ -350,12 +388,14 @@
         columns,
         flops=ROWS * ROWS * WIDTH,
     )
-    own, right, left, right2, left2 = run(
-        cores_kernel,
-        tuple(sent_rows(count) for count in (ROWS // 2, PIECE, PIECE, PIECE // 2, PIECE // 2)),
-        keep(own),
-        keep(got),
-    )
+    own, got = keep(own), keep(got)
+    right, left, right2, left2 = run(
+        start_kernel,
+        tuple(sent_rows(count) for count in (PIECE, PIECE, PIECE // 2, PIECE // 2)),
+        own,
+        got,
+    )
+    own = run(cores_kernel, sent_rows(PIECE * len(LATE)), own, got)
     own = keep(own)
     right, left = shift_z(right, 1), shift_z(left, -1)
     right2, left2 = shift_z(right2, 2), shift_z(left2, -2)

time: 148 us -> 147 us (level)
  starting transfers between devices: 37.2 us -> 35.4 us
    ppermute x16 -> x8, starting transfers between devices: 29.5 us -> 14.2 us  [shift_z(): lax.ppermute(a, AXES, device_pairs(lambda x, yh, c, yl, z: (x, yh, c, yl,...]
    ppermute x0 -> x7, waiting for transfers between devices: none -> 15.1 us  [shift_out(): lax.ppermute(a, AXES, device_pairs(lambda x, yh, c, yl, z: (x, yh, c, yl,...]
    ppermute x0 -> x7, starting transfers between devices: none -> 13.4 us  [shift_out(): lax.ppermute(a, AXES, device_pairs(lambda x, yh, c, yl, z: (x, yh, c, yl,...]
    ppermute x16 -> x8, waiting for transfers between devices: 19.2 us -> 8.42 us  [shift_z(): lax.ppermute(a, AXES, device_pairs(lambda x, yh, c, yl, z: (x, yh, c, yl,...]
    all_to_all x1, waiting for transfers between devices: 3.84 us -> 0.01 us  [spread(): return lax.all_to_all(copies, group, 0, 0)]
    pallas_call x15 -> x17, Pallas kernels: 14.7 us -> 16.1 us  [run(): pl.pallas_call(kernel, out_shape=outs, in_specs=[pl.BlockSpec(memory_spac...]
  transfers between devices with their start and end apart: 19 -> 18, of which waited for: 9 -> 12; matrix products, arithmetic and copies ran while one was open for 0% -> 0% of each run, Pallas kernels for 1% -> 3%
where the time goes in v8:
time: 147 us
  blocking collectives  66.7 us (45%)
  starting transfers between devices  35.4 us (24%)
  waiting for transfers between devices  27.5 us (19%)
  Pallas kernels  16.1 us (11%)
    all_to_all x6, blocking collectives, spread(): return lax.all_to_all(copies, group, 0, 0)  66.7 us
    pallas_call x17, Pallas kernels, run(): pl.pallas_call(kernel, out_shape=outs, in_specs=[pl.BlockSpec(memory_spac...  16.1 us
    ppermute x7, waiting for transfers between devices, shift_out(): lax.ppermute(a, AXES, device_pairs(lambda x, yh, c, yl, z: (x, yh, c, yl,...  15.1 us
    ppermute x8, starting transfers between devices, shift_z(): lax.ppermute(a, AXES, device_pairs(lambda x, yh, c, yl, z: (x, yh, c, yl,...  14.2 us
    ppermute x7, starting transfers between devices, shift_out(): lax.ppermute(a, AXES, device_pairs(lambda x, yh, c, yl, z: (x, yh, c, yl,...  13.4 us
    ppermute x8, waiting for transfers between devices, shift_z(): lax.ppermute(a, AXES, device_pairs(lambda x, yh, c, yl, z: (x, yh, c, yl,...  8.42 us
    all_to_all x1, starting transfers between devices, spread(): return lax.all_to_all(copies, group, 0, 0)  7.62 us
    ppermute x2, waiting for transfers between devices, swap_core(): lax.ppermute(a, AXES, device_pairs(lambda x, yh, c, yl, z: (x, yh, 1 - c,...  4.03 us
  transfers between devices with their start and end apart: 18, of which 12 were waited for; matrix products, arithmetic and copies ran while one was open for 0% of the time, Pallas kernels for 3%

profile of v8, /device:TPU:2, one launch (start us, length us, event | category | flops | bytes accessed | tf_op | source)
XLA Modules:
  0.0 146.8 jit_solution(11978997052093054663)
XLA Ops:
  2.4 7.6 %all-to-all-start = ((bf16[16,64,1024]{2,1,0:T(8,128)(2,1)}), bf16[16,64,1024]{2,1,0:T(8,128)(2,1)S(1)}, u32[]{:S(2)}, u32[]{:S(2)}) async-start(bf16[16,64,1024]{2,1,0:T(8,128)(2,1)} %shard_map.31), calls=%async_computation | async-start | bytes 4194304 | tf_op jit(solution)/shard_map/all_to_all | solution.py:56
  10.0 28.5 %conditional.1 = (bf16[64,1024]{1,0:T(8,128)(2,1)}, bf16[64,1024]{1,0:T(8,128)(2,1)}, bf16[64,1024]{1,0:T(8,128)(2,1)}, bf16[64,1024]{1,0:T(8,128)(2,1)}, bf16[6...) conditional(s32[]{:T(128)} %convert_element_type.3, () %tuple.13, ...), branch_computations={%region_0.0_spmd, %region_1.0_spmd} | conditional | bytes 3670352 | solution.py:339
  10.0 5.9 %collective-permute-start.1 = (bf16[64,1024]{1,0:T(8,128)(2,1)S(1)}, bf16[64,1024]{1,0:T(8,128)(2,1)}, u32[]{:S(2)}, u32[]{:S(2)}) collective-permute-start(bf16[64,1024]{1,0:T(8,128)(2,1)S(1)} %param.1), channel_id=1, source_target_pairs={{0,7},{1,0},{2,1},{3,2},{4,3},{5,4},{6,5},{7,6},{8,15},{9,8},{10,9... | collective-permute-start | bytes 393224 | tf_op jit(solution)/shard_map/cond/branch_1_fun/ppermute | solution.py:60
  16.0 2.5 %collective-permute-done.1 = bf16[64,1024]{1,0:T(8,128)(2,1)} collective-permute-done((bf16[64,1024]{1,0:T(8,128)(2,1)S(1)}, bf16[64,1024]{1,0:T(8,128)(2,1)}, u32[]{:S(2)}, u32[]{:S(2)}) %collective-permute-start.1) | collective-permute-done | bytes 131104 | tf_op jit(solution)/shard_map/cond/branch_1_fun/ppermute | solution.py:60
  18.5 3.8 %collective-permute-start.3 = (bf16[64,1024]{1,0:T(8,128)(2,1)}, bf16[64,1024]{1,0:T(8,128)(2,1)}, u32[]{:S(2)}, u32[]{:S(2)}) collective-permute-start(bf16[64,1024]{1,0:T(8,128)(2,1)} %collective-permute-done.1), channel_id=1, source_target_pairs={{0,7},{1,0},{2,1},{3,2},{4,3},{5,4},{6,5},{7,6},{8,15},{9,8},{10,9... | collective-permute-start | bytes 393224 | tf_op jit(solution)/shard_map/cond/branch_1_fun/ppermute | solution.py:60
  22.8 2.3 %collective-permute-done.3 = bf16[64,1024]{1,0:T(8,128)(2,1)} collective-permute-done((bf16[64,1024]{1,0:T(8,128)(2,1)}, bf16[64,1024]{1,0:T(8,128)(2,1)}, u32[]{:S(2)}, u32[]{:S(2)}) %collective-permute-start.3) | collective-permute-done | bytes 131104 | tf_op jit(solution)/shard_map/cond/branch_1_fun/ppermute | solution.py:60
  25.1 3.7 %collective-permute-start.5 = (bf16[64,1024]{1,0:T(8,128)(2,1)}, bf16[64,1024]{1,0:T(8,128)(2,1)}, u32[]{:S(2)}, u32[]{:S(2)}) collective-permute-start(bf16[64,1024]{1,0:T(8,128)(2,1)} %collective-permute-done.3), channel_id=1, source_target_pairs={{0,7},{1,0},{2,1},{3,2},{4,3},{5,4},{6,5},{7,6},{8,15},{9,8},{10,9... | collective-permute-start | bytes 393224 | tf_op jit(solution)/shard_map/cond/branch_1_fun/ppermute | solution.py:60
  32.5 5.6 %collective-permute-done.6 = bf16[64,1024]{1,0:T(8,128)(2,1)} collective-permute-done((bf16[64,1024]{1,0:T(8,128)(2,1)}, bf16[64,1024]{1,0:T(8,128)(2,1)}, u32[]{:S(2)}, u32[]{:S(2)}) %collective-permute-start.6) | collective-permute-done | bytes 131104 | tf_op jit(solution)/shard_map/cond/branch_1_fun/ppermute | solution.py:60
  40.1 2.8 %collective-permute-done.7.far_ref = bf16[512,1024]{1,0:T(8,128)(2,1)} collective-permute-done((bf16[512,1024]{1,0:T(8,128)(2,1)S(1)}, bf16[512,1024]{1,0:T(8,128)(2,1)}, u32[]{:S(2)}, u32[]{:S(2)}) %collective-permute-start.7) | collective-permute-done | bytes 1048608 | tf_op jit(solution)/shard_map/ppermute | solution.py:52
  42.8 3.7 %shard_map.33 = (f32[1024,1024]{1,0:T(8,128)S(1)}, f32[16,8,128]{2,1,0:T(8,128)S(1)}) custom-call(bf16[1024,1024]{1,0:T(8,128)(2,1)S(1)} %bitcast.1, bf16[512,1024]{1,0:T(8,128)(2,1)S(1)} %shard_map.32.own_ref, bf16[512,1024]{1,0:T(8,128)(2,1)} %collective-permute-done.7.far_ref), custom_call_target="tpu_custom_call" | custom-call | flops 2147483648 | bytes 4194304 | tf_op jit(solution)/shard_map/pallas_call | solution.py:310
  46.6 10.7 %all_to_all.35.in_ref = f32[16,8,128]{2,1,0:T(8,128)S(1)} all-to-all(f32[16,8,128]{2,1,0:T(8,128)S(1)} %get-tuple-element.33), channel_id=1, replica_groups=mesh['x'=4,'yh'=2,'core'=2,'yl'=2,'z'=8] {'core','z'}, dimensions={0} | all-to-all | bytes 131072 | tf_op jit(solution)/shard_map/all_to_all | solution.py:56
  58.4 13.3 %all_to_all.36.in_ref = f32[16,8,128]{2,1,0:T(8,128)S(1)} all-to-all(f32[16,8,128]{2,1,0:T(8,128)S(1)} %get-tuple-element.35), channel_id=1, replica_groups=mesh['x'=4,'yh'=2,'core'=2,'yl'=2,'z'=8] {'x','yh','yl'}, dimensions={0} | all-to-all | bytes 131072 | tf_op jit(solution)/shard_map/all_to_all | solution.py:56
  72.6 10.5 %all_to_all.37.in_ref = f32[16,8,128]{2,1,0:T(8,128)S(1)} all-to-all(f32[16,8,128]{2,1,0:T(8,128)S(1)} %get-tuple-element.37), channel_id=1, replica_groups=mesh['x'=4,'yh'=2,'core'=2,'yl'=2,'z'=8] {'core','z'}, dimensions={0} | all-to-all | bytes 131072 | tf_op jit(solution)/shard_map/all_to_all | solution.py:56
  83.7 10.9 %all_to_all.38.in_ref = f32[16,8,128]{2,1,0:T(8,128)S(1)} all-to-all(f32[16,8,128]{2,1,0:T(8,128)S(1)} %shard_map.36), channel_id=1, replica_groups=mesh['x'=4,'yh'=2,'core'=2,'yl'=2,'z'=8] {'x','yh','yl'}, dimensions={0} | all-to-all | bytes 131072 | tf_op jit(solution)/shard_map/all_to_all | solution.py:56
  95.0 10.5 %all_to_all.39.in_ref = f32[16,8,128]{2,1,0:T(8,128)S(1)} all-to-all(f32[16,8,128]{2,1,0:T(8,128)S(1)} %shard_map.37), channel_id=1, replica_groups=mesh['x'=4,'yh'=2,'core'=2,'yl'=2,'z'=8] {'core','z'}, dimensions={0} | all-to-all | bytes 131072 | tf_op jit(solution)/shard_map/all_to_all | solution.py:56
  106.2 10.9 %all_to_all.40.in_ref = f32[16,8,128]{2,1,0:T(8,128)S(1)} all-to-all(f32[16,8,128]{2,1,0:T(8,128)S(1)} %shard_map.38), channel_id=1, replica_groups=mesh['x'=4,'yh'=2,'core'=2,'yl'=2,'z'=8] {'x','yh','yl'}, dimensions={0} | all-to-all | bytes 131072 | tf_op jit(solution)/shard_map/all_to_all | solution.py:56
  117.1 2.2 %shard_map.39 = (bf16[1024,1024]{1,0:T(8,128)(2,1)S(1)}, bf16[512,1152]{1,0:T(8,128)(2,1)S(1)}) custom-call(bf16[1024,1024]{1,0:T(8,128)(2,1)S(1)} %get-tuple-element.36.plan_ref, f32[16,8,128]{2,1,0:T(8,128)S(1)} %all_to_all.40.in_ref, bf16[1024,1024]{1,0:T(8,128)(2,1)S(1)} %bitcast.2), custom_call_target="tpu_custom_call" | custom-call | flops 1073741824 | bytes 4194304 | tf_op jit(solution)/shard_map/pallas_call | solution.py:310
  123.4 2.3 %collective-permute-start.13 = (bf16[64,1152]{1,0:T(8,128)(2,1)S(1)}, bf16[64,1152]{1,0:T(8,128)(2,1)S(1)}, u32[]{:S(2)}, u32[]{:S(2)}) collective-permute-start(bf16[64,1152]{1,0:T(8,128)(2,1)S(1)} %get-tuple-element.42), channel_id=1, source_target_pairs={{0,7},{1,0},{2,1},{3,2},{4,3},{5,4},{6,5},{7,6},{8,15},{9,8},{10,9... | collective-permute-start | bytes 442376 | tf_op jit(solution)/shard_map/ppermute | solution.py:48
  125.7 4.1 %collective-permute-start.14 = (bf16[32,1152]{1,0:T(8,128)(2,1)S(1)}, bf16[32,1152]{1,0:T(8,128)(2,1)S(1)}, u32[]{:S(2)}, u32[]{:S(2)}) collective-permute-start(bf16[32,1152]{1,0:T(8,128)(2,1)S(1)} %get-tuple-element.43), channel_id=1, source_target_pairs={{0,6},{1,7},{2,0},{3,1},{4,2},{5,3},{6,4},{7,5},{8,14},{9,15},{10,... | collective-permute-start | bytes 221192 | tf_op jit(solution)/shard_map/ppermute | solution.py:48
  130.2 2.6 %collective-permute-done.10.far_ref = bf16[32,1152]{1,0:T(8,128)(2,1)S(1)} collective-permute-done((bf16[32,1152]{1,0:T(8,128)(2,1)S(1)}, bf16[32,1152]{1,0:T(8,128)(2,1)S(1)}, u32[]{:S(2)}, u32[]{:S(2)}) %collective-permute-start.10) | collective-permute-done | bytes 73760 | tf_op jit(solution)/shard_map/ppermute | solution.py:48
  133.8 2.7 %collective-permute-start.15 = (bf16[64,1152]{1,0:T(8,128)(2,1)S(1)}, bf16[64,1152]{1,0:T(8,128)(2,1)S(1)}, u32[]{:S(2)}, u32[]{:S(2)}) collective-permute-start(bf16[64,1152]{1,0:T(8,128)(2,1)S(1)} %shard_map.45), channel_id=1, source_target_pairs={{0,7},{1,0},{2,1},{3,2},{4,3},{5,4},{6,5},{7,6},{8,15},{9,8},{10,9... | collective-permute-start | bytes 442376 | tf_op jit(solution)/shard_map/ppermute | solution.py:48
  136.5 2.9 %collective-permute-done.11.got_ref = bf16[64,1152]{1,0:T(8,128)(2,1)S(1)} collective-permute-done((bf16[64,1152]{1,0:T(8,128)(2,1)S(1)}, bf16[64,1152]{1,0:T(8,128)(2,1)S(1)}, u32[]{:S(2)}, u32[]{:S(2)}) %collective-permute-start.11) | collective-permute-done | bytes 147488 | tf_op jit(solution)/shard_map/ppermute | solution.py:48
  139.7 3.3 %collective-permute-start.16 = (bf16[64,1152]{1,0:T(8,128)(2,1)S(1)}, bf16[64,1152]{1,0:T(8,128)(2,1)S(1)}, u32[]{:S(2)}, u32[]{:S(2)}) collective-permute-start(bf16[64,1152]{1,0:T(8,128)(2,1)S(1)} %shard_map.46), channel_id=1, source_target_pairs={{0,7},{1,0},{2,1},{3,2},{4,3},{5,4},{6,5},{7,6},{8,15},{9,8},{10,9... | collective-permute-start | bytes 442376 | tf_op jit(solution)/shard_map/ppermute | solution.py:48
  143.0 2.9 %collective-permute-done.12.right_ref = bf16[64,1152]{1,0:T(8,128)(2,1)S(1)} collective-permute-done((bf16[64,1152]{1,0:T(8,128)(2,1)S(1)}, bf16[64,1152]{1,0:T(8,128)(2,1)S(1)}, u32[]{:S(2)}, u32[]{:S(2)}) %collective-permute-start.12) | collective-permute-done | bytes 147488 | tf_op jit(solution)/shard_map/ppermute | solution.py:48
  (40 shorter events, 19.0 us)
Async XLA Ops:
  0.0 0.9 copy-start
  2.4 7.6 %copy-start.1 = (bf16[64,1024]{1,0:T(8,128)(2,1)S(1)}, bf16[64,1024]{1,0:T(8,128)(2,1)}, u32[]{:S(2)}) copy-start(bf16[64,1024]{1,0:T(8,128)(2,1)} %noise_ref.1) | copy-start | bytes 393220
  2.4 40.4 %all-to-all-start = ((bf16[16,64,1024]{2,1,0:T(8,128)(2,1)}), bf16[16,64,1024]{2,1,0:T(8,128)(2,1)S(1)}, u32[]{:S(2)}, u32[]{:S(2)}) async-start(bf16[16,64,1024]{2,1,0:T(8,128)(2,1)} %shard_map.31), calls=%async_computation | async-start | bytes 4194304 | tf_op jit(solution)/shard_map/all_to_all | solution.py:56
  10.0 8.5 %collective-permute-start.1 = (bf16[64,1024]{1,0:T(8,128)(2,1)S(1)}, bf16[64,1024]{1,0:T(8,128)(2,1)}, u32[]{:S(2)}, u32[]{:S(2)}) collective-permute-start(bf16[64,1024]{1,0:T(8,128)(2,1)S(1)} %param.1), channel_id=1, source_target_pairs={{0,7},{1,0},{2,1},{3,2},{4,3},{5,4},{6,5},{7,6},{8,15},{9,8},{10,9... | collective-permute-start | bytes 393224 | tf_op jit(solution)/shard_map/cond/branch_1_fun/ppermute | solution.py:60
  16.0 6.8 %collective-permute-start = (bf16[64,1024]{1,0:T(8,128)(2,1)S(1)}, bf16[64,1024]{1,0:T(8,128)(2,1)}, u32[]{:S(2)}, u32[]{:S(2)}) collective-permute-start(bf16[64,1024]{1,0:T(8,128)(2,1)S(1)} %param.1), channel_id=1, source_target_pairs={{0,1},{1,2},{2,3},{3,4},{4,5},{5,6},{6,7},{7,0},{8,9},{9,10},{10,1... | collective-permute-start | bytes 393224 | tf_op jit(solution)/shard_map/cond/branch_1_fun/ppermute | solution.py:60
  18.5 6.6 %collective-permute-start.3 = (bf16[64,1024]{1,0:T(8,128)(2,1)}, bf16[64,1024]{1,0:T(8,128)(2,1)}, u32[]{:S(2)}, u32[]{:S(2)}) collective-permute-start(bf16[64,1024]{1,0:T(8,128)(2,1)} %collective-permute-done.1), channel_id=1, source_target_pairs={{0,7},{1,0},{2,1},{3,2},{4,3},{5,4},{6,5},{7,6},{8,15},{9,8},{10,9... | collective-permute-start | bytes 393224 | tf_op jit(solution)/shard_map/cond/branch_1_fun/ppermute | solution.py:60
  22.8 7.8 %collective-permute-start.2 = (bf16[64,1024]{1,0:T(8,128)(2,1)}, bf16[64,1024]{1,0:T(8,128)(2,1)}, u32[]{:S(2)}, u32[]{:S(2)}) collective-permute-start(bf16[64,1024]{1,0:T(8,128)(2,1)} %collective-permute-done), channel_id=1, source_target_pairs={{0,1},{1,2},{2,3},{3,4},{4,5},{5,6},{6,7},{7,0},{8,9},{9,10},{10,1... | collective-permute-start | bytes 393224 | tf_op jit(solution)/shard_map/cond/branch_1_fun/ppermute | solution.py:60
  25.1 7.4 %collective-permute-start.5 = (bf16[64,1024]{1,0:T(8,128)(2,1)}, bf16[64,1024]{1,0:T(8,128)(2,1)}, u32[]{:S(2)}, u32[]{:S(2)}) collective-permute-start(bf16[64,1024]{1,0:T(8,128)(2,1)} %collective-permute-done.3), channel_id=1, source_target_pairs={{0,7},{1,0},{2,1},{3,2},{4,3},{5,4},{6,5},{7,6},{8,15},{9,8},{10,9... | collective-permute-start | bytes 393224 | tf_op jit(solution)/shard_map/cond/branch_1_fun/ppermute | solution.py:60
  30.6 7.5 %collective-permute-start.6 = (bf16[64,1024]{1,0:T(8,128)(2,1)}, bf16[64,1024]{1,0:T(8,128)(2,1)}, u32[]{:S(2)}, u32[]{:S(2)}) collective-permute-start(bf16[64,1024]{1,0:T(8,128)(2,1)} %collective-permute-done.2), channel_id=1, source_target_pairs={{0,2},{1,3},{2,4},{3,5},{4,6},{5,7},{6,0},{7,1},{8,10},{9,11},{10,... | collective-permute-start | bytes 393224 | tf_op jit(solution)/shard_map/cond/branch_1_fun/ppermute | solution.py:60
  30.6 7.9 %collective-permute-start.4 = (bf16[64,1024]{1,0:T(8,128)(2,1)}, bf16[64,1024]{1,0:T(8,128)(2,1)}, u32[]{:S(2)}, u32[]{:S(2)}) collective-permute-start(bf16[64,1024]{1,0:T(8,128)(2,1)} %collective-permute-done.2), channel_id=1, source_target_pairs={{0,1},{1,2},{2,3},{3,4},{4,5},{5,6},{6,7},{7,0},{8,9},{9,10},{10,1... | collective-permute-start | bytes 393224 | tf_op jit(solution)/shard_map/cond/branch_1_fun/ppermute | solution.py:60
  40.0 2.9 %collective-permute-start.7 = (bf16[512,1024]{1,0:T(8,128)(2,1)S(1)}, bf16[512,1024]{1,0:T(8,128)(2,1)}, u32[]{:S(2)}, u32[]{:S(2)}) collective-permute-start(bf16[512,1024]{1,0:T(8,128)(2,1)S(1)} %shard_map.32.own_ref), channel_id=1, source_target_pairs={{0,16},{1,17},{2,18},{3,19},{4,20},{5,21},{6,22},{7,23},{8,24},{9,... | collective-permute-start | bytes 3145736 | tf_op jit(solution)/shard_map/ppermute | solution.py:52
  119.3 2.9 %collective-permute-start.8 = (bf16[512,1152]{1,0:T(8,128)(2,1)S(1)}, bf16[512,1152]{1,0:T(8,128)(2,1)S(1)}, u32[]{:S(2)}, u32[]{:S(2)}) collective-permute-start(bf16[512,1152]{1,0:T(8,128)(2,1)S(1)} %get-tuple-element.39), channel_id=1, source_target_pairs={{0,16},{1,17},{2,18},{3,19},{4,20},{5,21},{6,22},{7,23},{8,24},{9,... | collective-permute-start | bytes 3538952 | tf_op jit(solution)/shard_map/ppermute | solution.py:52
  122.4 10.4 %collective-permute-start.9 = (bf16[64,1152]{1,0:T(8,128)(2,1)S(1)}, bf16[64,1152]{1,0:T(8,128)(2,1)S(1)}, u32[]{:S(2)}, u32[]{:S(2)}) collective-permute-start(bf16[64,1152]{1,0:T(8,128)(2,1)S(1)} %get-tuple-element.40), channel_id=1, source_target_pairs={{0,1},{1,2},{2,3},{3,4},{4,5},{5,6},{6,7},{7,0},{8,9},{9,10},{10,1... | collective-permute-start | bytes 442376 | tf_op jit(solution)/shard_map/ppermute | solution.py:48
  123.4 10.2 %collective-permute-start.13 = (bf16[64,1152]{1,0:T(8,128)(2,1)S(1)}, bf16[64,1152]{1,0:T(8,128)(2,1)S(1)}, u32[]{:S(2)}, u32[]{:S(2)}) collective-permute-start(bf16[64,1152]{1,0:T(8,128)(2,1)S(1)} %get-tuple-element.42), channel_id=1, source_target_pairs={{0,7},{1,0},{2,1},{3,2},{4,3},{5,4},{6,5},{7,6},{8,15},{9,8},{10,9... | collective-permute-start | bytes 442376 | tf_op jit(solution)/shard_map/ppermute | solution.py:48
  125.7 7.1 %collective-permute-start.10 = (bf16[32,1152]{1,0:T(8,128)(2,1)S(1)}, bf16[32,1152]{1,0:T(8,128)(2,1)S(1)}, u32[]{:S(2)}, u32[]{:S(2)}) collective-permute-start(bf16[32,1152]{1,0:T(8,128)(2,1)S(1)} %get-tuple-element.41), channel_id=1, source_target_pairs={{0,2},{1,3},{2,4},{3,5},{4,6},{5,7},{6,0},{7,1},{8,10},{9,11},{10,... | collective-permute-start | bytes 221192 | tf_op jit(solution)/shard_map/ppermute | solution.py:48
  125.7 7.9 %collective-permute-start.14 = (bf16[32,1152]{1,0:T(8,128)(2,1)S(1)}, bf16[32,1152]{1,0:T(8,128)(2,1)S(1)}, u32[]{:S(2)}, u32[]{:S(2)}) collective-permute-start(bf16[32,1152]{1,0:T(8,128)(2,1)S(1)} %get-tuple-element.43), channel_id=1, source_target_pairs={{0,6},{1,7},{2,0},{3,1},{4,2},{5,3},{6,4},{7,5},{8,14},{9,15},{10,... | collective-permute-start | bytes 221192 | tf_op jit(solution)/shard_map/ppermute | solution.py:48
  133.0 6.4 %collective-permute-start.11 = (bf16[64,1152]{1,0:T(8,128)(2,1)S(1)}, bf16[64,1152]{1,0:T(8,128)(2,1)S(1)}, u32[]{:S(2)}, u32[]{:S(2)}) collective-permute-start(bf16[64,1152]{1,0:T(8,128)(2,1)S(1)} %shard_map.43), channel_id=1, source_target_pairs={{0,1},{1,2},{2,3},{3,4},{4,5},{5,6},{6,7},{7,0},{8,9},{9,10},{10,1... | collective-permute-start | bytes 442376 | tf_op jit(solution)/shard_map/ppermute | solution.py:48
  133.8 5.8 %collective-permute-start.15 = (bf16[64,1152]{1,0:T(8,128)(2,1)S(1)}, bf16[64,1152]{1,0:T(8,128)(2,1)S(1)}, u32[]{:S(2)}, u32[]{:S(2)}) collective-permute-start(bf16[64,1152]{1,0:T(8,128)(2,1)S(1)} %shard_map.45), channel_id=1, source_target_pairs={{0,7},{1,0},{2,1},{3,2},{4,3},{5,4},{6,5},{7,6},{8,15},{9,8},{10,9... | collective-permute-start | bytes 442376 | tf_op jit(solution)/shard_map/ppermute | solution.py:48
  139.5 6.4 %collective-permute-start.12 = (bf16[64,1152]{1,0:T(8,128)(2,1)S(1)}, bf16[64,1152]{1,0:T(8,128)(2,1)S(1)}, u32[]{:S(2)}, u32[]{:S(2)}) collective-permute-start(bf16[64,1152]{1,0:T(8,128)(2,1)S(1)} %shard_map.44), channel_id=1, source_target_pairs={{0,1},{1,2},{2,3},{3,4},{4,5},{5,6},{6,7},{7,0},{8,9},{9,10},{10,1... | collective-permute-start | bytes 442376 | tf_op jit(solution)/shard_map/ppermute | solution.py:48
  139.7 6.2 %collective-permute-start.16 = (bf16[64,1152]{1,0:T(8,128)(2,1)S(1)}, bf16[64,1152]{1,0:T(8,128)(2,1)S(1)}, u32[]{:S(2)}, u32[]{:S(2)}) collective-permute-start(bf16[64,1152]{1,0:T(8,128)(2,1)S(1)} %shard_map.46), channel_id=1, source_target_pairs={{0,7},{1,0},{2,1},{3,2},{4,3},{5,4},{6,5},{7,6},{8,15},{9,8},{10,9... | collective-permute-start | bytes 442376 | tf_op jit(solution)/shard_map/ppermute | solution.py:48

commit v9 on v8

--- a/solution.py
+++ b/solution.py
@@ -17,7 +17,7 @@
 
 AXES = ("x", "yh", "core", "yl", "z")
 SIZES = (4, 2, 2, 2, 8)
-ROW_GROUP = ("core", "z")
+ROW_GROUP = ("z", "core")
 COL_GROUP = ("x", "yh", "yl")
 
 EPSILON = eps_factor * math.sqrt(WIDTH)
@@ -63,13 +63,10 @@
 
 
 def gather_z(shard):
-    ahead, behind = [shard], [shard]
-    for step in range(3):
-        if step == 2:
-            far = shift_out(ahead[2], 2)
-        ahead.append(shift_out(ahead[-1], 1))
-        behind.append(shift_out(behind[-1], -1))
-    return ahead[1], behind[1], ahead[2], behind[2], ahead[3], behind[3], far
+    ahead, behind = shift_out(shard, 1), shift_out(shard, -1)
+    ahead2, behind2 = shift_out(shard, 2), shift_out(shard, -2)
+    far = shift_out(ahead2, 2)
+    return ahead, behind, ahead2, behind2, shift_out(ahead2, 1), shift_out(behind2, -1), far
 
 
 FOUND = (-1, 1, -2, 2, -3, 3, 4)

time: 147 us -> 146 us (level)
  waiting for transfers between devices: 27.5 us -> 23.2 us
  blocking collectives: 66.7 us -> 69.1 us
    ppermute x7, waiting for transfers between devices: 15.1 us -> 10.9 us  [shift_out(): lax.ppermute(a, AXES, device_pairs(lambda x, yh, c, yl, z: (x, yh, c, yl,...]
    all_to_all x6, blocking collectives: 66.7 us -> 69.1 us  [spread(): return lax.all_to_all(copies, group, 0, 0)]
  transfers between devices with their start and end apart: 18 -> 18, of which waited for: 12 -> 10; matrix products, arithmetic and copies ran while one was open for 0% -> 0% of each run, Pallas kernels for 3% -> 3%
where the time goes in v9:
time: 146 us
  blocking collectives  69.1 us (47%)
  starting transfers between devices  36.5 us (25%)
  waiting for transfers between devices  23.2 us (16%)
  Pallas kernels  16.1 us (11%)
    all_to_all x6, blocking collectives, spread(): return lax.all_to_all(copies, group, 0, 0)  69.1 us
    pallas_call x17, Pallas kernels, run(): pl.pallas_call(kernel, out_shape=outs, in_specs=[pl.BlockSpec(memory_spac...  16.1 us
    ppermute x7, starting transfers between devices, shift_out(): lax.ppermute(a, AXES, device_pairs(lambda x, yh, c, yl, z: (x, yh, c, yl,...  14.5 us
    ppermute x8, starting transfers between devices, shift_z(): lax.ppermute(a, AXES, device_pairs(lambda x, yh, c, yl, z: (x, yh, c, yl,...  14.2 us
    ppermute x7, waiting for transfers between devices, shift_out(): lax.ppermute(a, AXES, device_pairs(lambda x, yh, c, yl, z: (x, yh, c, yl,...  10.9 us
    ppermute x8, waiting for transfers between devices, shift_z(): lax.ppermute(a, AXES, device_pairs(lambda x, yh, c, yl, z: (x, yh, c, yl,...  8.22 us
    all_to_all x1, starting transfers between devices, spread(): return lax.all_to_all(copies, group, 0, 0)  7.62 us
    ppermute x2, waiting for transfers between devices, swap_core(): lax.ppermute(a, AXES, device_pairs(lambda x, yh, c, yl, z: (x, yh, 1 - c,...  4.03 us
  transfers between devices with their start and end apart: 18, of which 10 were waited for; matrix products, arithmetic and copies ran while one was open for 0% of the time, Pallas kernels for 3%

profile of v9, /device:TPU:2, one launch (start us, length us, event | category | flops | bytes accessed | tf_op | source)
XLA Modules:
  0.0 145.9 jit_solution(7014743102766996310)
XLA Ops:
  2.4 7.6 %all-to-all-start = ((bf16[16,64,1024]{2,1,0:T(8,128)(2,1)}), bf16[16,64,1024]{2,1,0:T(8,128)(2,1)S(1)}, u32[]{:S(2)}, u32[]{:S(2)}) async-start(bf16[16,64,1024]{2,1,0:T(8,128)(2,1)} %shard_map.31), calls=%async_computation | async-start | bytes 4194304 | tf_op jit(solution)/shard_map/all_to_all | solution.py:56
  10.0 25.4 %conditional.1 = (bf16[64,1024]{1,0:T(8,128)(2,1)}, bf16[64,1024]{1,0:T(8,128)(2,1)}, bf16[64,1024]{1,0:T(8,128)(2,1)}, bf16[64,1024]{1,0:T(8,128)(2,1)}, bf16[6...) conditional(s32[]{:T(128)} %convert_element_type.3, () %tuple.13, ...), branch_computations={%region_0.0_spmd, %region_1.0_spmd} | conditional | bytes 3670352 | solution.py:336
  10.0 6.4 %collective-permute-start.3 = (bf16[64,1024]{1,0:T(8,128)(2,1)S(1)}, bf16[64,1024]{1,0:T(8,128)(2,1)}, u32[]{:S(2)}, u32[]{:S(2)}) collective-permute-start(bf16[64,1024]{1,0:T(8,128)(2,1)S(1)} %param.1), channel_id=1, source_target_pairs={{0,6},{1,7},{2,0},{3,1},{4,2},{5,3},{6,4},{7,5},{8,14},{9,15},{10,... | collective-permute-start | bytes 393224 | tf_op jit(solution)/shard_map/cond/branch_1_fun/ppermute | solution.py:60
  16.4 3.7 %collective-permute-start.1 = (bf16[64,1024]{1,0:T(8,128)(2,1)S(1)}, bf16[64,1024]{1,0:T(8,128)(2,1)}, u32[]{:S(2)}, u32[]{:S(2)}) collective-permute-start(bf16[64,1024]{1,0:T(8,128)(2,1)S(1)} %param.1), channel_id=1, source_target_pairs={{0,7},{1,0},{2,1},{3,2},{4,3},{5,4},{6,5},{7,6},{8,15},{9,8},{10,9... | collective-permute-start | bytes 393224 | tf_op jit(solution)/shard_map/cond/branch_1_fun/ppermute | solution.py:60
  20.1 2.2 %collective-permute-done.3 = bf16[64,1024]{1,0:T(8,128)(2,1)} collective-permute-done((bf16[64,1024]{1,0:T(8,128)(2,1)S(1)}, bf16[64,1024]{1,0:T(8,128)(2,1)}, u32[]{:S(2)}, u32[]{:S(2)}) %collective-permute-start.3) | collective-permute-done | bytes 131104 | tf_op jit(solution)/shard_map/cond/branch_1_fun/ppermute | solution.py:60
  22.3 3.3 %collective-permute-start.5 = (bf16[64,1024]{1,0:T(8,128)(2,1)}, bf16[64,1024]{1,0:T(8,128)(2,1)}, u32[]{:S(2)}, u32[]{:S(2)}) collective-permute-start(bf16[64,1024]{1,0:T(8,128)(2,1)} %collective-permute-done.3), channel_id=1, source_target_pairs={{0,7},{1,0},{2,1},{3,2},{4,3},{5,4},{6,5},{7,6},{8,15},{9,8},{10,9... | collective-permute-start | bytes 393224 | tf_op jit(solution)/shard_map/cond/branch_1_fun/ppermute | solution.py:60
  27.4 3.0 %collective-permute-done.5 = bf16[64,1024]{1,0:T(8,128)(2,1)} collective-permute-done((bf16[64,1024]{1,0:T(8,128)(2,1)}, bf16[64,1024]{1,0:T(8,128)(2,1)}, u32[]{:S(2)}, u32[]{:S(2)}) %collective-permute-start.5) | collective-permute-done | bytes 131104 | tf_op jit(solution)/shard_map/cond/branch_1_fun/ppermute | solution.py:60
  30.3 4.1 %collective-permute-done.6 = bf16[64,1024]{1,0:T(8,128)(2,1)} collective-permute-done((bf16[64,1024]{1,0:T(8,128)(2,1)}, bf16[64,1024]{1,0:T(8,128)(2,1)}, u32[]{:S(2)}, u32[]{:S(2)}) %collective-permute-start.6) | collective-permute-done | bytes 131104 | tf_op jit(solution)/shard_map/cond/branch_1_fun/ppermute | solution.py:60
  37.0 2.8 %collective-permute-done.7.far_ref = bf16[512,1024]{1,0:T(8,128)(2,1)} collective-permute-done((bf16[512,1024]{1,0:T(8,128)(2,1)S(1)}, bf16[512,1024]{1,0:T(8,128)(2,1)}, u32[]{:S(2)}, u32[]{:S(2)}) %collective-permute-start.7) | collective-permute-done | bytes 1048608 | tf_op jit(solution)/shard_map/ppermute | solution.py:52
  39.8 3.7 %shard_map.33 = (f32[1024,1024]{1,0:T(8,128)S(1)}, f32[16,8,128]{2,1,0:T(8,128)S(1)}) custom-call(bf16[1024,1024]{1,0:T(8,128)(2,1)S(1)} %bitcast.1, bf16[512,1024]{1,0:T(8,128)(2,1)S(1)} %shard_map.32.own_ref, bf16[512,1024]{1,0:T(8,128)(2,1)} %collective-permute-done.7.far_ref), custom_call_target="tpu_custom_call" | custom-call | flops 2147483648 | bytes 4194304 | tf_op jit(solution)/shard_map/pallas_call | solution.py:307
  43.5 13.6 %all_to_all.35.in_ref = f32[16,8,128]{2,1,0:T(8,128)S(1)} all-to-all(f32[16,8,128]{2,1,0:T(8,128)S(1)} %get-tuple-element.33), channel_id=1, replica_groups=mesh['x'=4,'yh'=2,'core'=2,'yl'=2,'z'=8] {'z','core'}, dimensions={0} | all-to-all | bytes 131072 | tf_op jit(solution)/shard_map/all_to_all | solution.py:56
  58.3 12.9 %all_to_all.36.in_ref = f32[16,8,128]{2,1,0:T(8,128)S(1)} all-to-all(f32[16,8,128]{2,1,0:T(8,128)S(1)} %get-tuple-element.35), channel_id=1, replica_groups=mesh['x'=4,'yh'=2,'core'=2,'yl'=2,'z'=8] {'x','yh','yl'}, dimensions={0} | all-to-all | bytes 131072 | tf_op jit(solution)/shard_map/all_to_all | solution.py:56
  72.1 10.4 %all_to_all.37.in_ref = f32[16,8,128]{2,1,0:T(8,128)S(1)} all-to-all(f32[16,8,128]{2,1,0:T(8,128)S(1)} %get-tuple-element.37), channel_id=1, replica_groups=mesh['x'=4,'yh'=2,'core'=2,'yl'=2,'z'=8] {'z','core'}, dimensions={0} | all-to-all | bytes 131072 | tf_op jit(solution)/shard_map/all_to_all | solution.py:56
  83.2 10.9 %all_to_all.38.in_ref = f32[16,8,128]{2,1,0:T(8,128)S(1)} all-to-all(f32[16,8,128]{2,1,0:T(8,128)S(1)} %shard_map.36), channel_id=1, replica_groups=mesh['x'=4,'yh'=2,'core'=2,'yl'=2,'z'=8] {'x','yh','yl'}, dimensions={0} | all-to-all | bytes 131072 | tf_op jit(solution)/shard_map/all_to_all | solution.py:56
  94.5 10.4 %all_to_all.39.in_ref = f32[16,8,128]{2,1,0:T(8,128)S(1)} all-to-all(f32[16,8,128]{2,1,0:T(8,128)S(1)} %shard_map.37), channel_id=1, replica_groups=mesh['x'=4,'yh'=2,'core'=2,'yl'=2,'z'=8] {'z','core'}, dimensions={0} | all-to-all | bytes 131072 | tf_op jit(solution)/shard_map/all_to_all | solution.py:56
  105.5 10.9 %all_to_all.40.in_ref = f32[16,8,128]{2,1,0:T(8,128)S(1)} all-to-all(f32[16,8,128]{2,1,0:T(8,128)S(1)} %shard_map.38), channel_id=1, replica_groups=mesh['x'=4,'yh'=2,'core'=2,'yl'=2,'z'=8] {'x','yh','yl'}, dimensions={0} | all-to-all | bytes 131072 | tf_op jit(solution)/shard_map/all_to_all | solution.py:56
  116.4 2.2 %shard_map.39 = (bf16[1024,1024]{1,0:T(8,128)(2,1)S(1)}, bf16[512,1152]{1,0:T(8,128)(2,1)S(1)}) custom-call(bf16[1024,1024]{1,0:T(8,128)(2,1)S(1)} %get-tuple-element.36.plan_ref, f32[16,8,128]{2,1,0:T(8,128)S(1)} %all_to_all.40.in_ref, bf16[1024,1024]{1,0:T(8,128)(2,1)S(1)} %bitcast.2), custom_call_target="tpu_custom_call" | custom-call | flops 1073741824 | bytes 4194304 | tf_op jit(solution)/shard_map/pallas_call | solution.py:307
  122.5 2.6 %collective-permute-start.13 = (bf16[64,1152]{1,0:T(8,128)(2,1)S(1)}, bf16[64,1152]{1,0:T(8,128)(2,1)S(1)}, u32[]{:S(2)}, u32[]{:S(2)}) collective-permute-start(bf16[64,1152]{1,0:T(8,128)(2,1)S(1)} %get-tuple-element.42), channel_id=1, source_target_pairs={{0,7},{1,0},{2,1},{3,2},{4,3},{5,4},{6,5},{7,6},{8,15},{9,8},{10,9... | collective-permute-start | bytes 442376 | tf_op jit(solution)/shard_map/ppermute | solution.py:48
  125.1 4.1 %collective-permute-start.14 = (bf16[32,1152]{1,0:T(8,128)(2,1)S(1)}, bf16[32,1152]{1,0:T(8,128)(2,1)S(1)}, u32[]{:S(2)}, u32[]{:S(2)}) collective-permute-start(bf16[32,1152]{1,0:T(8,128)(2,1)S(1)} %get-tuple-element.43), channel_id=1, source_target_pairs={{0,6},{1,7},{2,0},{3,1},{4,2},{5,3},{6,4},{7,5},{8,14},{9,15},{10,... | collective-permute-start | bytes 221192 | tf_op jit(solution)/shard_map/ppermute | solution.py:48
  129.5 2.4 %collective-permute-done.10.far_ref = bf16[32,1152]{1,0:T(8,128)(2,1)S(1)} collective-permute-done((bf16[32,1152]{1,0:T(8,128)(2,1)S(1)}, bf16[32,1152]{1,0:T(8,128)(2,1)S(1)}, u32[]{:S(2)}, u32[]{:S(2)}) %collective-permute-start.10) | collective-permute-done | bytes 73760 | tf_op jit(solution)/shard_map/ppermute | solution.py:48
  132.1 1.7 %collective-permute-start.11 = (bf16[64,1152]{1,0:T(8,128)(2,1)S(1)}, bf16[64,1152]{1,0:T(8,128)(2,1)S(1)}, u32[]{:S(2)}, u32[]{:S(2)}) collective-permute-start(bf16[64,1152]{1,0:T(8,128)(2,1)S(1)} %shard_map.43), channel_id=1, source_target_pairs={{0,1},{1,2},{2,3},{3,4},{4,5},{5,6},{6,7},{7,0},{8,9},{9,10},{10,1... | collective-permute-start | bytes 442376 | tf_op jit(solution)/shard_map/ppermute | solution.py:48
  135.6 2.9 %collective-permute-done.11.got_ref = bf16[64,1152]{1,0:T(8,128)(2,1)S(1)} collective-permute-done((bf16[64,1152]{1,0:T(8,128)(2,1)S(1)}, bf16[64,1152]{1,0:T(8,128)(2,1)S(1)}, u32[]{:S(2)}, u32[]{:S(2)}) %collective-permute-start.11) | collective-permute-done | bytes 147488 | tf_op jit(solution)/shard_map/ppermute | solution.py:48
  139.3 2.9 %collective-permute-start.16 = (bf16[64,1152]{1,0:T(8,128)(2,1)S(1)}, bf16[64,1152]{1,0:T(8,128)(2,1)S(1)}, u32[]{:S(2)}, u32[]{:S(2)}) collective-permute-start(bf16[64,1152]{1,0:T(8,128)(2,1)S(1)} %shard_map.46), channel_id=1, source_target_pairs={{0,7},{1,0},{2,1},{3,2},{4,3},{5,4},{6,5},{7,6},{8,15},{9,8},{10,9... | collective-permute-start | bytes 442376 | tf_op jit(solution)/shard_map/ppermute | solution.py:48
  142.1 2.9 %collective-permute-done.12.right_ref = bf16[64,1152]{1,0:T(8,128)(2,1)S(1)} collective-permute-done((bf16[64,1152]{1,0:T(8,128)(2,1)S(1)}, bf16[64,1152]{1,0:T(8,128)(2,1)S(1)}, u32[]{:S(2)}, u32[]{:S(2)}) %collective-permute-start.12) | collective-permute-done | bytes 147488 | tf_op jit(solution)/shard_map/ppermute | solution.py:48
  (40 shorter events, 18.2 us)
Async XLA Ops:
  0.0 0.9 copy-start
  2.4 7.6 %copy-start.1 = (bf16[64,1024]{1,0:T(8,128)(2,1)S(1)}, bf16[64,1024]{1,0:T(8,128)(2,1)}, u32[]{:S(2)}) copy-start(bf16[64,1024]{1,0:T(8,128)(2,1)} %noise_ref.1) | copy-start | bytes 393220
  2.4 37.4 %all-to-all-start = ((bf16[16,64,1024]{2,1,0:T(8,128)(2,1)}), bf16[16,64,1024]{2,1,0:T(8,128)(2,1)S(1)}, u32[]{:S(2)}, u32[]{:S(2)}) async-start(bf16[16,64,1024]{2,1,0:T(8,128)(2,1)} %shard_map.31), calls=%async_computation | async-start | bytes 4194304 | tf_op jit(solution)/shard_map/all_to_all | solution.py:56
  10.0 12.3 %collective-permute-start.3 = (bf16[64,1024]{1,0:T(8,128)(2,1)S(1)}, bf16[64,1024]{1,0:T(8,128)(2,1)}, u32[]{:S(2)}, u32[]{:S(2)}) collective-permute-start(bf16[64,1024]{1,0:T(8,128)(2,1)S(1)} %param.1), channel_id=1, source_target_pairs={{0,6},{1,7},{2,0},{3,1},{4,2},{5,3},{6,4},{7,5},{8,14},{9,15},{10,... | collective-permute-start | bytes 393224 | tf_op jit(solution)/shard_map/cond/branch_1_fun/ppermute | solution.py:60
  16.4 9.2 %collective-permute-start.2 = (bf16[64,1024]{1,0:T(8,128)(2,1)S(1)}, bf16[64,1024]{1,0:T(8,128)(2,1)}, u32[]{:S(2)}, u32[]{:S(2)}) collective-permute-start(bf16[64,1024]{1,0:T(8,128)(2,1)S(1)} %param.1), channel_id=1, source_target_pairs={{0,2},{1,3},{2,4},{3,5},{4,6},{5,7},{6,0},{7,1},{8,10},{9,11},{10,... | collective-permute-start | bytes 393224 | tf_op jit(solution)/shard_map/cond/branch_1_fun/ppermute | solution.py:60
  16.4 10.3 %collective-permute-start.1 = (bf16[64,1024]{1,0:T(8,128)(2,1)S(1)}, bf16[64,1024]{1,0:T(8,128)(2,1)}, u32[]{:S(2)}, u32[]{:S(2)}) collective-permute-start(bf16[64,1024]{1,0:T(8,128)(2,1)S(1)} %param.1), channel_id=1, source_target_pairs={{0,7},{1,0},{2,1},{3,2},{4,3},{5,4},{6,5},{7,6},{8,15},{9,8},{10,9... | collective-permute-start | bytes 393224 | tf_op jit(solution)/shard_map/cond/branch_1_fun/ppermute | solution.py:60
  20.1 7.3 %collective-permute-start = (bf16[64,1024]{1,0:T(8,128)(2,1)S(1)}, bf16[64,1024]{1,0:T(8,128)(2,1)}, u32[]{:S(2)}, u32[]{:S(2)}) collective-permute-start(bf16[64,1024]{1,0:T(8,128)(2,1)S(1)} %param.1), channel_id=1, source_target_pairs={{0,1},{1,2},{2,3},{3,4},{4,5},{5,6},{6,7},{7,0},{8,9},{9,10},{10,1... | collective-permute-start | bytes 393224 | tf_op jit(solution)/shard_map/cond/branch_1_fun/ppermute | solution.py:60
  22.3 8.0 %collective-permute-start.5 = (bf16[64,1024]{1,0:T(8,128)(2,1)}, bf16[64,1024]{1,0:T(8,128)(2,1)}, u32[]{:S(2)}, u32[]{:S(2)}) collective-permute-start(bf16[64,1024]{1,0:T(8,128)(2,1)} %collective-permute-done.3), channel_id=1, source_target_pairs={{0,7},{1,0},{2,1},{3,2},{4,3},{5,4},{6,5},{7,6},{8,15},{9,8},{10,9... | collective-permute-start | bytes 393224 | tf_op jit(solution)/shard_map/cond/branch_1_fun/ppermute | solution.py:60
  25.6 8.9 %collective-permute-start.6 = (bf16[64,1024]{1,0:T(8,128)(2,1)}, bf16[64,1024]{1,0:T(8,128)(2,1)}, u32[]{:S(2)}, u32[]{:S(2)}) collective-permute-start(bf16[64,1024]{1,0:T(8,128)(2,1)} %collective-permute-done.2), channel_id=1, source_target_pairs={{0,2},{1,3},{2,4},{3,5},{4,6},{5,7},{6,0},{7,1},{8,10},{9,11},{10,... | collective-permute-start | bytes 393224 | tf_op jit(solution)/shard_map/cond/branch_1_fun/ppermute | solution.py:60
  25.6 9.9 %collective-permute-start.4 = (bf16[64,1024]{1,0:T(8,128)(2,1)}, bf16[64,1024]{1,0:T(8,128)(2,1)}, u32[]{:S(2)}, u32[]{:S(2)}) collective-permute-start(bf16[64,1024]{1,0:T(8,128)(2,1)} %collective-permute-done.2), channel_id=1, source_target_pairs={{0,1},{1,2},{2,3},{3,4},{4,5},{5,6},{6,7},{7,0},{8,9},{9,10},{10,1... | collective-permute-start | bytes 393224 | tf_op jit(solution)/shard_map/cond/branch_1_fun/ppermute | solution.py:60
  36.9 2.9 %collective-permute-start.7 = (bf16[512,1024]{1,0:T(8,128)(2,1)S(1)}, bf16[512,1024]{1,0:T(8,128)(2,1)}, u32[]{:S(2)}, u32[]{:S(2)}) collective-permute-start(bf16[512,1024]{1,0:T(8,128)(2,1)S(1)} %shard_map.32.own_ref), channel_id=1, source_target_pairs={{0,16},{1,17},{2,18},{3,19},{4,20},{5,21},{6,22},{7,23},{8,24},{9,... | collective-permute-start | bytes 3145736 | tf_op jit(solution)/shard_map/ppermute | solution.py:52
  118.6 2.9 %collective-permute-start.8 = (bf16[512,1152]{1,0:T(8,128)(2,1)S(1)}, bf16[512,1152]{1,0:T(8,128)(2,1)S(1)}, u32[]{:S(2)}, u32[]{:S(2)}) collective-permute-start(bf16[512,1152]{1,0:T(8,128)(2,1)S(1)} %get-tuple-element.39), channel_id=1, source_target_pairs={{0,16},{1,17},{2,18},{3,19},{4,20},{5,21},{6,22},{7,23},{8,24},{9,... | collective-permute-start | bytes 3538952 | tf_op jit(solution)/shard_map/ppermute | solution.py:52
  121.7 10.2 %collective-permute-start.9 = (bf16[64,1152]{1,0:T(8,128)(2,1)S(1)}, bf16[64,1152]{1,0:T(8,128)(2,1)S(1)}, u32[]{:S(2)}, u32[]{:S(2)}) collective-permute-start(bf16[64,1152]{1,0:T(8,128)(2,1)S(1)} %get-tuple-element.40), channel_id=1, source_target_pairs={{0,1},{1,2},{2,3},{3,4},{4,5},{5,6},{6,7},{7,0},{8,9},{9,10},{10,1... | collective-permute-start | bytes 442376 | tf_op jit(solution)/shard_map/ppermute | solution.py:48
  122.5 11.3 %collective-permute-start.13 = (bf16[64,1152]{1,0:T(8,128)(2,1)S(1)}, bf16[64,1152]{1,0:T(8,128)(2,1)S(1)}, u32[]{:S(2)}, u32[]{:S(2)}) collective-permute-start(bf16[64,1152]{1,0:T(8,128)(2,1)S(1)} %get-tuple-element.42), channel_id=1, source_target_pairs={{0,7},{1,0},{2,1},{3,2},{4,3},{5,4},{6,5},{7,6},{8,15},{9,8},{10,9... | collective-permute-start | bytes 442376 | tf_op jit(solution)/shard_map/ppermute | solution.py:48
  125.1 6.8 %collective-permute-start.10 = (bf16[32,1152]{1,0:T(8,128)(2,1)S(1)}, bf16[32,1152]{1,0:T(8,128)(2,1)S(1)}, u32[]{:S(2)}, u32[]{:S(2)}) collective-permute-start(bf16[32,1152]{1,0:T(8,128)(2,1)S(1)} %get-tuple-element.41), channel_id=1, source_target_pairs={{0,2},{1,3},{2,4},{3,5},{4,6},{5,7},{6,0},{7,1},{8,10},{9,11},{10,... | collective-permute-start | bytes 221192 | tf_op jit(solution)/shard_map/ppermute | solution.py:48
  125.1 8.7 %collective-permute-start.14 = (bf16[32,1152]{1,0:T(8,128)(2,1)S(1)}, bf16[32,1152]{1,0:T(8,128)(2,1)S(1)}, u32[]{:S(2)}, u32[]{:S(2)}) collective-permute-start(bf16[32,1152]{1,0:T(8,128)(2,1)S(1)} %get-tuple-element.43), channel_id=1, source_target_pairs={{0,6},{1,7},{2,0},{3,1},{4,2},{5,3},{6,4},{7,5},{8,14},{9,15},{10,... | collective-permute-start | bytes 221192 | tf_op jit(solution)/shard_map/ppermute | solution.py:48
  132.1 6.4 %collective-permute-start.11 = (bf16[64,1152]{1,0:T(8,128)(2,1)S(1)}, bf16[64,1152]{1,0:T(8,128)(2,1)S(1)}, u32[]{:S(2)}, u32[]{:S(2)}) collective-permute-start(bf16[64,1152]{1,0:T(8,128)(2,1)S(1)} %shard_map.43), channel_id=1, source_target_pairs={{0,1},{1,2},{2,3},{3,4},{4,5},{5,6},{6,7},{7,0},{8,9},{9,10},{10,1... | collective-permute-start | bytes 442376 | tf_op jit(solution)/shard_map/ppermute | solution.py:48
  133.9 5.2 %collective-permute-start.15 = (bf16[64,1152]{1,0:T(8,128)(2,1)S(1)}, bf16[64,1152]{1,0:T(8,128)(2,1)S(1)}, u32[]{:S(2)}, u32[]{:S(2)}) collective-permute-start(bf16[64,1152]{1,0:T(8,128)(2,1)S(1)} %shard_map.45), channel_id=1, source_target_pairs={{0,7},{1,0},{2,1},{3,2},{4,3},{5,4},{6,5},{7,6},{8,15},{9,8},{10,9... | collective-permute-start | bytes 442376 | tf_op jit(solution)/shard_map/ppermute | solution.py:48
  138.6 6.4 %collective-permute-start.12 = (bf16[64,1152]{1,0:T(8,128)(2,1)S(1)}, bf16[64,1152]{1,0:T(8,128)(2,1)S(1)}, u32[]{:S(2)}, u32[]{:S(2)}) collective-permute-start(bf16[64,1152]{1,0:T(8,128)(2,1)S(1)} %shard_map.44), channel_id=1, source_target_pairs={{0,1},{1,2},{2,3},{3,4},{4,5},{5,6},{6,7},{7,0},{8,9},{9,10},{10,1... | collective-permute-start | bytes 442376 | tf_op jit(solution)/shard_map/ppermute | solution.py:48
  139.3 5.8 %collective-permute-start.16 = (bf16[64,1152]{1,0:T(8,128)(2,1)S(1)}, bf16[64,1152]{1,0:T(8,128)(2,1)S(1)}, u32[]{:S(2)}, u32[]{:S(2)}) collective-permute-start(bf16[64,1152]{1,0:T(8,128)(2,1)S(1)} %shard_map.46), channel_id=1, source_target_pairs={{0,7},{1,0},{2,1},{3,2},{4,3},{5,4},{6,5},{7,6},{8,15},{9,8},{10,9... | collective-permute-start | bytes 442376 | tf_op jit(solution)/shard_map/ppermute | solution.py:48

commit v10 on v9

--- a/solution.py
+++ b/solution.py
@@ -96,7 +96,11 @@
 
 
 def send(out_ref, square):
-    out_ref[...] = jnp.broadcast_to(square[None], (16, 8, 128))
+    out_ref[...] = jnp.broadcast_to(square[None], (16, 8, 128)).astype(out_ref.dtype)
+
+
+def received(in_ref):
+    return jnp.sum(in_ref[...].astype(jnp.float32), axis=0)
 
 
 def terms(lanes):
@@ -174,7 +178,7 @@
 
 
 def column_sums_kernel(plan_ref, in_ref, out_ref):
-    scale = own_first(1.0 / jnp.sum(in_ref[...], axis=0))
+    scale = own_first(1.0 / received(in_ref))
     sums = lax.dot_general(
         terms(to_lanes(scale)),
         plan_ref[...],
@@ -185,7 +189,7 @@
 
 
 def row_sums_kernel(plan_ref, in_ref, out_ref):
-    scale = 1.0 / jnp.sum(in_ref[...], axis=0)
+    scale = 1.0 / received(in_ref)
     sums = jnp.dot(terms(to_lanes(scale)), plan_ref[...], preferred_element_type=jnp.float32)
     send(out_ref, own_first(to_square(sums[0:1, :] + sums[1:2, :])))
 
@@ -239,7 +243,7 @@
 
 
 def other_targets_kernel(plan_ref, in_ref, data_ref, weight_ref, out_ref):
-    scale = 1.0 / jnp.sum(in_ref[...], axis=0)
+    scale = 1.0 / received(in_ref)
     for k in range(8):
         part = pl.ds(128 * k, 128)
         weights = plan_ref[part, :].astype(jnp.float32) * down(scale[k : k + 1, :])
@@ -296,6 +300,7 @@
 
 SQUARE = jax.ShapeDtypeStruct((8, 128), jnp.float32)
 COPIES = jax.ShapeDtypeStruct((16, 8, 128), jnp.float32)
+SUMS = jax.ShapeDtypeStruct((16, 8, 128), jnp.bfloat16)
 
 
 def in_vmem(rows, dtype):
@@ -360,15 +365,15 @@
     row_dual, parts = run(columns_kernel, (SQUARE, COPIES), scores, spread(parts, ROW_GROUP))
     plan, parts = run(
         plan_kernel,
-        (in_vmem(ROWS, jnp.bfloat16), COPIES),
+        (in_vmem(ROWS, jnp.bfloat16), SUMS),
         scores,
         row_dual,
         spread(parts, COL_GROUP),
     )
     plan = keep(plan)
-    parts = run(column_sums_kernel, COPIES, plan, spread(parts, ROW_GROUP))
-    parts = run(row_sums_kernel, COPIES, plan, spread(parts, COL_GROUP))
-    parts = run(column_sums_kernel, COPIES, plan, spread(parts, ROW_GROUP))
+    parts = run(column_sums_kernel, SUMS, plan, spread(parts, ROW_GROUP))
+    parts = run(row_sums_kernel, SUMS, plan, spread(parts, COL_GROUP))
+    parts = run(column_sums_kernel, SUMS, plan, spread(parts, ROW_GROUP))
     weights, others = run(
         other_targets_kernel,
         (in_vmem(ROWS, jnp.bfloat16), sent_rows(ROWS // 2)),

time: 146 us -> 146 us (level)
  no operation moved by 1% of the time
where the time goes in v10:
time: 146 us; the launch traced here: 145 us
  blocking collectives  68.6 us (47%)
  starting transfers between devices  36.4 us (25%)
  waiting for transfers between devices  23.2 us (16%)
  Pallas kernels  16 us (11%)
    all_to_all x6, blocking collectives, spread(): return lax.all_to_all(copies, group, 0, 0)  68.6 us
    pallas_call x17, Pallas kernels, run(): pl.pallas_call(kernel, out_shape=outs, in_specs=[pl.BlockSpec(memory_spac...  16 us
    ppermute x7, starting transfers between devices, shift_out(): lax.ppermute(a, AXES, device_pairs(lambda x, yh, c, yl, z: (x, yh, c, yl,...  14.5 us
    ppermute x8, starting transfers between devices, shift_z(): lax.ppermute(a, AXES, device_pairs(lambda x, yh, c, yl, z: (x, yh, c, yl,...  14.1 us
    ppermute x7, waiting for transfers between devices, shift_out(): lax.ppermute(a, AXES, device_pairs(lambda x, yh, c, yl, z: (x, yh, c, yl,...  10.9 us
    ppermute x8, waiting for transfers between devices, shift_z(): lax.ppermute(a, AXES, device_pairs(lambda x, yh, c, yl, z: (x, yh, c, yl,...  8.21 us
    all_to_all x1, starting transfers between devices, spread(): return lax.all_to_all(copies, group, 0, 0)  7.62 us
    ppermute x2, waiting for transfers between devices, swap_core(): lax.ppermute(a, AXES, device_pairs(lambda x, yh, c, yl, z: (x, yh, 1 - c,...  4.03 us
  transfers between devices with their start and end apart: 18, of which 10 were waited for; matrix products, arithmetic and copies ran while one was open for 0% of the time, Pallas kernels for 3%

profile of v10, /device:TPU:2, one launch (start us, length us, event | category | flops | bytes accessed | tf_op | source)
XLA Modules:
  0.0 145.3 jit_solution(11013522741073226311)
XLA Ops:
  2.4 7.6 %all-to-all-start = ((bf16[16,64,1024]{2,1,0:T(8,128)(2,1)}), bf16[16,64,1024]{2,1,0:T(8,128)(2,1)S(1)}, u32[]{:S(2)}, u32[]{:S(2)}) async-start(bf16[16,64,1024]{2,1,0:T(8,128)(2,1)} %shard_map.31), calls=%async_computation | async-start | bytes 4194304 | tf_op jit(solution)/shard_map/all_to_all | solution.py:56
  10.0 25.4 %conditional.1 = (bf16[64,1024]{1,0:T(8,128)(2,1)}, bf16[64,1024]{1,0:T(8,128)(2,1)}, bf16[64,1024]{1,0:T(8,128)(2,1)}, bf16[64,1024]{1,0:T(8,128)(2,1)}, bf16[6...) conditional(s32[]{:T(128)} %convert_element_type.3, () %tuple.13, ...), branch_computations={%region_0.0_spmd, %region_1.0_spmd} | conditional | bytes 3670352 | solution.py:341
  10.0 6.4 %collective-permute-start.3 = (bf16[64,1024]{1,0:T(8,128)(2,1)S(1)}, bf16[64,1024]{1,0:T(8,128)(2,1)}, u32[]{:S(2)}, u32[]{:S(2)}) collective-permute-start(bf16[64,1024]{1,0:T(8,128)(2,1)S(1)} %param.1), channel_id=1, source_target_pairs={{0,6},{1,7},{2,0},{3,1},{4,2},{5,3},{6,4},{7,5},{8,14},{9,15},{10,... | collective-permute-start | bytes 393224 | tf_op jit(solution)/shard_map/cond/branch_1_fun/ppermute | solution.py:60
  16.4 3.7 %collective-permute-start.1 = (bf16[64,1024]{1,0:T(8,128)(2,1)S(1)}, bf16[64,1024]{1,0:T(8,128)(2,1)}, u32[]{:S(2)}, u32[]{:S(2)}) collective-permute-start(bf16[64,1024]{1,0:T(8,128)(2,1)S(1)} %param.1), channel_id=1, source_target_pairs={{0,7},{1,0},{2,1},{3,2},{4,3},{5,4},{6,5},{7,6},{8,15},{9,8},{10,9... | collective-permute-start | bytes 393224 | tf_op jit(solution)/shard_map/cond/branch_1_fun/ppermute | solution.py:60
  20.1 2.2 %collective-permute-done.3 = bf16[64,1024]{1,0:T(8,128)(2,1)} collective-permute-done((bf16[64,1024]{1,0:T(8,128)(2,1)S(1)}, bf16[64,1024]{1,0:T(8,128)(2,1)}, u32[]{:S(2)}, u32[]{:S(2)}) %collective-permute-start.3) | collective-permute-done | bytes 131104 | tf_op jit(solution)/shard_map/cond/branch_1_fun/ppermute | solution.py:60
  22.3 3.3 %collective-permute-start.5 = (bf16[64,1024]{1,0:T(8,128)(2,1)}, bf16[64,1024]{1,0:T(8,128)(2,1)}, u32[]{:S(2)}, u32[]{:S(2)}) collective-permute-start(bf16[64,1024]{1,0:T(8,128)(2,1)} %collective-permute-done.3), channel_id=1, source_target_pairs={{0,7},{1,0},{2,1},{3,2},{4,3},{5,4},{6,5},{7,6},{8,15},{9,8},{10,9... | collective-permute-start | bytes 393224 | tf_op jit(solution)/shard_map/cond/branch_1_fun/ppermute | solution.py:60
  27.4 3.0 %collective-permute-done.5 = bf16[64,1024]{1,0:T(8,128)(2,1)} collective-permute-done((bf16[64,1024]{1,0:T(8,128)(2,1)}, bf16[64,1024]{1,0:T(8,128)(2,1)}, u32[]{:S(2)}, u32[]{:S(2)}) %collective-permute-start.5) | collective-permute-done | bytes 131104 | tf_op jit(solution)/shard_map/cond/branch_1_fun/ppermute | solution.py:60
  30.3 4.1 %collective-permute-done.6 = bf16[64,1024]{1,0:T(8,128)(2,1)} collective-permute-done((bf16[64,1024]{1,0:T(8,128)(2,1)}, bf16[64,1024]{1,0:T(8,128)(2,1)}, u32[]{:S(2)}, u32[]{:S(2)}) %collective-permute-start.6) | collective-permute-done | bytes 131104 | tf_op jit(solution)/shard_map/cond/branch_1_fun/ppermute | solution.py:60
  37.0 2.8 %collective-permute-done.7.far_ref = bf16[512,1024]{1,0:T(8,128)(2,1)} collective-permute-done((bf16[512,1024]{1,0:T(8,128)(2,1)S(1)}, bf16[512,1024]{1,0:T(8,128)(2,1)}, u32[]{:S(2)}, u32[]{:S(2)}) %collective-permute-start.7) | collective-permute-done | bytes 1048608 | tf_op jit(solution)/shard_map/ppermute | solution.py:52
  39.8 3.7 %shard_map.33 = (f32[1024,1024]{1,0:T(8,128)S(1)}, f32[16,8,128]{2,1,0:T(8,128)S(1)}) custom-call(bf16[1024,1024]{1,0:T(8,128)(2,1)S(1)} %bitcast.1, bf16[512,1024]{1,0:T(8,128)(2,1)S(1)} %shard_map.32.own_ref, bf16[512,1024]{1,0:T(8,128)(2,1)} %collective-permute-done.7.far_ref), custom_call_target="tpu_custom_call" | custom-call | flops 2147483648 | bytes 4194304 | tf_op jit(solution)/shard_map/pallas_call | solution.py:312
  43.5 13.6 %all_to_all.35.in_ref = f32[16,8,128]{2,1,0:T(8,128)S(1)} all-to-all(f32[16,8,128]{2,1,0:T(8,128)S(1)} %get-tuple-element.33), channel_id=1, replica_groups=mesh['x'=4,'yh'=2,'core'=2,'yl'=2,'z'=8] {'z','core'}, dimensions={0} | all-to-all | bytes 131072 | tf_op jit(solution)/shard_map/all_to_all | solution.py:56
  58.3 12.9 %all_to_all.36.in_ref = f32[16,8,128]{2,1,0:T(8,128)S(1)} all-to-all(f32[16,8,128]{2,1,0:T(8,128)S(1)} %get-tuple-element.35), channel_id=1, replica_groups=mesh['x'=4,'yh'=2,'core'=2,'yl'=2,'z'=8] {'x','yh','yl'}, dimensions={0} | all-to-all | bytes 131072 | tf_op jit(solution)/shard_map/all_to_all | solution.py:56
  72.1 10.3 %all_to_all.37.in_ref = bf16[16,8,128]{2,1,0:T(8,128)(2,1)S(1)} all-to-all(bf16[16,8,128]{2,1,0:T(8,128)(2,1)S(1)} %get-tuple-element.37), channel_id=1, replica_groups=mesh['x'=4,'yh'=2,'core'=2,'yl'=2,'z'=8] {'z','core'}, dimensions={0} | all-to-all | bytes 65536 | tf_op jit(solution)/shard_map/all_to_all | solution.py:56
  83.0 10.9 %all_to_all.38.in_ref = bf16[16,8,128]{2,1,0:T(8,128)(2,1)S(1)} all-to-all(bf16[16,8,128]{2,1,0:T(8,128)(2,1)S(1)} %shard_map.36), channel_id=1, replica_groups=mesh['x'=4,'yh'=2,'core'=2,'yl'=2,'z'=8] {'x','yh','yl'}, dimensions={0} | all-to-all | bytes 65536 | tf_op jit(solution)/shard_map/all_to_all | solution.py:56
  94.3 10.3 %all_to_all.39.in_ref = bf16[16,8,128]{2,1,0:T(8,128)(2,1)S(1)} all-to-all(bf16[16,8,128]{2,1,0:T(8,128)(2,1)S(1)} %shard_map.37), channel_id=1, replica_groups=mesh['x'=4,'yh'=2,'core'=2,'yl'=2,'z'=8] {'z','core'}, dimensions={0} | all-to-all | bytes 65536 | tf_op jit(solution)/shard_map/all_to_all | solution.py:56
  105.2 10.7 %all_to_all.40.in_ref = bf16[16,8,128]{2,1,0:T(8,128)(2,1)S(1)} all-to-all(bf16[16,8,128]{2,1,0:T(8,128)(2,1)S(1)} %shard_map.38), channel_id=1, replica_groups=mesh['x'=4,'yh'=2,'core'=2,'yl'=2,'z'=8] {'x','yh','yl'}, dimensions={0} | all-to-all | bytes 65536 | tf_op jit(solution)/shard_map/all_to_all | solution.py:56
  115.9 2.2 %shard_map.39 = (bf16[1024,1024]{1,0:T(8,128)(2,1)S(1)}, bf16[512,1152]{1,0:T(8,128)(2,1)S(1)}) custom-call(bf16[1024,1024]{1,0:T(8,128)(2,1)S(1)} %get-tuple-element.36.plan_ref, bf16[16,8,128]{2,1,0:T(8,128)(2,1)S(1)} %all_to_all.40.in_ref, bf16[1024,1024]{1,0:T(8,128)(2,1)S(1)} %bitcast.2), custom_call_target="tpu_custom_call" | custom-call | flops 1073741824 | bytes 4194304 | tf_op jit(solution)/shard_map/pallas_call | solution.py:312
  121.8 2.7 %collective-permute-start.13 = (bf16[64,1152]{1,0:T(8,128)(2,1)S(1)}, bf16[64,1152]{1,0:T(8,128)(2,1)S(1)}, u32[]{:S(2)}, u32[]{:S(2)}) collective-permute-start(bf16[64,1152]{1,0:T(8,128)(2,1)S(1)} %get-tuple-element.42), channel_id=1, source_target_pairs={{0,7},{1,0},{2,1},{3,2},{4,3},{5,4},{6,5},{7,6},{8,15},{9,8},{10,9... | collective-permute-start | bytes 442376 | tf_op jit(solution)/shard_map/ppermute | solution.py:48
  124.6 4.1 %collective-permute-start.14 = (bf16[32,1152]{1,0:T(8,128)(2,1)S(1)}, bf16[32,1152]{1,0:T(8,128)(2,1)S(1)}, u32[]{:S(2)}, u32[]{:S(2)}) collective-permute-start(bf16[32,1152]{1,0:T(8,128)(2,1)S(1)} %get-tuple-element.43), channel_id=1, source_target_pairs={{0,6},{1,7},{2,0},{3,1},{4,2},{5,3},{6,4},{7,5},{8,14},{9,15},{10,... | collective-permute-start | bytes 221192 | tf_op jit(solution)/shard_map/ppermute | solution.py:48
  129.0 2.3 %collective-permute-done.10.far_ref = bf16[32,1152]{1,0:T(8,128)(2,1)S(1)} collective-permute-done((bf16[32,1152]{1,0:T(8,128)(2,1)S(1)}, bf16[32,1152]{1,0:T(8,128)(2,1)S(1)}, u32[]{:S(2)}, u32[]{:S(2)}) %collective-permute-start.10) | collective-permute-done | bytes 73760 | tf_op jit(solution)/shard_map/ppermute | solution.py:48
  131.5 1.8 %collective-permute-start.11 = (bf16[64,1152]{1,0:T(8,128)(2,1)S(1)}, bf16[64,1152]{1,0:T(8,128)(2,1)S(1)}, u32[]{:S(2)}, u32[]{:S(2)}) collective-permute-start(bf16[64,1152]{1,0:T(8,128)(2,1)S(1)} %shard_map.43), channel_id=1, source_target_pairs={{0,1},{1,2},{2,3},{3,4},{4,5},{5,6},{6,7},{7,0},{8,9},{9,10},{10,1... | collective-permute-start | bytes 442376 | tf_op jit(solution)/shard_map/ppermute | solution.py:48
  135.0 2.9 %collective-permute-done.11.got_ref = bf16[64,1152]{1,0:T(8,128)(2,1)S(1)} collective-permute-done((bf16[64,1152]{1,0:T(8,128)(2,1)S(1)}, bf16[64,1152]{1,0:T(8,128)(2,1)S(1)}, u32[]{:S(2)}, u32[]{:S(2)}) %collective-permute-start.11) | collective-permute-done | bytes 147488 | tf_op jit(solution)/shard_map/ppermute | solution.py:48
  138.7 2.8 %collective-permute-start.16 = (bf16[64,1152]{1,0:T(8,128)(2,1)S(1)}, bf16[64,1152]{1,0:T(8,128)(2,1)S(1)}, u32[]{:S(2)}, u32[]{:S(2)}) collective-permute-start(bf16[64,1152]{1,0:T(8,128)(2,1)S(1)} %shard_map.46), channel_id=1, source_target_pairs={{0,7},{1,0},{2,1},{3,2},{4,3},{5,4},{6,5},{7,6},{8,15},{9,8},{10,9... | collective-permute-start | bytes 442376 | tf_op jit(solution)/shard_map/ppermute | solution.py:48
  141.5 2.9 %collective-permute-done.12.right_ref = bf16[64,1152]{1,0:T(8,128)(2,1)S(1)} collective-permute-done((bf16[64,1152]{1,0:T(8,128)(2,1)S(1)}, bf16[64,1152]{1,0:T(8,128)(2,1)S(1)}, u32[]{:S(2)}, u32[]{:S(2)}) %collective-permute-start.12) | collective-permute-done | bytes 147488 | tf_op jit(solution)/shard_map/ppermute | solution.py:48
  (40 shorter events, 18.0 us)
Async XLA Ops:
  0.0 0.9 copy-start
  2.4 7.6 %copy-start.1 = (bf16[64,1024]{1,0:T(8,128)(2,1)S(1)}, bf16[64,1024]{1,0:T(8,128)(2,1)}, u32[]{:S(2)}) copy-start(bf16[64,1024]{1,0:T(8,128)(2,1)} %noise_ref.1) | copy-start | bytes 393220
  2.4 37.4 %all-to-all-start = ((bf16[16,64,1024]{2,1,0:T(8,128)(2,1)}), bf16[16,64,1024]{2,1,0:T(8,128)(2,1)S(1)}, u32[]{:S(2)}, u32[]{:S(2)}) async-start(bf16[16,64,1024]{2,1,0:T(8,128)(2,1)} %shard_map.31), calls=%async_computation | async-start | bytes 4194304 | tf_op jit(solution)/shard_map/all_to_all | solution.py:56
  10.0 12.3 %collective-permute-start.3 = (bf16[64,1024]{1,0:T(8,128)(2,1)S(1)}, bf16[64,1024]{1,0:T(8,128)(2,1)}, u32[]{:S(2)}, u32[]{:S(2)}) collective-permute-start(bf16[64,1024]{1,0:T(8,128)(2,1)S(1)} %param.1), channel_id=1, source_target_pairs={{0,6},{1,7},{2,0},{3,1},{4,2},{5,3},{6,4},{7,5},{8,14},{9,15},{10,... | collective-permute-start | bytes 393224 | tf_op jit(solution)/shard_map/cond/branch_1_fun/ppermute | solution.py:60
  16.4 9.2 %collective-permute-start.2 = (bf16[64,1024]{1,0:T(8,128)(2,1)S(1)}, bf16[64,1024]{1,0:T(8,128)(2,1)}, u32[]{:S(2)}, u32[]{:S(2)}) collective-permute-start(bf16[64,1024]{1,0:T(8,128)(2,1)S(1)} %param.1), channel_id=1, source_target_pairs={{0,2},{1,3},{2,4},{3,5},{4,6},{5,7},{6,0},{7,1},{8,10},{9,11},{10,... | collective-permute-start | bytes 393224 | tf_op jit(solution)/shard_map/cond/branch_1_fun/ppermute | solution.py:60
  16.4 10.3 %collective-permute-start.1 = (bf16[64,1024]{1,0:T(8,128)(2,1)S(1)}, bf16[64,1024]{1,0:T(8,128)(2,1)}, u32[]{:S(2)}, u32[]{:S(2)}) collective-permute-start(bf16[64,1024]{1,0:T(8,128)(2,1)S(1)} %param.1), channel_id=1, source_target_pairs={{0,7},{1,0},{2,1},{3,2},{4,3},{5,4},{6,5},{7,6},{8,15},{9,8},{10,9... | collective-permute-start | bytes 393224 | tf_op jit(solution)/shard_map/cond/branch_1_fun/ppermute | solution.py:60
  20.1 7.3 %collective-permute-start = (bf16[64,1024]{1,0:T(8,128)(2,1)S(1)}, bf16[64,1024]{1,0:T(8,128)(2,1)}, u32[]{:S(2)}, u32[]{:S(2)}) collective-permute-start(bf16[64,1024]{1,0:T(8,128)(2,1)S(1)} %param.1), channel_id=1, source_target_pairs={{0,1},{1,2},{2,3},{3,4},{4,5},{5,6},{6,7},{7,0},{8,9},{9,10},{10,1... | collective-permute-start | bytes 393224 | tf_op jit(solution)/shard_map/cond/branch_1_fun/ppermute | solution.py:60
  22.3 8.0 %collective-permute-start.5 = (bf16[64,1024]{1,0:T(8,128)(2,1)}, bf16[64,1024]{1,0:T(8,128)(2,1)}, u32[]{:S(2)}, u32[]{:S(2)}) collective-permute-start(bf16[64,1024]{1,0:T(8,128)(2,1)} %collective-permute-done.3), channel_id=1, source_target_pairs={{0,7},{1,0},{2,1},{3,2},{4,3},{5,4},{6,5},{7,6},{8,15},{9,8},{10,9... | collective-permute-start | bytes 393224 | tf_op jit(solution)/shard_map/cond/branch_1_fun/ppermute | solution.py:60
  25.6 8.9 %collective-permute-start.6 = (bf16[64,1024]{1,0:T(8,128)(2,1)}, bf16[64,1024]{1,0:T(8,128)(2,1)}, u32[]{:S(2)}, u32[]{:S(2)}) collective-permute-start(bf16[64,1024]{1,0:T(8,128)(2,1)} %collective-permute-done.2), channel_id=1, source_target_pairs={{0,2},{1,3},{2,4},{3,5},{4,6},{5,7},{6,0},{7,1},{8,10},{9,11},{10,... | collective-permute-start | bytes 393224 | tf_op jit(solution)/shard_map/cond/branch_1_fun/ppermute | solution.py:60
  25.6 9.9 %collective-permute-start.4 = (bf16[64,1024]{1,0:T(8,128)(2,1)}, bf16[64,1024]{1,0:T(8,128)(2,1)}, u32[]{:S(2)}, u32[]{:S(2)}) collective-permute-start(bf16[64,1024]{1,0:T(8,128)(2,1)} %collective-permute-done.2), channel_id=1, source_target_pairs={{0,1},{1,2},{2,3},{3,4},{4,5},{5,6},{6,7},{7,0},{8,9},{9,10},{10,1... | collective-permute-start | bytes 393224 | tf_op jit(solution)/shard_map/cond/branch_1_fun/ppermute | solution.py:60
  36.9 2.9 %collective-permute-start.7 = (bf16[512,1024]{1,0:T(8,128)(2,1)S(1)}, bf16[512,1024]{1,0:T(8,128)(2,1)}, u32[]{:S(2)}, u32[]{:S(2)}) collective-permute-start(bf16[512,1024]{1,0:T(8,128)(2,1)S(1)} %shard_map.32.own_ref), channel_id=1, source_target_pairs={{0,16},{1,17},{2,18},{3,19},{4,20},{5,21},{6,22},{7,23},{8,24},{9,... | collective-permute-start | bytes 3145736 | tf_op jit(solution)/shard_map/ppermute | solution.py:52
  118.1 2.9 %collective-permute-start.8 = (bf16[512,1152]{1,0:T(8,128)(2,1)S(1)}, bf16[512,1152]{1,0:T(8,128)(2,1)S(1)}, u32[]{:S(2)}, u32[]{:S(2)}) collective-permute-start(bf16[512,1152]{1,0:T(8,128)(2,1)S(1)} %get-tuple-element.39), channel_id=1, source_target_pairs={{0,16},{1,17},{2,18},{3,19},{4,20},{5,21},{6,22},{7,23},{8,24},{9,... | collective-permute-start | bytes 3538952 | tf_op jit(solution)/shard_map/ppermute | solution.py:52
  121.2 10.1 %collective-permute-start.9 = (bf16[64,1152]{1,0:T(8,128)(2,1)S(1)}, bf16[64,1152]{1,0:T(8,128)(2,1)S(1)}, u32[]{:S(2)}, u32[]{:S(2)}) collective-permute-start(bf16[64,1152]{1,0:T(8,128)(2,1)S(1)} %get-tuple-element.40), channel_id=1, source_target_pairs={{0,1},{1,2},{2,3},{3,4},{4,5},{5,6},{6,7},{7,0},{8,9},{9,10},{10,1... | collective-permute-start | bytes 442376 | tf_op jit(solution)/shard_map/ppermute | solution.py:48
  121.8 11.4 %collective-permute-start.13 = (bf16[64,1152]{1,0:T(8,128)(2,1)S(1)}, bf16[64,1152]{1,0:T(8,128)(2,1)S(1)}, u32[]{:S(2)}, u32[]{:S(2)}) collective-permute-start(bf16[64,1152]{1,0:T(8,128)(2,1)S(1)} %get-tuple-element.42), channel_id=1, source_target_pairs={{0,7},{1,0},{2,1},{3,2},{4,3},{5,4},{6,5},{7,6},{8,15},{9,8},{10,9... | collective-permute-start | bytes 442376 | tf_op jit(solution)/shard_map/ppermute | solution.py:48
  124.6 6.8 %collective-permute-start.10 = (bf16[32,1152]{1,0:T(8,128)(2,1)S(1)}, bf16[32,1152]{1,0:T(8,128)(2,1)S(1)}, u32[]{:S(2)}, u32[]{:S(2)}) collective-permute-start(bf16[32,1152]{1,0:T(8,128)(2,1)S(1)} %get-tuple-element.41), channel_id=1, source_target_pairs={{0,2},{1,3},{2,4},{3,5},{4,6},{5,7},{6,0},{7,1},{8,10},{9,11},{10,... | collective-permute-start | bytes 221192 | tf_op jit(solution)/shard_map/ppermute | solution.py:48
  124.6 8.7 %collective-permute-start.14 = (bf16[32,1152]{1,0:T(8,128)(2,1)S(1)}, bf16[32,1152]{1,0:T(8,128)(2,1)S(1)}, u32[]{:S(2)}, u32[]{:S(2)}) collective-permute-start(bf16[32,1152]{1,0:T(8,128)(2,1)S(1)} %get-tuple-element.43), channel_id=1, source_target_pairs={{0,6},{1,7},{2,0},{3,1},{4,2},{5,3},{6,4},{7,5},{8,14},{9,15},{10,... | collective-permute-start | bytes 221192 | tf_op jit(solution)/shard_map/ppermute | solution.py:48
  131.5 6.4 %collective-permute-start.11 = (bf16[64,1152]{1,0:T(8,128)(2,1)S(1)}, bf16[64,1152]{1,0:T(8,128)(2,1)S(1)}, u32[]{:S(2)}, u32[]{:S(2)}) collective-permute-start(bf16[64,1152]{1,0:T(8,128)(2,1)S(1)} %shard_map.43), channel_id=1, source_target_pairs={{0,1},{1,2},{2,3},{3,4},{4,5},{5,6},{6,7},{7,0},{8,9},{9,10},{10,1... | collective-permute-start | bytes 442376 | tf_op jit(solution)/shard_map/ppermute | solution.py:48
  133.4 5.2 %collective-permute-start.15 = (bf16[64,1152]{1,0:T(8,128)(2,1)S(1)}, bf16[64,1152]{1,0:T(8,128)(2,1)S(1)}, u32[]{:S(2)}, u32[]{:S(2)}) collective-permute-start(bf16[64,1152]{1,0:T(8,128)(2,1)S(1)} %shard_map.45), channel_id=1, source_target_pairs={{0,7},{1,0},{2,1},{3,2},{4,3},{5,4},{6,5},{7,6},{8,15},{9,8},{10,9... | collective-permute-start | bytes 442376 | tf_op jit(solution)/shard_map/ppermute | solution.py:48
  138.0 6.4 %collective-permute-start.12 = (bf16[64,1152]{1,0:T(8,128)(2,1)S(1)}, bf16[64,1152]{1,0:T(8,128)(2,1)S(1)}, u32[]{:S(2)}, u32[]{:S(2)}) collective-permute-start(bf16[64,1152]{1,0:T(8,128)(2,1)S(1)} %shard_map.44), channel_id=1, source_target_pairs={{0,1},{1,2},{2,3},{3,4},{4,5},{5,6},{6,7},{7,0},{8,9},{9,10},{10,1... | collective-permute-start | bytes 442376 | tf_op jit(solution)/shard_map/ppermute | solution.py:48
  138.7 5.7 %collective-permute-start.16 = (bf16[64,1152]{1,0:T(8,128)(2,1)S(1)}, bf16[64,1152]{1,0:T(8,128)(2,1)S(1)}, u32[]{:S(2)}, u32[]{:S(2)}) collective-permute-start(bf16[64,1152]{1,0:T(8,128)(2,1)S(1)} %shard_map.46), channel_id=1, source_target_pairs={{0,7},{1,0},{2,1},{3,2},{4,3},{5,4},{6,5},{7,6},{8,15},{9,8},{10,9... | collective-permute-start | bytes 442376 | tf_op jit(solution)/shard_map/ppermute | solution.py:48
